TPU v7x, 128 devices: a whole 4x4x4 slice. The times are simulated.
128 devices in a mesh: group: 2 (over core), wide: 64 (over y, z, x).
Axes of the slice: x: 4, y: 4, z: 4, core: 2. Of those that a mesh axis runs over, the one named last changes fastest.
Arguments:
- hot_table: bfloat16 [4096, 256], replicated, may hold values from -6 to 6
- tail_table: bfloat16 [524288, 256], P('wide'), may hold values from -6 to 6
- word_table: bfloat16 [4096, 256], replicated, may hold values from -6 to 6
- out_table: bfloat16 [8192, 256], replicated, may hold values from -1.796875 to 1.796875
- w_first: bfloat16 [600, 1024], replicated, may hold values from -0.5 to 0.5
- b_first: bfloat16 [1024], replicated, may hold values from -1.5 to 1.5
- w_second: bfloat16 [1024, 512], replicated, may hold values from -0.25 to 0.25
- b_second: bfloat16 [512], replicated, may hold values from -1.5 to 1.5
- w_third: bfloat16 [512, 256], replicated, may hold values from -0.5 to 0.5
- b_third: bfloat16 [256], replicated, may hold values from -1.5 to 1.5
- dense_feats: bfloat16 [131072, 88], P(('group', 'wide')), may hold values from -6 to 6
- hist_ids: int32 [131072, 50], P(('group', 'wide')), may hold values from 0 to 12287, as said below
- hist_len: int32 [131072], P(('group', 'wide')), may hold values from 1 to 50
- search_ids: int32 [131072, 50], P(('group', 'wide')), may hold values from 0 to 4095
- search_len: int32 [131072], P(('group', 'wide')), may hold values from 1 to 50
- requests: int32 [8192, 128], P(('group', 'wide')), may hold values from -1 to 8191, as said below
- labels: int32 [131072], P(('group', 'wide')), may hold values from 0 to 8191
- negatives: int32 [5000], replicated, may hold values from 0 to 8191, as said below
Outputs:
- loss_value: float32 [], replicated
- hot_grad: float32 [4096, 256], replicated
- tail_grad: float32 [524288, 256], P('wide')
- word_grad: float32 [4096, 256], replicated
- out_grad: float32 [8192, 256], replicated
- w_first_grad: float32 [600, 1024], replicated
- b_first_grad: float32 [1024], replicated
- w_second_grad: float32 [1024, 512], replicated
- b_second_grad: float32 [512], replicated
- w_third_grad: float32 [512, 256], replicated
- b_third_grad: float32 [256], replicated
Inputs may be any that keep to these rules, and one draw needn't show every extreme that they name: `requests`: row p * 64 + o belongs to device p and owner o: its first entries name rows of that owner's 8192 rows, the rest are -1; at least 64 are filled and in every draw some blocks are full. `hist_ids`: an entry below 4096 names a row of hot_table; an entry v of 4096 or more names the device's request slot v - 4096 (owner (v - 4096) // 128), which is always a filled slot. `negatives`: all different.
All inputs are finite; a program needn't handle non-finite values.
Results may differ from a plain program's by a relative error of at most 0.012.
The roundings to bfloat16 on the way count: a program that leaves them out, or rounds other values in their place, can miss the bound.
Values may be sent and summed in bfloat16 or wider, within the bound.
No kernel may reach another device: no remote copies, remote signals or barrier semaphores. Data moves between devices by JAX's collectives and lax.ppermute only.
A program may use at most 256 MiB of HBM per device.

v0:
```python
import jax
import jax.numpy as jnp
from jax import lax
from jax.sharding import PartitionSpec as P


def count_table(id_table, lengths, table_rows):
    in_range = (lax.broadcasted_iota(jnp.int32, id_table.shape, 1) < lengths[:, None]).astype(
        jnp.float32
    )
    row_index = lax.broadcasted_iota(jnp.int32, id_table.shape, 0)
    counts = (
        jnp.zeros((id_table.shape[0], table_rows), jnp.float32)
        .at[row_index, id_table]
        .add(in_range)
    )
    return counts.astype(jnp.bfloat16)


def pooled(table, id_table, lengths, table_rows):
    counts = count_table(id_table, lengths, table_rows)
    summed = jnp.dot(counts, table, preferred_element_type=jnp.float32)
    return (summed / lengths[:, None].astype(jnp.float32), counts)


def left_product(first_op, second_op):
    return lax.dot_general(
        first_op, second_op, (((0,), (0,)), ((), ())), preferred_element_type=jnp.float32
    )


def right_product(first_op, second_op):
    return lax.dot_general(
        first_op, second_op, (((1,), (1,)), ((), ())), preferred_element_type=jnp.float32
    )


def spread(d_mean, lengths, counts):
    portion = d_mean / lengths[:, None].astype(jnp.float32)
    upper = portion.astype(jnp.bfloat16)
    lower = (portion - upper.astype(jnp.float32)).astype(jnp.bfloat16)
    return left_product(counts, upper) + left_product(counts, lower)


def gelu_back(pre_value, d_act):
    unused, pull = jax.vjp(jax.nn.gelu, pre_value)
    return pull(d_act)[0]


def local(
    hot_table,
    tail_table,
    word_table,
    out_table,
    w_first,
    b_first,
    w_second,
    b_second,
    w_third,
    b_third,
    dense_feats,
    hist_ids,
    hist_len,
    search_ids,
    search_len,
    requests,
    labels,
    negatives,
):
    feat_width = hot_table.shape[1]
    hot_rows = hot_table.shape[0]
    owners = requests.shape[0]
    per_owner = requests.shape[1]
    examples_dev = hist_ids.shape[0]
    examples_all = examples_dev * lax.axis_size("group") * lax.axis_size("wide")
    shard_rows = tail_table.shape[0]
    asked_ids = lax.all_to_all(requests, "wide", split_axis=0, concat_axis=0, tiled=True)
    filled = asked_ids >= 0
    looked = jnp.take(tail_table, jnp.clip(asked_ids, 0, shard_rows - 1), axis=0)
    looked = jnp.where(filled[:, :, None], looked, jnp.zeros((), jnp.bfloat16))
    returned = lax.all_to_all(looked, "wide", split_axis=0, concat_axis=0, tiled=True)
    source = jnp.concatenate([hot_table, returned.reshape(owners * per_owner, feat_width)], axis=0)
    hist_mean, hist_counts = pooled(source, hist_ids, hist_len, source.shape[0])
    search_mean, search_counts = pooled(word_table, search_ids, search_len, word_table.shape[0])
    inputs = jnp.concatenate(
        [hist_mean, search_mean, dense_feats.astype(jnp.float32)], axis=1
    ).astype(jnp.bfloat16)
    pre_first = jnp.dot(inputs, w_first, preferred_element_type=jnp.float32) + b_first.astype(
        jnp.float32
    )
    act_first = jax.nn.gelu(pre_first).astype(jnp.bfloat16)
    pre_second = jnp.dot(act_first, w_second, preferred_element_type=jnp.float32) + b_second.astype(
        jnp.float32
    )
    act_second = jax.nn.gelu(pre_second).astype(jnp.bfloat16)
    user = (
        jnp.dot(act_second, w_third, preferred_element_type=jnp.float32)
        + b_third.astype(jnp.float32)
    ).astype(jnp.bfloat16)
    neg_rows = jnp.take(out_table, negatives, axis=0)
    label_rows = jnp.take(out_table, labels, axis=0).astype(jnp.float32)
    user_float = user.astype(jnp.float32)
    neg_logits = right_product(user, neg_rows)
    pos_logits = jnp.sum(user_float * label_rows, axis=1)
    peak_logit = jnp.maximum(pos_logits, jnp.max(neg_logits, axis=1))
    pos_exp = jnp.exp(pos_logits - peak_logit)
    neg_exp = jnp.exp(neg_logits - peak_logit[:, None])
    totals = pos_exp + jnp.sum(neg_exp, axis=1)
    per_example = peak_logit + jnp.log(totals) - pos_logits
    half_count = examples_dev // 2
    loss_halves = jnp.stack([jnp.sum(per_example[:half_count]), jnp.sum(per_example[half_count:])])
    inv_count = 1.0 / examples_dev
    d_neg = (neg_exp / totals[:, None] * inv_count).astype(jnp.bfloat16)
    d_pos = ((pos_exp / totals - 1.0) * inv_count).astype(jnp.bfloat16).astype(jnp.float32)
    d_user = (
        jnp.dot(d_neg, neg_rows, preferred_element_type=jnp.float32) + d_pos[:, None] * label_rows
    ).astype(jnp.bfloat16)
    out_grad = jnp.zeros(out_table.shape, jnp.float32)
    out_grad = out_grad.at[negatives].add(left_product(d_neg, user))
    out_grad = out_grad.at[labels].add(d_pos[:, None] * user_float)
    w_third_grad = left_product(act_second, d_user)
    b_third_grad = jnp.sum(d_user.astype(jnp.float32), axis=0)
    d_pre_second = gelu_back(pre_second, right_product(d_user, w_third)).astype(jnp.bfloat16)
    w_second_grad = left_product(act_first, d_pre_second)
    b_second_grad = jnp.sum(d_pre_second.astype(jnp.float32), axis=0)
    d_pre_first = gelu_back(pre_first, right_product(d_pre_second, w_second)).astype(jnp.bfloat16)
    w_first_grad = left_product(inputs, d_pre_first)
    b_first_grad = jnp.sum(d_pre_first.astype(jnp.float32), axis=0)
    d_inputs = right_product(d_pre_first, w_first)
    source_grad = spread(d_inputs[:, :feat_width], hist_len, hist_counts)
    word_grad = spread(d_inputs[:, feat_width : 2 * feat_width], search_len, search_counts)
    hot_grad = source_grad[:hot_rows]
    slot_grad = source_grad[hot_rows:].reshape(owners, per_owner, feat_width)
    owed = lax.all_to_all(slot_grad, "wide", split_axis=0, concat_axis=0, tiled=True)
    owed = jnp.where((asked_ids >= 0)[:, :, None], owed, jnp.float32(0.0))
    tail_local = jax.ops.segment_sum(
        owed.reshape(-1, feat_width),
        jnp.clip(asked_ids, 0, shard_rows - 1).reshape(-1),
        num_segments=shard_rows,
    )
    tail_grad = lax.psum(tail_local, "group")
    summed = lax.psum(
        (
            hot_grad,
            word_grad,
            out_grad,
            w_first_grad,
            b_first_grad,
            w_second_grad,
            b_second_grad,
            w_third_grad,
            b_third_grad,
            loss_halves,
        ),
        ("group", "wide"),
    )
    hot_sum, word_sum, out_sum, w1_sum, b1_sum, w2_sum, b2_sum, w3_sum, b3_sum, loss_sum = summed
    loss_value = (loss_sum[0] + loss_sum[1]) / examples_all
    return (
        loss_value,
        hot_sum,
        tail_grad,
        word_sum,
        out_sum,
        w1_sum,
        b1_sum,
        w2_sum,
        b2_sum,
        w3_sum,
        b3_sum,
    )


def solution(mesh):
    in_specs = (
        P(),
        P("wide", None),
        P(),
        P(),
        P(),
        P(),
        P(),
        P(),
        P(),
        P(),
        P(("group", "wide"), None),
        P(("group", "wide"), None),
        P(("group", "wide")),
        P(("group", "wide"), None),
        P(("group", "wide")),
        P(("group", "wide"), None),
        P(("group", "wide")),
        P(),
    )
    out_specs = (P(), P(), P("wide", None), P(), P(), P(), P(), P(), P(), P(), P())
    return jax.shard_map(local, mesh=mesh, in_specs=in_specs, out_specs=out_specs, check_vma=False)
```

profile of v0, /device:TPU:1, one launch (start us, length us, event | category | flops | bytes accessed | tf_op | source)
XLA Modules:
  0.0 1340.9 jit_solution(16892060098760972300)
XLA Ops:
  7.2 20.4 %all_to_all.19 = s32[64,1,128]{2,1,0:T(1,128)S(1)} all-to-all(s32[64,1,128]{2,1,0:T(1,128)} %bitcast.66), channel_id=1, replica_groups=mesh['group'=2,'wide'=64] {'wide'}, dimensions={0} | all-to-all | bytes 65536 | tf_op jit(solution)/shard_map/all_to_all | solution.py:77
  28.2 33.9 %gather_fusion = bf16[8192,256]{1,0:T(8,128)(2,1)} fusion(bf16[8192,256]{1,0:T(8,128)(2,1)} %param.19, s32[8192]{0:T(1024)S(1)} %fusion.47), kind=kCustom, calls=%fused_computation | custom fusion | bytes 8421376 | tf_op jit(solution)/shard_map/jit(_take)/gather | solution.py:79
  77.6 286.7 %scatter_custom_fusion.3 = f32[12582912]{0:T(1024)} fusion(s32[51200]{0:T(1024)S(1)} %reshape.204, f32[51200]{0:T(1024)S(1)} %reshape.206, f32[]{:T(128)} %constant.25.clone.1), kind=kCustom, calls=%fused_computation.8 | custom fusion | flops 51200 | bytes 50331652
  364.4 25.4 %convert_element_type.130 = bf16[12582912]{0:T(1024)(128)(2,1)} convert(f32[12582912]{0:T(1024)} %scatter_custom_fusion.3) | non-fusion elementwise | flops 12582912 | bytes 75497472 | tf_op jit(solution)/shard_map/convert_element_type | solution.py:17
  389.7 35.5 %reshape.154 = bf16[1024,12288]{1,0:T(8,128)(2,1)} reshape(bf16[12582912]{0:T(1024)(128)(2,1)} %convert_element_type.130) | data formatting | bytes 50331648 | tf_op jit(solution)/shard_map/convert_element_type | solution.py:17
  426.6 273.9 %scatter_custom_fusion.4 = f32[4194304]{0:T(1024)} fusion(s32[51200]{0:T(1024)S(1)} %reshape.210, f32[51200]{0:T(1024)S(1)} %reshape.212, f32[]{:T(128)} %constant.25.clone.1), kind=kCustom, calls=%fused_computation.14 | custom fusion | flops 51200 | bytes 16777220
  700.5 8.9 convert_element_type.131
  709.4 13.3 reshape.155
  730.0 22.5 %gather_fusion.2 = bf16[5000,256]{1,0:T(8,128)(2,1)} fusion(bf16[8192,256]{1,0:T(8,128)(2,1)} %param.21, s32[5120]{0:T(1024)S(1)} %pad_clamp_fusion), kind=kCustom, calls=%fused_computation.2 | custom fusion | bytes 5140000 | tf_op jit(solution)/shard_map/jit(_take)/gather | solution.py:100
  758.4 16.1 %fusion.31 = bf16[1024,256]{0,1:T(8,128)(2,1)S(1)} fusion(bf16[1024,12288]{1,0:T(8,128)(2,1)} %reshape.154, bf16[8192,256]{1,0:T(8,128)(2,1)} %bitcast.9, bf16[4096,256]{1,0:T(8,128)(2,1)} %param.18, f32[1024]{0:T(1024)S(1)} %convert_element_type.103), kind=kOutput, calls=%fused_computation.56 | convolution fusion | flops 6455558144 | bytes 31985664 | tf_op jit(solution)/shard_map/dot_general | solution.py:22
  783.5 9.0 fusion.62
  792.5 9.5 fusion.2
  802.1 9.3 multiply_convert_fusion
  839.0 14.9 %fusion.59 = f32[12288,256]{1,0:T(8,128)} fusion(bf16[1024,12288]{1,0:T(8,128)(2,1)} %reshape.154, f32[1024]{0:T(1024)S(1)} %convert_element_type.103, f32[1024,600]{0,1:T(8,128)S(1)} %fusion.63), kind=kOutput, calls=%fused_computation.117 | convolution fusion | flops 6442975232 | bytes 38801408 | tf_op jit(solution)/shard_map/dot_general | solution.py:27
  854.2 29.6 %scatter_custom_fusion.1 = f32[8192,256]{1,0:T(8,128)} fusion(s32[5000]{0:T(1024)S(1)} %compare_select_fusion.4, f32[5000,256]{1,0:T(8,128)} %fusion.64, f32[]{:T(128)} %constant.25.clone.1), kind=kCustom, calls=%fused_computation.32 | custom fusion | flops 1280000 | bytes 8389120 | tf_op jit(solution)/shard_map/scatter-add | solution.py:119
  883.8 9.5 convolution_add_fusion.1
  893.4 20.0 %convolution_add_fusion = f32[12288,256]{1,0:T(8,128)} fusion(f32[12288,256]{1,0:T(8,128)} %fusion.59, bf16[1024,12288]{1,0:T(8,128)(2,1)} %reshape.154, f32[1024,600]{0,1:T(8,128)} %copy-done.11, f32[1024]{0:T(1024)S(1)} %convert_element_type.103), kind=kOutput, calls=%fused_computation.13 | convolution fusion | flops 6446907392 | bytes 51384320 | tf_op jit(solution)/shard_map/dot_general | solution.py:27
  917.8 12.8 scatter_fusion
  938.0 10.1 all-to-all-start.2
  948.1 109.1 %all-to-all-done.2 = f32[64,128,256]{2,1,0:T(8,128)} async-done(((f32[64,128,256]{2,1,0:T(8,128)}), f32[64,128,256]{2,1,0:T(8,128)}, u32[]{:S(2)}, u32[]{:S(2)}) %all-to-all-start.2) | async-done | bytes 8388640 | tf_op jit(solution)/shard_map/all_to_all | solution.py:134
  1064.8 50.5 %scatter_custom_fusion = f32[8192,256]{1,0:T(8,128)} fusion(s32[8192]{0:T(1024)S(1)} %clamp_bitcast_fusion, f32[8192,256]{1,0:T(8,128)} %bitcast.61, f32[]{:T(128)} %constant.25.clone.1), kind=kCustom, calls=%fused_computation.34 | custom fusion | flops 2097152 | bytes 8389120 | tf_op jit(solution)/shard_map/scatter-add | solution.py:136
  1117.3 69.2 %all-reduce = (f32[2]{0:T(128)S(1)}, f32[1024]{0:T(1024)}, f32[512]{0:T(512)}, f32[256]{0:T(256)}) all-reduce(f32[2]{0:T(128)S(1)} %pad_maximum_fusion.3, f32[1024]{0:T(1024)S(1)} %get-tuple-element.42, f32[512]{0:T(512)S(1)} %get-tuple-element.44, f32[256]{0:T(256)S(1)} %get-tuple-element.46), channel_id=1, replica_groups=mesh['group'=2,'wide'=64] {'group','wide'}, use_global_device_ids=true, to_apply=%region_7.8 | all-reduce | flops 1794 | bytes 14352 | tf_op jit(solution)/shard_map/psum | solution.py:142
  1188.4 74.4 %all-reduce.7.cloned.1.call-done = (f32[4096,256]{1,0:T(8,128)}, f32[4096,256]{1,0:T(8,128)}, f32[8192,256]{1,0:T(8,128)}, f32[600,1024]{1,0:T(8,128)}, f32[1024,512]{1,0:T(8,128)}, /*index=5*/f32[512,256]{1,0:T(8,128)}) async-done(((f32[4096,256]{1,0:T(8,128)}, f32[4096,256]{1,0:T(8,128)}, f32[8192,256]{1,0:T(8,128)}, f32[600,1024]{1,0:T(8,128)}, f32[1024,512]{1,0:T(8,128)}, ...) | async-done | bytes 21856272 | tf_op jit(solution)/shard_map/psum | solution.py:142
  1262.8 45.6 %all-reduce.5.cloned.1.call-done = f32[8192,256]{1,0:T(8,128)} async-done(((f32[8192,256]{1,0:T(8,128)}), f32[8192,256]{1,0:T(8,128)}) %all-reduce.5.cloned.1.call-update) | async-done | bytes 8388624 | tf_op jit(solution)/shard_map/psum | solution.py:141
  (161 shorter events, 113.1 us)
Async XLA Ops:
  7.2 745.4 %copy-start = (bf16[4096,256]{1,0:T(8,128)(2,1)S(1)}, bf16[4096,256]{1,0:T(8,128)(2,1)}, u32[]{:S(2)}) copy-start(bf16[4096,256]{1,0:T(8,128)(2,1)} %param.20) | copy-start | bytes 6291460
  27.6 34.5 %copy-start.15 = (pred[64,128]{1,0:T(8,128)(4,1)}, pred[64,128]{1,0:T(8,128)(4,1)S(1)}, u32[]{:S(2)}) copy-start(pred[64,128]{1,0:T(8,128)(4,1)S(1)} %compare_bitcast_fusion) | copy-start | bytes 24580
  69.8 688.5 %all-to-all-start.1 = ((bf16[64,128,256]{2,1,0:T(8,128)(2,1)}), bf16[64,128,256]{2,1,0:T(8,128)(2,1)}, u32[]{:S(2)}, u32[]{:S(2)}) async-start(bf16[64,128,256]{2,1,0:T(8,128)(2,1)} %select_select_fusion), calls=%async_computation.1 | async-start | bytes 8388608 | tf_op jit(solution)/shard_map/all_to_all | solution.py:81
  75.6 1187.2 %all-reduce.7.cloned.1.call-start = ((), (), s32[]{:S(2)}) async-start(), calls=%async_computation.4 | async-start | bytes 43712512 | tf_op jit(solution)/shard_map/psum | solution.py:142
  389.7 36.2 %copy-start.18 = (s32[1024]{0:T(1024)S(1)}, s32[1024]{0:T(1024)}, u32[]{:S(2)}) copy-start(s32[1024]{0:T(1024)} %param.32) | copy-start | bytes 12292
  709.4 13.3 copy-start.20
  709.4 13.3 copy-start.21
  709.4 13.3 copy-start.19
  722.7 7.3 copy-start.33
  722.7 7.3 copy-start.14
  758.3 16.2 %copy-start.37 = (bf16[1024,256]{0,1:T(8,128)(2,1)}, bf16[1024,256]{0,1:T(8,128)(2,1)S(1)}, u32[]{:S(2)}) copy-start(bf16[1024,256]{0,1:T(8,128)(2,1)S(1)} %fusion.34) | copy-start | bytes 1572868
  758.3 16.2 %copy-start.26 = (bf16[600,1024]{1,0:T(8,128)(2,1)S(1)}, bf16[600,1024]{1,0:T(8,128)(2,1)}, u32[]{:S(2)}) copy-start(bf16[600,1024]{1,0:T(8,128)(2,1)} %param.22) | copy-start | bytes 3686404
  758.3 16.2 %copy-start.31 = (bf16[1024,88]{0,1:T(8,128)(2,1)S(1)}, bf16[1024,88]{0,1:T(8,128)(2,1)}, u32[]{:S(2)}) copy-start(bf16[1024,88]{0,1:T(8,128)(2,1)} %param.28) | copy-start | bytes 540676
  802.0 9.4 copy-start.3
  814.6 6.4 copy-start.36
  822.9 11.5 slice-start
  825.9 8.5 slice-start.1
  937.9 10.2 copy-start.8
  937.9 119.2 %copy-start.16 = (pred[64,128]{1,0:T(8,128)(4,1)S(1)}, pred[64,128]{1,0:T(8,128)(4,1)}, u32[]{:S(2)}) copy-start(pred[64,128]{1,0:T(8,128)(4,1)} %copy-done.15) | copy-start | bytes 24580
  938.0 119.2 %all-to-all-start.2 = ((f32[64,128,256]{2,1,0:T(8,128)}), f32[64,128,256]{2,1,0:T(8,128)}, u32[]{:S(2)}, u32[]{:S(2)}) async-start(f32[64,128,256]{2,1,0:T(8,128)} %bitcast.55), calls=%async_computation.2 | async-start | bytes 16777216 | tf_op jit(solution)/shard_map/all_to_all | solution.py:134
  948.1 360.3 %all-reduce.5.cloned.1.call-start = ((), (), s32[]{:S(2)}) async-start(), calls=%async_computation.3 | async-start | bytes 16777216 | tf_op jit(solution)/shard_map/psum | solution.py:141
  1308.4 15.0 %slice-start.2 = ((s8[8388608]{0:T(1024)(128)(4,1)}), s8[4194304]{0:T(1024)(128)(4,1)S(1)}, s32[]{:S(2)}) async-start(s8[8388608]{0:T(1024)(128)(4,1)} %bitcast.59), calls=%async_computation.7 | async-start | bytes 8388608
  1314.6 8.9 slice-start.3
  1323.5 9.0 copy-start.1
  (26 other events, 101.6 us)
Sparse Core Ops, SparseCore 0:
  930.7 332.0 all-reduce.6
  1265.4 42.9 all-reduce.4
where the time goes:
time: 1350 us; the launch traced here: 1340 us
  other arithmetic  725 us (54%)
  waiting for transfers between devices  229 us (17%)
  local copies, waits for them, and re-layouts  154 us (11%)
  matrix products  110 us (8%)
  blocking collectives  89.7 us (7%)
  between operations  17.6 us (1%)
  starting transfers between devices  16 us (1%)
    unnamed x7, other arithmetic  561 us
    all_to_all x1, waiting for transfers between devices, local(): lax.all_to_all(slot_grad, 'wide', split_axis=0, concat_axis=0, tiled=True)  109 us
    psum x1, waiting for transfers between devices, local(): lax.psum((hot_grad, word_grad, out_grad, w_first_grad, b_first_grad, w_se...  74.4 us
    psum x1, blocking collectives, local(): lax.psum((hot_grad, word_grad, out_grad, w_first_grad, b_first_grad, w_se...  69.2 us
    dot_general x8, matrix products, left_product(): lax.dot_general(first_op, second_op, (((0,), (0,)), ((), ())), preferred_...  60.9 us
    scatter-add x1, other arithmetic, local(): jax.ops.segment_sum(owed.reshape(-1, feat_width), jnp.clip(asked_ids, 0,...  50.5 us
    convert_element_type x2, local copies, waits for them, and re-layouts, count_table(): return counts.astype(jnp.bfloat16)  48.8 us
    psum x1, waiting for transfers between devices, local(): tail_grad = lax.psum(tail_local, 'group')  45.6 us
  transfers between devices with their start and end apart: 4, of which 3 were waited for; matrix products, arithmetic and copies ran while one was open for 56% of the time, Pallas kernels for 0%

commit v1 on v0

v1 whole, which is shorter than its diff:
```python
import functools

import jax
import jax.numpy as jnp
from jax import lax
from jax.experimental import pallas as pl
from jax.experimental.pallas import tpu as pltpu
from jax.sharding import PartitionSpec as P

BF = jnp.bfloat16
F32 = jnp.float32
LANES = 128
MIB = 1024 * 1024


def params(mib):
    return pltpu.CompilerParams(vmem_limit_bytes=mib * MIB)


def whole_vmem():
    return pl.BlockSpec(memory_space=pltpu.VMEM)


def whole_smem():
    return pl.BlockSpec(memory_space=pltpu.SMEM)


def counts_body(cuts, ids_ref, hot_ref, word_ref, *refs):
    count_refs = refs[: len(cuts)]
    hist_ref, word_sum_ref, scratch, low_ref, high_ref = refs[len(cuts) :]
    block = ids_ref.shape[0]
    groups = sum(cuts)
    rows = groups + 8
    ids = ids_ref[...]
    low_ref[...] = (ids & (LANES - 1)).astype(F32)
    place = lax.broadcasted_iota(jnp.int32, ids.shape, 0) & 7
    high_ref[...] = (jnp.where(ids < 0, -64, ids >> 7) + place).astype(F32)
    low_iota = lax.broadcasted_iota(jnp.int32, (LANES, LANES), 0).astype(BF)
    high_iota = lax.broadcasted_iota(jnp.int32, (rows, LANES), 0).astype(BF)
    one = jnp.ones((), BF)
    zero = jnp.zeros((), BF)
    unroll = block

    def build(i, carry):
        for k in range(unroll):
            e = i * unroll + k
            low = jnp.broadcast_to(low_ref[pl.ds(e, 1), :], (LANES, LANES)).astype(BF)
            high = jnp.broadcast_to(high_ref[pl.ds(e, 1), :], (rows, LANES)).astype(BF)
            low_hot = jnp.where(low_iota == low, one, zero)
            high_hot = jnp.where(high_iota == high, one, zero)
            scratch[pl.ds(pl.multiple_of(e * rows, 8), rows), :] = right_product(high_hot, low_hot)
        return carry

    lax.fori_loop(0, block // unroll, build, 0)

    def regroup(i, carry):
        base = i * 16 * rows
        here = pl.ds(pl.multiple_of(i * 16, 16), 16)
        g = 0
        for ref, cut in zip(count_refs, cuts):
            for c in range(cut):
                upper = scratch[pl.ds(base + g, 8, stride=rows + 1), :]
                lower = scratch[pl.ds(base + 8 * rows + g, 8, stride=rows + 1), :]
                both = jnp.concatenate([upper, lower], axis=0)
                ref[here, c * LANES : (c + 1) * LANES] = both.astype(BF)
                g += 1
        return carry

    lax.fori_loop(0, block // 16, regroup, 0)
    hist_ref[...] = jnp.dot(count_refs[0][...], hot_ref[...], preferred_element_type=F32)
    word_sum_ref[...] = jnp.dot(count_refs[-1][...], word_ref[...], preferred_element_type=F32)


def counts_call(ids, hot, word, tail_rows, block=128):
    n = ids.shape[0]
    feat = hot.shape[1]
    widths = (hot.shape[0], tail_rows, word.shape[0])
    cuts = tuple(w // LANES for w in widths)
    rows_of = lambda w: pl.BlockSpec((block, w), lambda i: (i, 0))
    fixed = lambda s: pl.BlockSpec(s, lambda i: (0, 0))
    return pl.pallas_call(
        functools.partial(counts_body, cuts),
        grid=(n // block,),
        in_specs=[rows_of(LANES), fixed(hot.shape), fixed(word.shape)],
        out_specs=[rows_of(w) for w in widths] + [rows_of(feat)] * 2,
        out_shape=[jax.ShapeDtypeStruct((n, w), BF) for w in widths]
        + [jax.ShapeDtypeStruct((n, feat), F32)] * 2,
        scratch_shapes=[pltpu.VMEM((block * (sum(cuts) + 8), LANES), F32)]
        + [pltpu.VMEM((block, LANES), F32)] * 2,
        compiler_params=params(56),
        name="counts",
    )(ids, hot, word)


def gather_body(unroll, ids_ref, table_ref, out_ref, wide, picked):
    rows = table_ref.shape[0]
    count = out_ref.shape[0]

    def widen(i, carry):
        t = table_ref[pl.ds(pl.multiple_of(i * 64, 64), 64), :].astype(F32)
        wide[pl.ds(i * 128, 64, stride=2), :] = t[:, :LANES]
        wide[pl.ds(i * 128 + 1, 64, stride=2), :] = t[:, LANES:]
        return carry

    lax.fori_loop(0, rows // 64, widen, 0)

    def pick(i, carry):
        for k in range(unroll):
            at = i * unroll + k
            picked[pl.ds(at * 2, 2), :] = wide[pl.ds(ids_ref[at] * 2, 2), :]
        return carry

    lax.fori_loop(0, count // unroll, pick, 0)

    def join(i, carry):
        left = picked[pl.ds(i * 128, 64, stride=2), :]
        right = picked[pl.ds(i * 128 + 1, 64, stride=2), :]
        out_ref[pl.ds(pl.multiple_of(i * 64, 64), 64), :] = jnp.concatenate(
            [left, right], axis=1
        ).astype(BF)
        return carry

    lax.fori_loop(0, count // 64, join, 0)


def gather_call(ids, table, unroll=32):
    rows, feat = table.shape
    count = ids.shape[0]
    return pl.pallas_call(
        functools.partial(gather_body, unroll),
        in_specs=[whole_smem(), whole_vmem()],
        out_specs=whole_vmem(),
        out_shape=jax.ShapeDtypeStruct((count, feat), BF),
        scratch_shapes=[
            pltpu.VMEM((2 * rows, LANES), F32),
            pltpu.VMEM((2 * count, LANES), F32),
        ],
        compiler_params=params(48),
        name="gather_rows",
    )(ids, table)


def add_rows_body(unroll, ids_ref, again_ref, clash_ref, rows_ref, out_ref, total_a, total_b, wide):
    count = rows_ref.shape[0]
    rows = out_ref.shape[0]

    def clear(i, carry):
        for total in (total_a, total_b):
            total[pl.ds(pl.multiple_of(i * 256, 256), 256), :] = jnp.zeros((256, LANES), F32)
        return carry

    lax.fori_loop(0, rows // 128, clear, 0)

    def widen(i, carry):
        t = rows_ref[pl.ds(pl.multiple_of(i * 128, 128), 128), :].astype(F32)
        wide[pl.ds(i * 256, 128, stride=2), :] = t[:, :LANES]
        wide[pl.ds(i * 256 + 1, 128, stride=2), :] = t[:, LANES:]
        return carry

    lax.fori_loop(0, count // 128, widen, 0)

    def given(at):
        return wide[pl.ds(at * 2, 2), :]

    def add(i, carry):
        for total, base in ((total_a, i * 2 * unroll), (total_b, (i * 2 + 1) * unroll)):
            places = [pl.ds(ids_ref[base + k] * 2, 2) for k in range(unroll)]
            sums = [total[p, :] + given(base + k) for k, p in enumerate(places)]
            for p, v in zip(places, sums):
                total[p, :] = v
        return carry

    lax.fori_loop(0, count // (2 * unroll), add, 0)

    groups = count // unroll
    section = 16

    def check(i, carry):
        @pl.when(clash_ref[groups + i] != 0)
        def _():
            def add_again(j, inner):
                group = i * section + j

                @pl.when(clash_ref[group] != 0)
                def _():
                    for k in range(unroll):
                        p = pl.ds(again_ref[group * unroll + k] * 2, 2)
                        total_a[p, :] = total_a[p, :] + given(group * unroll + k)

                return inner

            lax.fori_loop(0, section, add_again, 0)

        return carry

    lax.fori_loop(0, groups // section, check, 0)

    def join(i, carry):
        left = pl.ds(i * 256, 128, stride=2)
        right = pl.ds(i * 256 + 1, 128, stride=2)
        both = [total_a[p, :] + total_b[p, :] for p in (left, right)]
        out_ref[pl.ds(pl.multiple_of(i * 128, 128), 128), :] = jnp.concatenate(both, axis=1).astype(
            out_ref.dtype
        )
        return carry

    lax.fori_loop(0, rows // 128, join, 0)


def row_plan(ids, rows, unroll):
    grouped = ids.reshape(-1, unroll)
    spare = rows + lax.broadcasted_iota(jnp.int32, grouped.shape, 1)
    earlier = lax.broadcasted_iota(jnp.int32, (unroll, unroll), 1) < lax.broadcasted_iota(
        jnp.int32, (unroll, unroll), 0
    )
    same = (grouped[:, :, None] == grouped[:, None, :]) & earlier[None]
    twice = jnp.any(same, axis=2) & (grouped >= 0)
    once = jnp.where((grouped >= 0) & ~twice, grouped, spare)
    again = jnp.where(twice, grouped, spare)
    clash = jnp.any(twice, axis=1).astype(jnp.int32)
    sections = jnp.max(clash.reshape(-1, 16), axis=1)
    return once.reshape(-1), again.reshape(-1), jnp.concatenate([clash, sections])


def add_rows_call(plan, given, rows, unroll):
    count, feat = given.shape
    return pl.pallas_call(
        functools.partial(add_rows_body, unroll),
        in_specs=[whole_smem()] * 3 + [whole_vmem()],
        out_specs=whole_vmem(),
        out_shape=jax.ShapeDtypeStruct((rows, feat), BF),
        scratch_shapes=[pltpu.VMEM((2 * (rows + unroll), LANES), F32)] * 2
        + [pltpu.VMEM((2 * count, LANES), F32)],
        compiler_params=params(48),
        name="add_rows",
        cost_estimate=pl.CostEstimate(flops=0, bytes_accessed=0, transcendentals=0),
    )(*plan, given)


def spread_body(pairs, *refs):
    for i in range(pairs):
        counts_ref, part_ref, out_ref = refs[2 * i], refs[2 * i + 1], refs[2 * pairs + i]
        out_ref[...] = left_product(counts_ref[...], part_ref[...]).astype(BF)


def spread_call(counts, parts, steps):
    n, feat = parts[0].shape
    specs, args = [], []
    for c, p in zip(counts, parts):
        specs += [
            pl.BlockSpec((n, c.shape[1] // steps), lambda i: (0, i)),
            pl.BlockSpec(p.shape, lambda i: (0, 0)),
        ]
        args += [c, p]
    return pl.pallas_call(
        functools.partial(spread_body, len(counts)),
        grid=(steps,),
        in_specs=specs,
        out_specs=[pl.BlockSpec((c.shape[1] // steps, feat), lambda i: (i, 0)) for c in counts],
        out_shape=[jax.ShapeDtypeStruct((c.shape[1], feat), BF) for c in counts],
        compiler_params=params(48),
        name="spread",
    )(*args)


def widen_body(blocked, *refs):
    given, outs = refs[: blocked + 4], refs[blocked + 4 :]
    for x_ref, out_ref in zip(given[:blocked], outs[:blocked]):
        out_ref[...] = x_ref[...].astype(F32)
    own_ref, other_ref, first_ref, last_ref = given[blocked:]
    tail_ref, first_out_ref, last_out_ref, small_ref = outs[blocked:]
    tail_ref[...] = own_ref[...].astype(F32) + other_ref[...].astype(F32)

    @pl.when(pl.program_id(0) == 0)
    def _():
        rows = last_out_ref.shape[0]
        first_out_ref[...] = first_ref[...].astype(F32)
        last_out_ref[...] = last_ref[:rows, :].astype(F32)
        small_ref[...] = last_ref[rows:, :].astype(F32)


def widen_call(arrays, own, other, first, last, last_rows, steps):
    spec = lambda a: pl.BlockSpec((a.shape[0] // steps, a.shape[1]), lambda i: (i, 0))
    shapes = [a.shape for a in (*arrays, own, first)]
    shapes += [(last_rows, last.shape[1]), (last.shape[0] - last_rows, last.shape[1])]
    return pl.pallas_call(
        functools.partial(widen_body, len(arrays)),
        grid=(steps,),
        in_specs=[spec(a) for a in (*arrays, own, other)] + [whole_vmem()] * 2,
        out_specs=[spec(a) for a in (*arrays, own)] + [whole_vmem()] * 3,
        out_shape=[jax.ShapeDtypeStruct(s, F32) for s in shapes],
        compiler_params=params(48),
        name="widen",
    )(*arrays, own, other, first, last)


def softmax_body(
    inv_count,
    chunk,
    mask_ref,
    table_ref,
    table_t_ref,
    user_ref,
    user_t_ref,
    label_ref,
    d_user_t_ref,
    grad_ref,
    loss_ref,
    logits,
    grad_sum,
):
    rows, feat = table_ref.shape
    block = user_ref.shape[0]
    chunks = rows // chunk
    step = pl.program_id(0)

    @pl.when(step == 0)
    def _():
        grad_sum[...] = jnp.zeros(grad_sum.shape, F32)

    label = label_ref[...]
    user_t = user_t_ref[...]
    user = user_ref[...]
    iota = lax.broadcasted_iota(jnp.int32, (chunk, block), 0)

    def at(c):
        return pl.ds(pl.multiple_of(c * chunk, chunk), chunk)

    def fold(v, op):
        return op(v.reshape(chunk // 8, 8, block), axis=0)

    def first(c, carry):
        peak, pos = carry
        s = jnp.dot(table_ref[at(c), :], user_t, preferred_element_type=F32)
        pos = pos + fold(jnp.where(iota == label - c * chunk, s, 0.0), jnp.sum)
        s = s + jnp.concatenate([mask_ref[at(c), :]] * (block // LANES), axis=1)
        logits[at(c), :] = s
        return jnp.maximum(peak, fold(s, jnp.max)), pos

    peak, pos = lax.fori_loop(
        0,
        chunks,
        first,
        (jnp.full((8, block), -jnp.inf, F32), jnp.zeros((8, block), F32)),
    )
    pos = jnp.sum(pos, axis=0, keepdims=True)
    peak = jnp.maximum(jnp.max(peak, axis=0, keepdims=True), pos)

    def second(c, total):
        p = jnp.exp(logits[at(c), :] - peak)
        logits[at(c), :] = p
        return total + fold(p, jnp.sum)

    total = lax.fori_loop(0, chunks, second, jnp.zeros((8, block), F32))
    pos_exp = jnp.exp(pos - peak)
    total = jnp.sum(total, axis=0, keepdims=True) + pos_exp
    loss_ref[...] = peak + jnp.log(total) - pos
    scale = inv_count / total
    d_pos = (pos_exp / total - 1.0) * inv_count

    def third(c, d_user_t):
        d = logits[at(c), :] * scale
        d = jnp.where(iota == label - c * chunk, d + d_pos, d).astype(BF)
        grad_sum[at(c), :] += jnp.dot(d, user, preferred_element_type=F32)
        return d_user_t + jnp.dot(table_t_ref[:, at(c)], d, preferred_element_type=F32)

    d_user_t = lax.fori_loop(0, chunks, third, jnp.zeros((feat, block), F32))
    d_user_t_ref[...] = d_user_t.astype(BF)

    @pl.when(step == pl.num_programs(0) - 1)
    def _():
        grad_ref[...] = grad_sum[...].astype(BF)


def softmax_call(mask, table, user, labels, block=512, chunk=2048):
    n, feat = user.shape
    rows = table.shape[0]
    across = lambda h: pl.BlockSpec((h, block), lambda i: (0, i))
    return pl.pallas_call(
        functools.partial(softmax_body, 1.0 / n, chunk),
        grid=(n // block,),
        in_specs=[
            whole_vmem(),
            whole_vmem(),
            whole_vmem(),
            pl.BlockSpec((block, feat), lambda i: (i, 0)),
            across(feat),
            across(1),
        ],
        out_specs=[across(feat), whole_vmem(), across(1)],
        out_shape=[
            jax.ShapeDtypeStruct((feat, n), BF),
            jax.ShapeDtypeStruct((rows, feat), BF),
            jax.ShapeDtypeStruct((1, n), F32),
        ],
        scratch_shapes=[pltpu.VMEM((rows, block), F32), pltpu.VMEM((rows, feat), F32)],
        compiler_params=params(46),
        name="sampled_softmax",
    )(mask, table, table.T, user, user.T, labels.reshape(1, n))


def sampled_mask(negatives, rows):
    high = lax.broadcasted_iota(jnp.int32, (rows // LANES, negatives.shape[0]), 0)
    low = lax.broadcasted_iota(jnp.int32, (LANES, negatives.shape[0]), 0)
    high_hot = (high == negatives[None, :] // LANES).astype(BF)
    low_hot = (low == negatives[None, :] % LANES).astype(BF)
    sampled = right_product(high_hot, low_hot).reshape(rows, 1)
    return jnp.broadcast_to(jnp.where(sampled > 0.5, F32(0.0), F32(-1e30)), (rows, LANES))


def left_product(first_op, second_op):
    return lax.dot_general(
        first_op, second_op, (((0,), (0,)), ((), ())), preferred_element_type=F32
    )


def right_product(first_op, second_op):
    return lax.dot_general(
        first_op, second_op, (((1,), (1,)), ((), ())), preferred_element_type=F32
    )


def gelu_back(pre_value, d_act):
    unused, pull = jax.vjp(jax.nn.gelu, pre_value)
    return pull(d_act)[0]


def in_range_ids(ids, lengths, offset):
    slot = lax.broadcasted_iota(jnp.int32, ids.shape, 1)
    kept = jnp.where(slot < lengths[:, None], ids + offset, -1)
    return jnp.pad(kept, ((0, 0), (0, LANES // 2 - ids.shape[1])), constant_values=-1)


def local(
    hot_table,
    tail_table,
    word_table,
    out_table,
    w_first,
    b_first,
    w_second,
    b_second,
    w_third,
    b_third,
    dense_feats,
    hist_ids,
    hist_len,
    search_ids,
    search_len,
    requests,
    labels,
    negatives,
):
    feat = hot_table.shape[1]
    hot_rows = hot_table.shape[0]
    owners, per_owner = requests.shape
    slots = owners * per_owner
    examples_dev = hist_ids.shape[0]
    examples_all = examples_dev * lax.axis_size("group") * lax.axis_size("wide")
    shard_rows = tail_table.shape[0]
    hist_float = hist_len[:, None].astype(F32)
    search_float = search_len[:, None].astype(F32)

    asked = lax.all_to_all(requests, "wide", split_axis=0, concat_axis=0, tiled=True)
    asked = asked.reshape(slots)
    looked = gather_call(jnp.maximum(asked, 0), tail_table)
    returned = lax.all_to_all(
        looked.reshape(owners, per_owner, feat), "wide", split_axis=0, concat_axis=0, tiled=True
    ).reshape(slots, feat)

    ids = jnp.concatenate(
        [
            in_range_ids(hist_ids, hist_len, 0),
            in_range_ids(search_ids, search_len, hot_rows + slots),
        ],
        axis=1,
    )
    mask = sampled_mask(negatives, out_table.shape[0])
    unroll = 16
    plan = row_plan(asked, shard_rows, unroll)
    ids, mask, plan, looked = lax.optimization_barrier((ids, mask, plan, looked))
    hot_counts, slot_counts, word_counts, hot_sum, word_sum = counts_call(
        ids, hot_table, word_table, slots
    )

    hist_mean = (hot_sum + jnp.dot(slot_counts, returned, preferred_element_type=F32)) / hist_float
    search_mean = word_sum / search_float
    inputs = jnp.concatenate([hist_mean, search_mean, dense_feats.astype(F32)], axis=1).astype(BF)
    pre_first = jnp.dot(inputs, w_first, preferred_element_type=F32) + b_first.astype(F32)
    act_first = jax.nn.gelu(pre_first).astype(BF)
    pre_second = jnp.dot(act_first, w_second, preferred_element_type=F32) + b_second.astype(F32)
    act_second = jax.nn.gelu(pre_second).astype(BF)
    user = (jnp.dot(act_second, w_third, preferred_element_type=F32) + b_third.astype(F32)).astype(
        BF
    )

    d_user_t, out_grad, per_example = softmax_call(mask, out_table, user, labels)
    d_user = d_user_t.T
    d_pre_second = gelu_back(pre_second, right_product(d_user, w_third)).astype(BF)
    d_pre_first = gelu_back(pre_first, right_product(d_pre_second, w_second)).astype(BF)
    d_inputs = right_product(d_pre_first, w_first[: 2 * feat])
    hist_part = (d_inputs[:, :feat] / hist_float).astype(BF)
    word_part = (d_inputs[:, feat:] / search_float).astype(BF)

    hot_grad, word_grad = spread_call((hot_counts, word_counts), (hist_part, word_part), 4)
    w1_grad = left_product(inputs, d_pre_first).astype(BF)
    w2_grad = left_product(act_first, d_pre_second).astype(BF)
    w3_grad = left_product(act_second, d_user).astype(BF)
    small = [
        per_example,
        jnp.sum(d_pre_first.astype(F32), axis=0),
        jnp.sum(d_pre_second.astype(F32), axis=0),
        jnp.sum(d_user.astype(F32), axis=0),
    ]
    small_rows = jnp.concatenate([x.reshape(-1, feat) for x in small], axis=0).astype(BF)
    w3_rows = w3_grad.shape[0]
    small_rows = jnp.pad(small_rows, ((0, -small_rows.shape[0] % 16), (0, 0)))
    packed = (
        hot_grad,
        word_grad,
        out_grad,
        w1_grad,
        w2_grad,
        jnp.concatenate([w3_grad, small_rows], axis=0),
    )
    packed, hist_part = lax.optimization_barrier((packed, hist_part))
    summed = lax.psum(packed, ("group", "wide"))

    (slot_grad,) = spread_call((slot_counts,), (hist_part,), 4)
    owed = lax.all_to_all(
        slot_grad.reshape(owners, per_owner, feat), "wide", split_axis=0, concat_axis=0, tiled=True
    ).reshape(slots, feat)
    own = add_rows_call(plan, owed, shard_rows, unroll)
    other = lax.ppermute(own, "group", [(0, 1), (1, 0)])
    hot_all, word_all, out_all, w2_all, tail_grad, w1_all, w3_all, small_all = widen_call(
        (summed[0], summed[1], summed[2], summed[4]), own, other, summed[3], summed[5], w3_rows, 4
    )
    small_sums = []
    start = 0
    for x in small:
        small_sums.append(small_all[start : start + x.size // feat].reshape(-1))
        start += x.size // feat
    loss_all, b1_all, b2_all, b3_all = small_sums
    loss_value = jnp.sum(loss_all) / examples_all
    return (
        loss_value,
        hot_all,
        tail_grad,
        word_all,
        out_all,
        w1_all,
        b1_all,
        w2_all,
        b2_all,
        w3_all,
        b3_all,
    )


def solution(mesh):
    split = ("group", "wide")
    in_specs = (
        (P(), P("wide", None))
        + (P(),) * 8
        + (P(split, None), P(split, None), P(split), P(split, None), P(split), P(split, None))
        + (P(split), P())
    )
    out_specs = (P(), P(), P("wide", None)) + (P(),) * 8
    return jax.shard_map(local, mesh=mesh, in_specs=in_specs, out_specs=out_specs, check_vma=False)
```

time: 1350 us -> 439 us (0.33)
  other arithmetic: 725 us -> 7.3 us
  Pallas kernels: 0 us -> 137 us
  local copies, waits for them, and re-layouts: 154 us -> 23.8 us
  blocking collectives: 89.7 us -> 0 us
  matrix products: 110 us -> 34.1 us
  waiting for transfers between devices: 229 us -> 185 us
  starting transfers between devices: 16 us -> 34.1 us
    unnamed x7 -> x1, other arithmetic: 561 us -> 0.6 us
    pallas_call x0 -> x7, Pallas kernels: none -> 137 us  [the longest x1 36.6 us: counts_call(): pl.pallas_call(functools.partial(counts_body, cuts), grid=(n // block,),...]
    scatter-add x3 -> x0, other arithmetic: 92.9 us -> none  [the longest x1 50.5 us: local(): jax.ops.segment_sum(owed.reshape(-1, feat_width), jnp.clip(asked_ids, 0,...]
    psum x1 -> x0, blocking collectives: 69.2 us -> none  [local(): lax.psum((hot_grad, word_grad, out_grad, w_first_grad, b_first_grad, w_se...]
    gather x4 -> x0, local copies, waits for them, and re-layouts: 63.6 us -> none  [the longest x1 33.9 us: local(): jnp.take(tail_table, jnp.clip(asked_ids, 0, shard_rows - 1), axis=0)]
    dot_general x8 -> x3, matrix products: 60.9 us -> 5.27 us  [left_product(): lax.dot_general(first_op, second_op, (((0,), (0,)), ((), ())), preferred_...]
    convert_element_type x4 -> x2, local copies, waits for them, and re-layouts: 49.7 us -> 0.28 us  [the longest x1 0.2 us: local(): (jnp.dot(act_second, w_third, preferred_element_type=F32) + b_third.astyp...]
    all_to_all x2 -> x3, waiting for transfers between devices: 109 us -> 62.1 us  [the longest x1 53.3 us: local(): lax.all_to_all(slot_grad.reshape(owners, per_owner, feat), 'wide', split_...]
  transfers between devices with their start and end apart: 4 -> 5, of which waited for: 3 -> 4; matrix products, arithmetic and copies ran while one was open for 56% -> 3% of each run, Pallas kernels for 0% -> 13%
where the time goes in v1:
time: 439 us; the launch traced here: 438 us
  waiting for transfers between devices  185 us (42%)
  Pallas kernels  137 us (31%)
  starting transfers between devices  34.1 us (8%)
  matrix products  34.1 us (8%)
  local copies, waits for them, and re-layouts  23.8 us (5%)
  between operations  16.4 us (4%)
  other arithmetic  7.3 us (2%)
    psum x1, waiting for transfers between devices, local(): summed = lax.psum(packed, ('group', 'wide'))  122 us
    all_to_all x1, waiting for transfers between devices, local(): lax.all_to_all(slot_grad.reshape(owners, per_owner, feat), 'wide', split_...  53.3 us
    pallas_call x1, Pallas kernels, counts_call(): pl.pallas_call(functools.partial(counts_body, cuts), grid=(n // block,),...  36.6 us
    pallas_call x1, Pallas kernels, softmax_call(): pl.pallas_call(functools.partial(softmax_body, 1.0 / n, chunk), grid=(n /...  31.4 us
    pallas_call x1, Pallas kernels, add_rows_call(): pl.pallas_call(functools.partial(add_rows_body, unroll), in_specs=[whole_...  20.7 us
    pallas_call x2, Pallas kernels, spread_call(): pl.pallas_call(functools.partial(spread_body, len(counts)), grid=(steps,)...  19.1 us
    unnamed x69, local copies, waits for them, and re-layouts  19 us
    pallas_call x1, Pallas kernels, widen_call(): pl.pallas_call(functools.partial(widen_body, len(arrays)), grid=(steps,),...  15.3 us
  transfers between devices with their start and end apart: 5, of which 4 were waited for; matrix products, arithmetic and copies ran while one was open for 3% of the time, Pallas kernels for 13%

profile of v1, /device:TPU:1, one launch (start us, length us, event | category | flops | bytes accessed | tf_op | source)
XLA Modules:
  0.0 437.7 jit_solution(17618548270974422713)
XLA Ops:
  7.2 12.1 %all-to-all-start = ((s32[64,1,128]{2,1,0:T(1,128)}), s32[64,1,128]{2,1,0:T(1,128)S(1)}, u32[]{:S(2)}, u32[]{:S(2)}) async-start(s32[64,1,128]{2,1,0:T(1,128)} %bitcast.41), calls=%async_computation | async-start | bytes 65536 | tf_op jit(solution)/shard_map/all_to_all | solution.py:464
  19.5 8.1 %all-to-all-done = s32[64,1,128]{2,1,0:T(1,128)S(1)} async-done(((s32[64,1,128]{2,1,0:T(1,128)}), s32[64,1,128]{2,1,0:T(1,128)S(1)}, u32[]{:S(2)}, u32[]{:S(2)}) %all-to-all-start) | async-done | bytes 32800 | tf_op jit(solution)/shard_map/all_to_all | solution.py:464
  29.7 13.9 %gather_rows.1 = bf16[8192,256]{1,0:T(8,128)(2,1)S(1)} custom-call(s32[8192]{0:T(1024)S(1)} %get-tuple-element.81.ids_ref, bf16[8192,256]{1,0:T(8,128)(2,1)} %table_ref.2), custom_call_target="tpu_custom_call" | custom-call | tf_op jit(solution)/shard_map/gather_rows/pallas_call | solution.py:129
  43.6 2.0 copy-done.2
  45.7 6.0 %all-to-all-start.1 = ((bf16[64,128,256]{2,1,0:T(8,128)(2,1)}), bf16[64,128,256]{2,1,0:T(8,128)(2,1)}, u32[]{:S(2)}, u32[]{:S(2)}) async-start(bf16[64,128,256]{2,1,0:T(8,128)(2,1)} %bitcast.35), calls=%async_computation.1 | async-start | bytes 8388608 | tf_op jit(solution)/shard_map/all_to_all | solution.py:467
  52.4 6.4 %copy.56 = bf16[8192,256]{0,1:T(8,128)(2,1)} copy(bf16[8192,256]{1,0:T(8,128)(2,1)} %table_ref.3) | data formatting | bytes 8388608 | tf_op args[3]
  61.1 2.6 broadcast_in_dim.18.mask_ref
  63.7 36.6 %counts.1 = (bf16[1024,4096]{1,0:T(8,128)(2,1)}, bf16[1024,8192]{1,0:T(8,128)(2,1)}, bf16[1024,4096]{1,0:T(8,128)(2,1)}, f32[1024,256]{1,0:T(8,128)}, f32[1024,256]{1,0:T(8,128)}) custom-call(s32[1024,128]{1,0:T(8,128)} %select_add_fusion.ids_ref, bf16[4096,256]{1,0:T(8,128)(2,1)} %hot_ref.1, bf16[4096,256]{1,0:T(8,128)(2,1)} %word_ref.1), custom_call_target="tpu_custom_call" | custom-call | tf_op jit(solution)/shard_map/counts/pallas_call | solution.py:81
  102.4 11.8 %fusion.18 = bf16[1024,256]{1,0:T(8,128)(2,1)S(1)} fusion(f32[1024,256]{1,0:T(8,128)} %get-tuple-element.44, bf16[1024,8192]{1,0:T(8,128)(2,1)} %get-tuple-element.45.refs_0_, bf16[8192,256]{1,0:T(8,128)(2,1)} %bitcast.5, f32[1024]{0:T(1024)S(1)} %convert_element_type.78), kind=kOutput, calls=%fused_computation.31 | convolution fusion | flops 4295753728 | bytes 22548480 | tf_op jit(solution)/shard_map/dot_general | solution.py:486
  114.3 4.2 multiply_convert_fusion
  118.5 3.0 multiply_convert_fusion.1
  123.2 31.4 %sampled_softmax.1 = (bf16[256,1024]{1,0:T(8,128)(2,1)S(1)}, bf16[8192,256]{1,0:T(8,128)(2,1)S(1)}, f32[1,1024]{1,0:T(1,128)S(1)}) custom-call(f32[8192,128]{1,0:T(8,128)} %broadcast_in_dim.18.mask_ref, bf16[8192,256]{1,0:T(8,128)(2,1)} %table_ref.3, bf16[256,8192]{1,0:T(8,128)(2,1)} %bitcast.39, bf16[1024,256]{1,0:T(8,128)(2,1)S(1)} %copy.60.user_ref, ...), custom_call_target="tpu_custom_call" | custom-call | tf_op jit(solution)/shard_map/sampled_softmax/pallas_call | solution.py:379
  157.7 2.3 convolution_convert_fusion.1
  159.9 4.3 fusion.43
  164.2 2.5 convolution_convert_fusion
  166.7 2.6 fusion.24
  172.2 10.3 %spread.2 = (bf16[4096,256]{1,0:T(8,128)(2,1)}, bf16[4096,256]{1,0:T(8,128)(2,1)}) custom-call(bf16[1024,4096]{1,0:T(8,128)(2,1)} %get-tuple-element.42.refs_0_, bf16[1024,256]{1,0:T(8,128)(2,1)S(1)} %get-tuple-element.60.refs_1_, bf16[1024,4096]{1,0:T(8,128)(2,1)} %get-tuple-element.48.refs_2_, bf16[1024,256]{1,0:T(8,128)(2,1)S(1)} %get-tuple-element.77.refs_3_), custom_call_target="tpu_custom_call" | custom-call | tf_op jit(solution)/shard_map/spread/pallas_call | solution.py:255
  182.5 8.8 %spread.3 = bf16[8192,256]{1,0:T(8,128)(2,1)S(1)} custom-call(bf16[1024,8192]{1,0:T(8,128)(2,1)} %get-tuple-element.45.refs_0_, bf16[1024,256]{1,0:T(8,128)(2,1)S(1)} %get-tuple-element.60.refs_1_), custom_call_target="tpu_custom_call" | custom-call | tf_op jit(solution)/shard_map/spread/pallas_call | solution.py:255
  193.3 9.2 %all-to-all-start.2 = ((bf16[64,128,256]{2,1,0:T(8,128)(2,1)}), bf16[64,128,256]{2,1,0:T(8,128)(2,1)}, u32[]{:S(2)}, u32[]{:S(2)}) async-start(bf16[64,128,256]{2,1,0:T(8,128)(2,1)} %bitcast.36), calls=%async_computation.2 | async-start | bytes 8388608 | tf_op jit(solution)/shard_map/all_to_all | solution.py:530
  203.2 53.3 %all-to-all-done.2 = bf16[64,128,256]{2,1,0:T(8,128)(2,1)} async-done(((bf16[64,128,256]{2,1,0:T(8,128)(2,1)}), bf16[64,128,256]{2,1,0:T(8,128)(2,1)}, u32[]{:S(2)}, u32[]{:S(2)}) %all-to-all-start.2) | async-done | bytes 4194336 | tf_op jit(solution)/shard_map/all_to_all | solution.py:530
  256.5 20.7 %add_rows.1.refs_4_ = bf16[8192,256]{1,0:T(8,128)(2,1)} custom-call(s32[8192]{0:T(1024)S(1)} %get-tuple-element.57.ids_ref, s32[8192]{0:T(1024)S(1)} %get-tuple-element.58.again_ref, s32[544]{0:T(1024)S(1)} %pad_add_fusion.clash_ref, bf16[8192,256]{1,0:T(8,128)(2,1)} %bitcast.9.rows_ref), custom_call_target="tpu_custom_call" | custom-call | tf_op jit(solution)/shard_map/add_rows/pallas_call | solution.py:227
  277.2 6.8 %collective-permute-start = (bf16[8192,256]{1,0:T(8,128)(2,1)}, bf16[8192,256]{1,0:T(8,128)(2,1)}, u32[]{:S(2)}, u32[]{:S(2)}) collective-permute-start(bf16[8192,256]{1,0:T(8,128)(2,1)} %add_rows.1.refs_4_), channel_id=1, source_target_pairs={{0,64},{64,0},{1,65},{65,1},{2,66},{66,2},{3,67},{67,3},{4,68},{68... | collective-permute-start | bytes 12582920 | tf_op jit(solution)/shard_map/ppermute | solution.py:534
  284.0 122.3 %all-reduce.6.cloned.1.call-done = (bf16[4096,256]{1,0:T(8,128)(2,1)}, bf16[4096,256]{1,0:T(8,128)(2,1)}, bf16[8192,256]{1,0:T(8,128)(2,1)}, bf16[1024,512]{1,0:...) async-done(((bf16[4096,256]{1,0:T(8,128)(2,1)}, bf16[4096,256]{1,0:T(8,128)(2,1)}, bf16[8192,256]{1,0:T(8,128)(2,1)}, bf16[1024,512]{1,0:T(8,128)(2,1)}, ...) | async-done | bytes 10936336 | tf_op jit(solution)/shard_map/psum | solution.py:527
  411.4 15.3 %widen.1 = (f32[4096,256]{1,0:T(8,128)}, f32[4096,256]{1,0:T(8,128)}, f32[8192,256]{1,0:T(8,128)}, f32[1024,512]{1,0:T(8,128)}, f32[8192,256]{1,0:T(8,128)}, /*i...) custom-call(bf16[4096,256]{1,0:T(8,128)(2,1)S(1)} %copy-done.5, ...), custom_call_target="tpu_custom_call" | custom-call | tf_op jit(solution)/shard_map/widen/pallas_call | solution.py:286
  (113 shorter events, 24.9 us)
Async XLA Ops:
  7.2 111.3 %copy-start = (bf16[1024,512]{1,0:T(8,128)(2,1)S(1)}, bf16[1024,512]{1,0:T(8,128)(2,1)}, u32[]{:S(2)}) copy-start(bf16[1024,512]{1,0:T(8,128)(2,1)} %param.24) | copy-start | bytes 3145732
  7.2 20.4 %all-to-all-start = ((s32[64,1,128]{2,1,0:T(1,128)}), s32[64,1,128]{2,1,0:T(1,128)S(1)}, u32[]{:S(2)}, u32[]{:S(2)}) async-start(s32[64,1,128]{2,1,0:T(1,128)} %bitcast.41), calls=%async_computation | async-start | bytes 65536 | tf_op jit(solution)/shard_map/all_to_all | solution.py:464
  45.6 6.1 %copy-start.22 = (bf16[256]{0:T(256)(128)(2,1)S(1)}, bf16[256]{0:T(256)(128)(2,1)}, u32[]{:S(2)}) copy-start(bf16[256]{0:T(256)(128)(2,1)} %param.27) | copy-start | bytes 1540
  45.6 6.1 %copy-start.17 = (bf16[512]{0:T(512)(128)(2,1)S(1)}, bf16[512]{0:T(512)(128)(2,1)}, u32[]{:S(2)}) copy-start(bf16[512]{0:T(512)(128)(2,1)} %param.25) | copy-start | bytes 3076
  45.6 6.1 %copy-start.16 = (bf16[1024]{0:T(1024)(128)(2,1)S(1)}, bf16[1024]{0:T(1024)(128)(2,1)}, u32[]{:S(2)}) copy-start(bf16[1024]{0:T(1024)(128)(2,1)} %param.23) | copy-start | bytes 6148
  45.6 6.1 %copy-start.15 = (s32[1024]{0:T(1024)S(1)}, s32[1024]{0:T(1024)}, u32[]{:S(2)}) copy-start(s32[1024]{0:T(1024)} %param.30) | copy-start | bytes 12292
  45.6 6.1 %copy-start.14 = (s32[1024]{0:T(1024)S(1)}, s32[1024]{0:T(1024)}, u32[]{:S(2)}) copy-start(s32[1024]{0:T(1024)} %param.32) | copy-start | bytes 12292
  45.6 6.1 %copy-start.12 = (bf16[1024,88]{0,1:T(8,128)(2,1)S(1)}, bf16[1024,88]{0,1:T(8,128)(2,1)}, u32[]{:S(2)}) copy-start(bf16[1024,88]{0,1:T(8,128)(2,1)} %param.28) | copy-start | bytes 540676
  45.6 6.3 %copy-start.10 = (s32[1024,50]{0,1:T(8,128)S(1)}, s32[1024,50]{0,1:T(8,128)}, u32[]{:S(2)}) copy-start(s32[1024,50]{0,1:T(8,128)} %param.29) | copy-start | bytes 614404
  45.6 6.5 %copy-start.11 = (s32[1024,50]{0,1:T(8,128)S(1)}, s32[1024,50]{0,1:T(8,128)}, u32[]{:S(2)}) copy-start(s32[1024,50]{0,1:T(8,128)} %param.31) | copy-start | bytes 614404
  45.7 56.7 %all-to-all-start.1 = ((bf16[64,128,256]{2,1,0:T(8,128)(2,1)}), bf16[64,128,256]{2,1,0:T(8,128)(2,1)}, u32[]{:S(2)}, u32[]{:S(2)}) async-start(bf16[64,128,256]{2,1,0:T(8,128)(2,1)} %bitcast.35), calls=%async_computation.1 | async-start | bytes 8388608 | tf_op jit(solution)/shard_map/all_to_all | solution.py:467
  102.4 11.9 %copy-start.18 = (bf16[600,1024]{1,0:T(8,128)(2,1)S(1)}, bf16[600,1024]{1,0:T(8,128)(2,1)}, u32[]{:S(2)}) copy-start(bf16[600,1024]{1,0:T(8,128)(2,1)} %param.22) | copy-start | bytes 3686404
  114.3 4.2 copy-start.27
  118.5 3.0 copy-start.25
  118.5 4.0 copy-start.20
  123.2 31.4 %copy-start.24 = (bf16[1024,512]{1,0:T(8,128)(2,1)S(1)}, bf16[1024,512]{1,0:T(8,128)(2,1)}, u32[]{:S(2)}) copy-start(bf16[1024,512]{1,0:T(8,128)(2,1)} %copy-done.23) | copy-start | bytes 3145732
  123.2 31.9 %copy-start.21 = (bf16[512,256]{1,0:T(8,128)(2,1)S(1)}, bf16[512,256]{1,0:T(8,128)(2,1)}, u32[]{:S(2)}) copy-start(bf16[512,256]{1,0:T(8,128)(2,1)} %param.26) | copy-start | bytes 786436
  123.2 31.9 %copy-start.29 = (f32[1024,512]{1,0:T(8,128)S(1)}, f32[1024,512]{1,0:T(8,128)}, u32[]{:S(2)}) copy-start(f32[1024,512]{1,0:T(8,128)} %get-tuple-element.89) | copy-start | bytes 6291460
  159.9 4.3 copy-start.28
  164.2 2.5 copy-start.19
  193.3 63.2 %all-to-all-start.2 = ((bf16[64,128,256]{2,1,0:T(8,128)(2,1)}), bf16[64,128,256]{2,1,0:T(8,128)(2,1)}, u32[]{:S(2)}, u32[]{:S(2)}) async-start(bf16[64,128,256]{2,1,0:T(8,128)(2,1)} %bitcast.36), calls=%async_computation.2 | async-start | bytes 8388608 | tf_op jit(solution)/shard_map/all_to_all | solution.py:530
  202.5 203.9 %all-reduce.6.cloned.1.call-start = ((), (), s32[]{:S(2)}) async-start(), calls=%async_computation.3 | async-start | bytes 21872640 | tf_op jit(solution)/shard_map/psum | solution.py:527
  277.2 129.2 %collective-permute-start = (bf16[8192,256]{1,0:T(8,128)(2,1)}, bf16[8192,256]{1,0:T(8,128)(2,1)}, u32[]{:S(2)}, u32[]{:S(2)}) collective-permute-start(bf16[8192,256]{1,0:T(8,128)(2,1)} %add_rows.1.refs_4_), channel_id=1, source_target_pairs={{0,64},{64,0},{1,65},{65,1},{2,66},{66,2},{3,67},{67,3},{4,68},{68... | collective-permute-start | bytes 12582920 | tf_op jit(solution)/shard_map/ppermute | solution.py:534
  411.4 18.3 %copy-start.1 = (bf16[1024,512]{1,0:T(8,128)(2,1)S(1)}, bf16[1024,512]{1,0:T(8,128)(2,1)}, u32[]{:S(2)}) copy-start(bf16[1024,512]{1,0:T(8,128)(2,1)} %param.24) | copy-start | bytes 3145732
  (12 other events, 20.3 us)
Sparse Core Ops, SparseCore 0:
  210.6 195.7 all-reduce.5

commit v2 on v1

--- a/solution.py
+++ b/solution.py
@@ -54,21 +54,25 @@
     lax.fori_loop(0, block // unroll, build, 0)
 
     def regroup(i, carry):
-        base = i * 16 * rows
-        here = pl.ds(pl.multiple_of(i * 16, 16), 16)
+        here = pl.ds(pl.multiple_of(i * 32, 32), 32)
         g = 0
         for ref, cut in zip(count_refs, cuts):
             for c in range(cut):
-                upper = scratch[pl.ds(base + g, 8, stride=rows + 1), :]
-                lower = scratch[pl.ds(base + 8 * rows + g, 8, stride=rows + 1), :]
-                both = jnp.concatenate([upper, lower], axis=0)
-                ref[here, c * LANES : (c + 1) * LANES] = both.astype(BF)
+                eights = [
+                    scratch[pl.ds((i * 32 + e) * rows + g, 8, stride=rows + 1), :]
+                    for e in range(0, 32, 8)
+                ]
+                ref[here, c * LANES : (c + 1) * LANES] = jnp.concatenate(eights, axis=0).astype(
+                    jnp.int8
+                )
                 g += 1
         return carry
 
-    lax.fori_loop(0, block // 16, regroup, 0)
-    hist_ref[...] = jnp.dot(count_refs[0][...], hot_ref[...], preferred_element_type=F32)
-    word_sum_ref[...] = jnp.dot(count_refs[-1][...], word_ref[...], preferred_element_type=F32)
+    lax.fori_loop(0, block // 32, regroup, 0)
+    hist_ref[...] = jnp.dot(count_refs[0][...].astype(BF), hot_ref[...], preferred_element_type=F32)
+    word_sum_ref[...] = jnp.dot(
+        count_refs[-1][...].astype(BF), word_ref[...], preferred_element_type=F32
+    )
 
 
 def counts_call(ids, hot, word, tail_rows, block=128):
@@ -83,7 +87,7 @@
         grid=(n // block,),
         in_specs=[rows_of(LANES), fixed(hot.shape), fixed(word.shape)],
         out_specs=[rows_of(w) for w in widths] + [rows_of(feat)] * 2,
-        out_shape=[jax.ShapeDtypeStruct((n, w), BF) for w in widths]
+        out_shape=[jax.ShapeDtypeStruct((n, w), jnp.int8) for w in widths]
         + [jax.ShapeDtypeStruct((n, feat), F32)] * 2,
         scratch_shapes=[pltpu.VMEM((block * (sum(cuts) + 8), LANES), F32)]
         + [pltpu.VMEM((block, LANES), F32)] * 2,
@@ -95,54 +99,60 @@
 def gather_body(unroll, ids_ref, table_ref, out_ref, wide, picked):
     rows = table_ref.shape[0]
     count = out_ref.shape[0]
-
-    def widen(i, carry):
-        t = table_ref[pl.ds(pl.multiple_of(i * 64, 64), 64), :].astype(F32)
-        wide[pl.ds(i * 128, 64, stride=2), :] = t[:, :LANES]
-        wide[pl.ds(i * 128 + 1, 64, stride=2), :] = t[:, LANES:]
-        return carry
-
-    lax.fori_loop(0, rows // 64, widen, 0)
+    step = pl.program_id(0)
+
+    @pl.when(step == 0)
+    def _():
+        def widen(i, carry):
+            t = table_ref[pl.ds(pl.multiple_of(i * 128, 128), 128), :].astype(F32)
+            wide[pl.ds(i * 256, 128, stride=2), :] = t[:, :LANES]
+            wide[pl.ds(i * 256 + 1, 128, stride=2), :] = t[:, LANES:]
+            return carry
+
+        lax.fori_loop(0, rows // 128, widen, 0)
 
     def pick(i, carry):
         for k in range(unroll):
             at = i * unroll + k
-            picked[pl.ds(at * 2, 2), :] = wide[pl.ds(ids_ref[at] * 2, 2), :]
+            picked[pl.ds(at * 2, 2), :] = wide[pl.ds(ids_ref[step * count + at] * 2, 2), :]
         return carry
 
     lax.fori_loop(0, count // unroll, pick, 0)
 
     def join(i, carry):
-        left = picked[pl.ds(i * 128, 64, stride=2), :]
-        right = picked[pl.ds(i * 128 + 1, 64, stride=2), :]
-        out_ref[pl.ds(pl.multiple_of(i * 64, 64), 64), :] = jnp.concatenate(
+        left = picked[pl.ds(i * 256, 128, stride=2), :]
+        right = picked[pl.ds(i * 256 + 1, 128, stride=2), :]
+        out_ref[pl.ds(pl.multiple_of(i * 128, 128), 128), :] = jnp.concatenate(
             [left, right], axis=1
         ).astype(BF)
         return carry
 
-    lax.fori_loop(0, count // 64, join, 0)
-
-
-def gather_call(ids, table, unroll=32):
+    lax.fori_loop(0, count // 128, join, 0)
+
+
+def gather_call(ids, table, steps=1, unroll=64):
     rows, feat = table.shape
     count = ids.shape[0]
     return pl.pallas_call(
         functools.partial(gather_body, unroll),
+        grid=(steps,),
         in_specs=[whole_smem(), whole_vmem()],
-        out_specs=whole_vmem(),
+        out_specs=pl.BlockSpec((count // steps, feat), lambda i: (i, 0)),
         out_shape=jax.ShapeDtypeStruct((count, feat), BF),
         scratch_shapes=[
             pltpu.VMEM((2 * rows, LANES), F32),
-            pltpu.VMEM((2 * count, LANES), F32),
+            pltpu.VMEM((2 * count // steps, LANES), F32),
         ],
-        compiler_params=params(48),
+        compiler_params=params(60),
         name="gather_rows",
     )(ids, table)
 
 
-def add_rows_body(unroll, ids_ref, again_ref, clash_ref, rows_ref, out_ref, total_a, total_b, wide):
+def add_rows_body(unroll, ids_ref, again_ref, clash_ref, rows_ref, *refs):
+    out_refs, (total_a, total_b, wide) = refs[:-3], refs[-3:]
     count = rows_ref.shape[0]
-    rows = out_ref.shape[0]
+    part = out_refs[0].shape[0]
+    rows = part * len(out_refs)
 
     def clear(i, carry):
         for total in (total_a, total_b):
@@ -195,16 +205,17 @@
 
     lax.fori_loop(0, groups // section, check, 0)
 
-    def join(i, carry):
-        left = pl.ds(i * 256, 128, stride=2)
-        right = pl.ds(i * 256 + 1, 128, stride=2)
-        both = [total_a[p, :] + total_b[p, :] for p in (left, right)]
-        out_ref[pl.ds(pl.multiple_of(i * 128, 128), 128), :] = jnp.concatenate(both, axis=1).astype(
-            out_ref.dtype
-        )
-        return carry
-
-    lax.fori_loop(0, rows // 128, join, 0)
+    for n, out_ref in enumerate(out_refs):
+
+        def join(i, carry, n=n, out_ref=out_ref):
+            left = pl.ds(n * part * 2 + i * 256, 128, stride=2)
+            right = pl.ds(n * part * 2 + i * 256 + 1, 128, stride=2)
+            both = [total_a[p, :] + total_b[p, :] for p in (left, right)]
+            here = pl.ds(pl.multiple_of(i * 128, 128), 128)
+            out_ref[here, :] = jnp.concatenate(both, axis=1).astype(out_ref.dtype)
+            return carry
+
+        lax.fori_loop(0, part // 128, join, 0)
 
 
 def row_plan(ids, rows, unroll):
@@ -222,13 +233,13 @@
     return once.reshape(-1), again.reshape(-1), jnp.concatenate([clash, sections])
 
 
-def add_rows_call(plan, given, rows, unroll):
+def add_rows_call(plan, given, rows, unroll, parts):
     count, feat = given.shape
     return pl.pallas_call(
         functools.partial(add_rows_body, unroll),
         in_specs=[whole_smem()] * 3 + [whole_vmem()],
-        out_specs=whole_vmem(),
-        out_shape=jax.ShapeDtypeStruct((rows, feat), BF),
+        out_specs=[whole_vmem()] * parts,
+        out_shape=[jax.ShapeDtypeStruct((rows // parts, feat), BF)] * parts,
         scratch_shapes=[pltpu.VMEM((2 * (rows + unroll), LANES), F32)] * 2
         + [pltpu.VMEM((2 * count, LANES), F32)],
         compiler_params=params(48),
@@ -240,17 +251,14 @@
 def spread_body(pairs, *refs):
     for i in range(pairs):
         counts_ref, part_ref, out_ref = refs[2 * i], refs[2 * i + 1], refs[2 * pairs + i]
-        out_ref[...] = left_product(counts_ref[...], part_ref[...]).astype(BF)
+        out_ref[...] = left_product(counts_ref[...].astype(BF), part_ref[...]).astype(BF)
 
 
 def spread_call(counts, parts, steps):
     n, feat = parts[0].shape
     specs, args = [], []
     for c, p in zip(counts, parts):
-        specs += [
-            pl.BlockSpec((n, c.shape[1] // steps), lambda i: (0, i)),
-            pl.BlockSpec(p.shape, lambda i: (0, 0)),
-        ]
+        specs += [pl.BlockSpec((n, c.shape[1] // steps), lambda i: (0, i)), whole_vmem()]
         args += [c, p]
     return pl.pallas_call(
         functools.partial(spread_body, len(counts)),
@@ -258,40 +266,70 @@
         in_specs=specs,
         out_specs=[pl.BlockSpec((c.shape[1] // steps, feat), lambda i: (i, 0)) for c in counts],
         out_shape=[jax.ShapeDtypeStruct((c.shape[1], feat), BF) for c in counts],
-        compiler_params=params(48),
+        compiler_params=params(60),
         name="spread",
     )(*args)
 
 
 def widen_body(blocked, *refs):
-    given, outs = refs[: blocked + 4], refs[blocked + 4 :]
+    given, outs = refs[: blocked + 2], refs[blocked + 2 :]
     for x_ref, out_ref in zip(given[:blocked], outs[:blocked]):
         out_ref[...] = x_ref[...].astype(F32)
-    own_ref, other_ref, first_ref, last_ref = given[blocked:]
-    tail_ref, first_out_ref, last_out_ref, small_ref = outs[blocked:]
-    tail_ref[...] = own_ref[...].astype(F32) + other_ref[...].astype(F32)
+    first_ref, last_ref = given[blocked:]
+    first_out_ref, last_out_ref, loss_ref, *bias_refs = outs[blocked:]
 
     @pl.when(pl.program_id(0) == 0)
     def _():
-        rows = last_out_ref.shape[0]
+        rows, feat = last_out_ref.shape
         first_out_ref[...] = first_ref[...].astype(F32)
         last_out_ref[...] = last_ref[:rows, :].astype(F32)
-        small_ref[...] = last_ref[rows:, :].astype(F32)
-
-
-def widen_call(arrays, own, other, first, last, last_rows, steps):
+        small = last_ref[rows:, :].astype(F32)
+        start = loss_ref.shape[0]
+        loss_ref[...] = small[:start]
+        for ref in bias_refs:
+            for i in range(ref.shape[1] // feat):
+                ref[:, i * feat : (i + 1) * feat] = small[start : start + 1]
+                start += 1
+
+
+def widen_call(arrays, first, last, last_rows, loss_rows, widths, steps):
+    feat = last.shape[1]
     spec = lambda a: pl.BlockSpec((a.shape[0] // steps, a.shape[1]), lambda i: (i, 0))
-    shapes = [a.shape for a in (*arrays, own, first)]
-    shapes += [(last_rows, last.shape[1]), (last.shape[0] - last_rows, last.shape[1])]
+    shapes = [a.shape for a in (*arrays, first)] + [(last_rows, feat), (loss_rows, feat)]
+    shapes += [(1, w) for w in widths]
     return pl.pallas_call(
         functools.partial(widen_body, len(arrays)),
         grid=(steps,),
-        in_specs=[spec(a) for a in (*arrays, own, other)] + [whole_vmem()] * 2,
-        out_specs=[spec(a) for a in (*arrays, own)] + [whole_vmem()] * 3,
+        in_specs=[spec(a) for a in arrays] + [whole_vmem()] * 2,
+        out_specs=[spec(a) for a in arrays] + [whole_vmem()] * (len(shapes) - len(arrays)),
         out_shape=[jax.ShapeDtypeStruct(s, F32) for s in shapes],
-        compiler_params=params(48),
+        compiler_params=params(60),
         name="widen",
-    )(*arrays, own, other, first, last)
+    )(*arrays, first, last)
+
+
+def add_parts_body(*refs):
+    count = len(refs) // 2
+    for k in range(count):
+
+        @pl.when(pl.program_id(0) == k)
+        def _(k=k):
+            refs[-1][...] = refs[k][...].astype(F32) + refs[count + k][...].astype(F32)
+
+
+def add_pair_call(own, others):
+    rows, feat = own[0].shape
+    spec = pl.BlockSpec((rows, feat), lambda i: (0, 0))
+    return pl.pallas_call(
+        add_parts_body,
+        grid=(len(own),),
+        in_specs=[spec] * (2 * len(own)),
+        out_specs=pl.BlockSpec((rows, feat), lambda i: (i, 0)),
+        out_shape=jax.ShapeDtypeStruct((rows * len(own), feat), F32),
+        compiler_params=params(60),
+        cost_estimate=pl.CostEstimate(flops=0, bytes_accessed=0, transcendentals=0),
+        name="add_parts",
+    )(*own, *others)
 
 
 def softmax_body(
@@ -372,7 +410,7 @@
         grad_ref[...] = grad_sum[...].astype(BF)
 
 
-def softmax_call(mask, table, user, labels, block=512, chunk=2048):
+def softmax_call(mask, table, table_t, user, labels, block=512, chunk=2048):
     n, feat = user.shape
     rows = table.shape[0]
     across = lambda h: pl.BlockSpec((h, block), lambda i: (0, i))
@@ -396,7 +434,7 @@
         scratch_shapes=[pltpu.VMEM((rows, block), F32), pltpu.VMEM((rows, feat), F32)],
         compiler_params=params(46),
         name="sampled_softmax",
-    )(mask, table, table.T, user, user.T, labels.reshape(1, n))
+    )(mask, table, table_t, user, user.T, labels.reshape(1, n))
 
 
 def sampled_mask(negatives, rows):
@@ -468,6 +506,7 @@
         looked.reshape(owners, per_owner, feat), "wide", split_axis=0, concat_axis=0, tiled=True
     ).reshape(slots, feat)
 
+    asked, negatives, looked = lax.optimization_barrier((asked, negatives, looked))
     ids = jnp.concatenate(
         [
             in_range_ids(hist_ids, hist_len, 0),
@@ -475,15 +514,18 @@
         ],
         axis=1,
     )
+    out_table_t = out_table.T
     mask = sampled_mask(negatives, out_table.shape[0])
     unroll = 16
     plan = row_plan(asked, shard_rows, unroll)
-    ids, mask, plan, looked = lax.optimization_barrier((ids, mask, plan, looked))
+    ids, out_table_t, mask, plan, looked = lax.optimization_barrier(
+        (ids, out_table_t, mask, plan, looked)
+    )
     hot_counts, slot_counts, word_counts, hot_sum, word_sum = counts_call(
         ids, hot_table, word_table, slots
     )
 
-    hist_mean = (hot_sum + jnp.dot(slot_counts, returned, preferred_element_type=F32)) / hist_float
+    hist_mean = (hot_sum + jnp.dot(slot_counts.astype(BF), returned, preferred_element_type=F32)) / hist_float
     search_mean = word_sum / search_float
     inputs = jnp.concatenate([hist_mean, search_mean, dense_feats.astype(F32)], axis=1).astype(BF)
     pre_first = jnp.dot(inputs, w_first, preferred_element_type=F32) + b_first.astype(F32)
@@ -494,7 +536,7 @@
         BF
     )
 
-    d_user_t, out_grad, per_example = softmax_call(mask, out_table, user, labels)
+    d_user_t, out_grad, per_example = softmax_call(mask, out_table, out_table_t, user, labels)
     d_user = d_user_t.T
     d_pre_second = gelu_back(pre_second, right_product(d_user, w_third)).astype(BF)
     d_pre_first = gelu_back(pre_first, right_product(d_pre_second, w_second)).astype(BF)
@@ -530,18 +572,20 @@
     owed = lax.all_to_all(
         slot_grad.reshape(owners, per_owner, feat), "wide", split_axis=0, concat_axis=0, tiled=True
     ).reshape(slots, feat)
-    own = add_rows_call(plan, owed, shard_rows, unroll)
-    other = lax.ppermute(own, "group", [(0, 1), (1, 0)])
-    hot_all, word_all, out_all, w2_all, tail_grad, w1_all, w3_all, small_all = widen_call(
-        (summed[0], summed[1], summed[2], summed[4]), own, other, summed[3], summed[5], w3_rows, 4
-    )
-    small_sums = []
-    start = 0
-    for x in small:
-        small_sums.append(small_all[start : start + x.size // feat].reshape(-1))
-        start += x.size // feat
-    loss_all, b1_all, b2_all, b3_all = small_sums
-    loss_value = jnp.sum(loss_all) / examples_all
+    own = add_rows_call(plan, owed, shard_rows, unroll, 4)
+    others = [lax.ppermute(x, "group", [(0, 1), (1, 0)]) for x in own]
+    tail_grad = add_pair_call(own, others)
+    summed, tail_grad = lax.optimization_barrier((summed, tail_grad))
+    hot_all, word_all, out_all, w2_all, w1_all, w3_all, losses, b1_all, b2_all, b3_all = widen_call(
+        (summed[0], summed[1], summed[2], summed[4]),
+        summed[3],
+        summed[5],
+        w3_rows,
+        examples_dev // feat,
+        (b_first.shape[0], b_second.shape[0], b_third.shape[0]),
+        4,
+    )
+    loss_value = jnp.sum(losses) / examples_all
     return (
         loss_value,
         hot_all,
@@ -549,11 +593,11 @@
         word_all,
         out_all,
         w1_all,
-        b1_all,
+        b1_all[0],
         w2_all,
-        b2_all,
+        b2_all[0],
         w3_all,
-        b3_all,
+        b3_all[0],
     )
 
 

time: 439 us -> 409 us (0.932)
  blocking collectives: 0 us -> 86.4 us
  waiting for transfers between devices: 185 us -> 106 us
  starting transfers between devices: 34.1 us -> 9.85 us
  local copies, waits for them, and re-layouts: 23.8 us -> 13.7 us
    all_to_all x0 -> x2, blocking collectives: none -> 86.4 us  [the longest x1 66 us: local(): lax.all_to_all(slot_grad.reshape(owners, per_owner, feat), 'wide', split_...]
    all_to_all x2 -> x0, waiting for transfers between devices: 61.4 us -> none  [the longest x1 53.3 us: local(): lax.all_to_all(slot_grad.reshape(owners, per_owner, feat), 'wide', split_...]
    psum x1, waiting for transfers between devices: 122 us -> 97.7 us  [local(): summed = lax.psum(packed, ('group', 'wide'))]
    all_to_all x2 -> x0, starting transfers between devices: 21.3 us -> none  [the longest x1 12.1 us: local(): lax.all_to_all(requests, 'wide', split_axis=0, concat_axis=0, tiled=True)]
    unnamed x69 -> x68, local copies, waits for them, and re-layouts: 19 us -> 10.1 us
    pallas_call x1 -> x2, Pallas kernels: 13.9 us -> 22.2 us  [the longest x1 15.1 us: gather_call(): pl.pallas_call(functools.partial(gather_body, unroll), grid=(steps,), in_...]
    ppermute x1 -> x4, waiting for transfers between devices: 0.01 us -> 6.18 us  [local(): others = [lax.ppermute(x, 'group', [(0, 1), (1, 0)]) for x in own]]
  transfers between devices with their start and end apart: 5 -> 6, of which waited for: 4 -> 5; matrix products, arithmetic and copies ran while one was open for 3% -> 4% of each run, Pallas kernels for 13% -> 17%
where the time goes in v2:
time: 409 us; the launch traced here: 408 us
  Pallas kernels  136 us (33%)
  waiting for transfers between devices  106 us (26%)
  blocking collectives  86.4 us (21%)
  matrix products  31.7 us (8%)
  between operations  16.4 us (4%)
  local copies, waits for them, and re-layouts  13.7 us (3%)
  starting transfers between devices  9.85 us (2%)
  other arithmetic  8.84 us (2%)
    psum x1, waiting for transfers between devices, local(): summed = lax.psum(packed, ('group', 'wide'))  97.7 us
    all_to_all x1, blocking collectives, local(): lax.all_to_all(slot_grad.reshape(owners, per_owner, feat), 'wide', split_...  66 us
    pallas_call x1, Pallas kernels, counts_call(): pl.pallas_call(functools.partial(counts_body, cuts), grid=(n // block,),...  34.5 us
    pallas_call x1, Pallas kernels, softmax_call(): pl.pallas_call(functools.partial(softmax_body, 1.0 / n, chunk), grid=(n /...  31.4 us
    all_to_all x1, blocking collectives, local(): lax.all_to_all(requests, 'wide', split_axis=0, concat_axis=0, tiled=True)  20.4 us
    pallas_call x1, Pallas kernels, add_rows_call(): pl.pallas_call(functools.partial(add_rows_body, unroll), in_specs=[whole_...  18 us
    pallas_call x2, Pallas kernels, spread_call(): pl.pallas_call(functools.partial(spread_body, len(counts)), grid=(steps,)...  17.6 us
    pallas_call x1, Pallas kernels, gather_call(): pl.pallas_call(functools.partial(gather_body, unroll), grid=(steps,), in_...  15.1 us
  transfers between devices with their start and end apart: 6, of which 5 were waited for; matrix products, arithmetic and copies ran while one was open for 4% of the time, Pallas kernels for 17%

profile of v2, /device:TPU:1, one launch (start us, length us, event | category | flops | bytes accessed | tf_op | source)
XLA Modules:
  0.0 408.2 jit_solution(9811516793844428390)
XLA Ops:
  7.2 20.4 %all_to_all.19 = s32[64,1,128]{2,1,0:T(1,128)S(1)} all-to-all(s32[64,1,128]{2,1,0:T(1,128)} %bitcast.39), channel_id=1, replica_groups=mesh['group'=2,'wide'=64] {'wide'}, dimensions={0} | all-to-all | bytes 65536 | tf_op jit(solution)/shard_map/all_to_all | solution.py:502
  28.2 15.1 %gather_rows.1 = bf16[8192,256]{1,0:T(8,128)(2,1)} custom-call(s32[8192]{0:T(1024)} %broadcast_maximum_fusion.ids_ref, bf16[8192,256]{1,0:T(8,128)(2,1)} %table_ref.2), custom_call_target="tpu_custom_call" | custom-call | tf_op jit(solution)/shard_map/gather_rows/pallas_call | solution.py:136
  43.4 5.8 %all-to-all-start.1 = ((bf16[64,128,256]{2,1,0:T(8,128)(2,1)}), bf16[64,128,256]{2,1,0:T(8,128)(2,1)}, u32[]{:S(2)}, u32[]{:S(2)}) async-start(bf16[64,128,256]{2,1,0:T(8,128)(2,1)} %bitcast.33), calls=%async_computation.1 | async-start | bytes 8388608 | tf_op jit(solution)/shard_map/all_to_all | solution.py:505
  50.2 6.6 %copy.52 = bf16[8192,256]{0,1:T(8,128)(2,1)} copy(bf16[8192,256]{1,0:T(8,128)(2,1)} %table_ref.3) | data formatting | bytes 8388608 | tf_op args[3]
  59.8 2.6 broadcast_in_dim.18.mask_ref
  62.4 34.5 %counts.1 = (s8[1024,4096]{1,0:T(32,128)(4,1)}, s8[1024,8192]{1,0:T(32,128)(4,1)}, s8[1024,4096]{1,0:T(32,128)(4,1)}, f32[1024,256]{1,0:T(8,128)}, f32[1024,256]{1,0:T(8,128)}) custom-call(s32[1024,128]{1,0:T(8,128)} %select_add_fusion.ids_ref, bf16[4096,256]{1,0:T(8,128)(2,1)} %hot_ref.1, bf16[4096,256]{1,0:T(8,128)(2,1)} %word_ref.1), custom_call_target="tpu_custom_call" | custom-call | tf_op jit(solution)/shard_map/counts/pallas_call | solution.py:85
  100.2 9.5 %fusion.24 = bf16[1024,256]{1,0:T(8,128)(2,1)S(1)} fusion(f32[1024,256]{1,0:T(8,128)} %get-tuple-element.63, bf16[8192,256]{1,0:T(8,128)(2,1)} %bitcast.5, s8[1024,8192]{1,0:T(32,128)(4,1)} %get-tuple-element.64.refs_0_, f32[1024]{0:T(1024)S(1)} %convert_element_type.79), kind=kOutput, calls=%fused_computation.32 | convolution fusion | flops 4304142336 | bytes 14159872 | tf_op jit(solution)/shard_map/dot_general | solution.py:528
  109.7 4.2 %multiply_convert_fusion = (bf16[1024,1024]{1,0:T(8,128)(2,1)S(1)}, f32[1024,1024]{1,0:T(8,128)}) fusion(f32[1024]{0:T(1024)S(1)} %convert_element_type.81, bf16[600,1024]{1,0:T(8,128)(2,1)S(1)} %copy-done.19, bf16[1024,88]{1,0:T(8,128)(2,1)S(1)} %copy.58, bf16[1024,256]{1,0:T(8,128)(2,1)S(1)} %divide_convert_fusion, bf16[1024,256]{1,0:T(8,128)(2,1)S(1)} %fusion.24), kind=kOutput, calls=%fused_computation.11 | convolution fusion | flops 1272463360 | bytes 8753152 | tf_op jit(solution)/shard_map/dot_general | solution.py:531
  113.9 3.0 multiply_convert_fusion.1
  118.6 31.4 %sampled_softmax.1 = (bf16[256,1024]{1,0:T(8,128)(2,1)S(1)}, bf16[8192,256]{1,0:T(8,128)(2,1)S(1)}, f32[1,1024]{1,0:T(1,128)S(1)}) custom-call(f32[8192,128]{1,0:T(8,128)} %broadcast_in_dim.18.mask_ref, bf16[8192,256]{1,0:T(8,128)(2,1)} %table_ref.3, bf16[256,8192]{1,0:T(8,128)(2,1)} %bitcast.34, bf16[1024,256]{1,0:T(8,128)(2,1)S(1)} %copy.60.user_ref, ...), custom_call_target="tpu_custom_call" | custom-call | tf_op jit(solution)/shard_map/sampled_softmax/pallas_call | solution.py:417
  153.1 2.3 convolution_convert_fusion.1
  155.4 4.3 %fusion.52 = (bf16[1024]{0:T(1024)(128)(2,1)S(1)}, bf16[1024,1024]{1,0:T(8,128)(2,1)S(1)}) fusion(f32[1024,1024]{1,0:T(8,128)S(1)} %copy-done.31, f32[1024]{0:T(1024)S(1)} %convert_element_type.81, bf16[1024,512]{1,0:T(8,128)(2,1)S(1)} %get-tuple-element.120, bf16[1024,512]{1,0:T(8,128)(2,1)S(1)} %copy-done), kind=kOutput, calls=%fused_computation.85 | convolution fusion | flops 1096809472 | bytes 8394752 | tf_op jit(solution)/shard_map/dot_general | solution.py:456
  159.7 2.5 convolution_convert_fusion
  162.2 2.6 fusion.33
  165.0 2.9 fusion.31
  168.6 8.8 %spread.2 = (bf16[4096,256]{1,0:T(8,128)(2,1)}, bf16[4096,256]{1,0:T(8,128)(2,1)}) custom-call(s8[1024,4096]{1,0:T(32,128)(4,1)} %get-tuple-element.60.refs_0_, bf16[1024,256]{1,0:T(8,128)(2,1)} %get-tuple-element.81.refs_1_, s8[1024,4096]{1,0:T(32,128)(4,1)} %get-tuple-element.67.refs_2_, bf16[1024,256]{1,0:T(8,128)(2,1)} %get-tuple-element.109.refs_3_), custom_call_target="tpu_custom_call" | custom-call | tf_op jit(solution)/shard_map/spread/pallas_call | solution.py:263
  177.5 8.7 %spread.3 = bf16[8192,256]{1,0:T(8,128)(2,1)} custom-call(s8[1024,8192]{1,0:T(32,128)(4,1)} %get-tuple-element.64.refs_0_, bf16[1024,256]{1,0:T(8,128)(2,1)} %get-tuple-element.81.refs_1_), custom_call_target="tpu_custom_call" | custom-call | tf_op jit(solution)/shard_map/spread/pallas_call | solution.py:263
  186.2 66.0 %all_to_all.20 = bf16[64,128,256]{2,1,0:T(8,128)(2,1)} all-to-all(bf16[64,128,256]{2,1,0:T(8,128)(2,1)} %bitcast.32), channel_id=1, replica_groups=mesh['group'=2,'wide'=64] {'wide'}, dimensions={0} | all-to-all | bytes 8388608 | tf_op jit(solution)/shard_map/all_to_all | solution.py:572
  252.2 18.0 %add_rows.1 = (bf16[2048,256]{1,0:T(8,128)(2,1)S(1)}, bf16[2048,256]{1,0:T(8,128)(2,1)S(1)}, bf16[2048,256]{1,0:T(8,128)(2,1)S(1)}, bf16[2048,256]{1,0:T(8,128)(2,1)S(1)}) custom-call(s32[8192]{0:T(1024)S(1)} %get-tuple-element.78.ids_ref, s32[8192]{0:T(1024)S(1)} %get-tuple-element.79.again_ref, s32[544]{0:T(1024)S(1)} %pad_add_fusion.clash_ref, ...), custom_call_target="tpu_custom_call" | custom-call | tf_op jit(solution)/shard_map/add_rows/pallas_call | solution.py:238
  270.2 3.4 collective-permute-start
  275.9 3.0 collective-permute-done.1.refs_5_
  281.4 7.2 %add_parts.1 = f32[8192,256]{1,0:T(8,128)} custom-call(bf16[2048,256]{1,0:T(8,128)(2,1)} %copy-done.3, bf16[2048,256]{1,0:T(8,128)(2,1)} %copy-done.4, bf16[2048,256]{1,0:T(8,128)(2,1)} %copy-done.5, bf16[2048,256]{1,0:T(8,128)(2,1)} %copy-done.6, bf16[2048,256]{1,0:T(8,128)(2,1)} %copy-done.8, bf16[2048,256]{1,0:T(8,128)(2,1)} %copy-done.9, ...), custom_call_target="tpu_custom_call" | custom-call | tf_op jit(solution)/shard_map/add_parts/pallas_call | solution.py:323
  288.6 97.7 %all-reduce.6.cloned.1.call-done = (bf16[4096,256]{1,0:T(8,128)(2,1)}, bf16[4096,256]{1,0:T(8,128)(2,1)}, bf16[8192,256]{1,0:T(8,128)(2,1)}, bf16[600,1024]{1,0:...) async-done(((bf16[4096,256]{1,0:T(8,128)(2,1)}, bf16[4096,256]{1,0:T(8,128)(2,1)}, bf16[8192,256]{1,0:T(8,128)(2,1)}, bf16[600,1024]{1,0:T(8,128)(2,1)}, ...) | async-done | bytes 10936336 | tf_op jit(solution)/shard_map/psum | solution.py:569
  386.3 12.0 %widen.1 = (f32[4096,256]{1,0:T(8,128)}, f32[4096,256]{1,0:T(8,128)}, f32[8192,256]{1,0:T(8,128)}, f32[1024,512]{1,0:T(8,128)}, f32[600,1024]{1,0:T(8,128)}, /*i...) custom-call(bf16[4096,256]{1,0:T(8,128)(2,1)} %get-tuple-element.86.refs_0_,, ...), custom_call_target="tpu_custom_call" | custom-call | tf_op jit(solution)/shard_map/widen/pallas_call | solution.py:300
  (115 shorter events, 19.6 us)
Async XLA Ops:
  7.2 106.7 %copy-start = (bf16[1024,512]{1,0:T(8,128)(2,1)S(1)}, bf16[1024,512]{1,0:T(8,128)(2,1)}, u32[]{:S(2)}) copy-start(bf16[1024,512]{1,0:T(8,128)(2,1)} %param.24) | copy-start | bytes 3145732
  43.3 5.9 %copy-start.23 = (bf16[256]{0:T(256)(128)(2,1)S(1)}, bf16[256]{0:T(256)(128)(2,1)}, u32[]{:S(2)}) copy-start(bf16[256]{0:T(256)(128)(2,1)} %param.27) | copy-start | bytes 1540
  43.3 5.9 %copy-start.18 = (bf16[512]{0:T(512)(128)(2,1)S(1)}, bf16[512]{0:T(512)(128)(2,1)}, u32[]{:S(2)}) copy-start(bf16[512]{0:T(512)(128)(2,1)} %param.25) | copy-start | bytes 3076
  43.3 6.0 %copy-start.17 = (bf16[1024]{0:T(1024)(128)(2,1)S(1)}, bf16[1024]{0:T(1024)(128)(2,1)}, u32[]{:S(2)}) copy-start(bf16[1024]{0:T(1024)(128)(2,1)} %param.23) | copy-start | bytes 6148
  43.3 6.0 %copy-start.16 = (s32[1024]{0:T(1024)S(1)}, s32[1024]{0:T(1024)}, u32[]{:S(2)}) copy-start(s32[1024]{0:T(1024)} %param.30) | copy-start | bytes 12292
  43.3 6.0 %copy-start.15 = (s32[1024]{0:T(1024)S(1)}, s32[1024]{0:T(1024)}, u32[]{:S(2)}) copy-start(s32[1024]{0:T(1024)} %param.32) | copy-start | bytes 12292
  43.3 6.2 %copy-start.13 = (bf16[1024,88]{0,1:T(8,128)(2,1)S(1)}, bf16[1024,88]{0,1:T(8,128)(2,1)}, u32[]{:S(2)}) copy-start(bf16[1024,88]{0,1:T(8,128)(2,1)} %param.28) | copy-start | bytes 540676
  43.3 6.3 %copy-start.11 = (s32[1024,50]{0,1:T(8,128)S(1)}, s32[1024,50]{0,1:T(8,128)}, u32[]{:S(2)}) copy-start(s32[1024,50]{0,1:T(8,128)} %param.29) | copy-start | bytes 614404
  43.4 6.6 %copy-start.12 = (s32[1024,50]{0,1:T(8,128)S(1)}, s32[1024,50]{0,1:T(8,128)}, u32[]{:S(2)}) copy-start(s32[1024,50]{0,1:T(8,128)} %param.31) | copy-start | bytes 614404
  43.4 56.8 %all-to-all-start.1 = ((bf16[64,128,256]{2,1,0:T(8,128)(2,1)}), bf16[64,128,256]{2,1,0:T(8,128)(2,1)}, u32[]{:S(2)}, u32[]{:S(2)}) async-start(bf16[64,128,256]{2,1,0:T(8,128)(2,1)} %bitcast.33), calls=%async_computation.1 | async-start | bytes 8388608 | tf_op jit(solution)/shard_map/all_to_all | solution.py:505
  49.2 337.1 %all-reduce.6.cloned.1.call-start = ((), (), s32[]{:S(2)}) async-start(), calls=%async_computation.3 | async-start | bytes 21872640 | tf_op jit(solution)/shard_map/psum | solution.py:569
  100.2 9.5 %copy-start.19 = (bf16[600,1024]{1,0:T(8,128)(2,1)S(1)}, bf16[600,1024]{1,0:T(8,128)(2,1)}, u32[]{:S(2)}) copy-start(bf16[600,1024]{1,0:T(8,128)(2,1)} %param.22) | copy-start | bytes 3686404
  118.6 31.4 %copy-start.25 = (bf16[1024,512]{1,0:T(8,128)(2,1)S(1)}, bf16[1024,512]{1,0:T(8,128)(2,1)}, u32[]{:S(2)}) copy-start(bf16[1024,512]{1,0:T(8,128)(2,1)} %copy-done.24) | copy-start | bytes 3145732
  118.6 31.9 %copy-start.22 = (bf16[512,256]{1,0:T(8,128)(2,1)S(1)}, bf16[512,256]{1,0:T(8,128)(2,1)}, u32[]{:S(2)}) copy-start(bf16[512,256]{1,0:T(8,128)(2,1)} %param.26) | copy-start | bytes 786436
  118.6 31.9 %copy-start.30 = (f32[1024,512]{1,0:T(8,128)S(1)}, f32[1024,512]{1,0:T(8,128)}, u32[]{:S(2)}) copy-start(f32[1024,512]{1,0:T(8,128)} %get-tuple-element.118) | copy-start | bytes 6291460
  270.1 10.2 %copy-start.6 = (bf16[2048,256]{1,0:T(8,128)(2,1)}, bf16[2048,256]{1,0:T(8,128)(2,1)S(1)}, u32[]{:S(2)}) copy-start(bf16[2048,256]{1,0:T(8,128)(2,1)S(1)} %get-tuple-element.85.refs_3_) | copy-start | bytes 3145732
  270.1 11.2 %copy-start.3 = (bf16[2048,256]{1,0:T(8,128)(2,1)}, bf16[2048,256]{1,0:T(8,128)(2,1)S(1)}, u32[]{:S(2)}) copy-start(bf16[2048,256]{1,0:T(8,128)(2,1)S(1)} %get-tuple-element.82.refs_0_) | copy-start | bytes 3145732
  270.2 11.2 %copy-start.4 = (bf16[2048,256]{1,0:T(8,128)(2,1)}, bf16[2048,256]{1,0:T(8,128)(2,1)S(1)}, u32[]{:S(2)}) copy-start(bf16[2048,256]{1,0:T(8,128)(2,1)S(1)} %get-tuple-element.83.refs_1_) | copy-start | bytes 3145732
  270.2 11.2 %copy-start.5 = (bf16[2048,256]{1,0:T(8,128)(2,1)}, bf16[2048,256]{1,0:T(8,128)(2,1)S(1)}, u32[]{:S(2)}) copy-start(bf16[2048,256]{1,0:T(8,128)(2,1)S(1)} %get-tuple-element.84.refs_2_) | copy-start | bytes 3145732
  270.2 5.7 %collective-permute-start = (bf16[2048,256]{1,0:T(8,128)(2,1)S(1)}, bf16[2048,256]{1,0:T(8,128)(2,1)S(1)}, u32[]{:S(2)}, u32[]{:S(2)}) collective-permute-start(bf16[2048,256]{1,0:T(8,128)(2,1)S(1)} %get-tuple-element.82.refs_0_), channel_id=1, source_target_pairs={{0,64},{64,0},{1,65},{65,1},{2,66},{66,2},{3,67},{67,3},{4,68},{68... | collective-permute-start | bytes 3145736 | tf_op jit(solution)/shard_map/ppermute | solution.py:576
  273.6 5.3 %collective-permute-start.1 = (bf16[2048,256]{1,0:T(8,128)(2,1)S(1)}, bf16[2048,256]{1,0:T(8,128)(2,1)S(1)}, u32[]{:S(2)}, u32[]{:S(2)}) collective-permute-start(bf16[2048,256]{1,0:T(8,128)(2,1)S(1)} %get-tuple-element.83.refs_1_), channel_id=1, source_target_pairs={{0,64},{64,0},{1,65},{65,1},{2,66},{66,2},{3,67},{67,3},{4,68},{68... | collective-permute-start | bytes 3145736 | tf_op jit(solution)/shard_map/ppermute | solution.py:576
  273.7 6.7 %collective-permute-start.2 = (bf16[2048,256]{1,0:T(8,128)(2,1)S(1)}, bf16[2048,256]{1,0:T(8,128)(2,1)S(1)}, u32[]{:S(2)}, u32[]{:S(2)}) collective-permute-start(bf16[2048,256]{1,0:T(8,128)(2,1)S(1)} %get-tuple-element.84.refs_2_), channel_id=1, source_target_pairs={{0,64},{64,0},{1,65},{65,1},{2,66},{66,2},{3,67},{67,3},{4,68},{68... | collective-permute-start | bytes 3145736 | tf_op jit(solution)/shard_map/ppermute | solution.py:576
  274.1 7.3 %collective-permute-start.3 = (bf16[2048,256]{1,0:T(8,128)(2,1)S(1)}, bf16[2048,256]{1,0:T(8,128)(2,1)}, u32[]{:S(2)}, u32[]{:S(2)}) collective-permute-start(bf16[2048,256]{1,0:T(8,128)(2,1)S(1)} %get-tuple-element.85.refs_3_), channel_id=1, source_target_pairs={{0,64},{64,0},{1,65},{65,1},{2,66},{66,2},{3,67},{67,3},{4,68},{68... | collective-permute-start | bytes 3145736 | tf_op jit(solution)/shard_map/ppermute | solution.py:576
  386.3 14.0 %copy-start.1 = (bf16[1024,512]{1,0:T(8,128)(2,1)S(1)}, bf16[1024,512]{1,0:T(8,128)(2,1)}, u32[]{:S(2)}) copy-start(bf16[1024,512]{1,0:T(8,128)(2,1)} %param.24) | copy-start | bytes 3145732
  (14 other events, 37.3 us)
Sparse Core Ops, SparseCore 0:
  177.6 208.6 all-reduce.5

commit v3 on v2

--- a/solution.py
+++ b/solution.py
@@ -96,52 +96,75 @@
     )(ids, hot, word)
 
 
-def gather_body(unroll, ids_ref, table_ref, out_ref, wide, picked):
-    rows = table_ref.shape[0]
-    count = out_ref.shape[0]
-    step = pl.program_id(0)
-
-    @pl.when(step == 0)
-    def _():
-        def widen(i, carry):
-            t = table_ref[pl.ds(pl.multiple_of(i * 128, 128), 128), :].astype(F32)
-            wide[pl.ds(i * 256, 128, stride=2), :] = t[:, :LANES]
-            wide[pl.ds(i * 256 + 1, 128, stride=2), :] = t[:, LANES:]
+def gather_body(parts, ids_ref, table_hbm, out_hbm, table, wide, picked, out, sems):
+    rows = table.shape[0]
+    owners, each = ids_ref.shape
+    here = lambda i, size: pl.ds(pl.multiple_of(i * size, size), size)
+    given = rows // parts
+    taken = owners // parts
+    inward = [
+        pltpu.make_async_copy(
+            table_hbm.at[here(p, given)], table.at[here(p, given)], sems.at[0, p]
+        )
+        for p in range(parts)
+    ]
+    outward = [
+        pltpu.make_async_copy(
+            out.at[here(p, taken * each)], out_hbm.at[here(p, taken * each)], sems.at[1, p]
+        )
+        for p in range(parts)
+    ]
+    for copy in inward:
+        copy.start()
+    wide[:8, :] = jnp.zeros((8, LANES), F32)
+    for p in range(parts):
+        inward[p].wait()
+
+        def widen(i, carry, p=p):
+            i = i + p * (given // 128)
+            t = table[here(i, 128), :].astype(F32)
+            wide[pl.ds(8 + i * 256, 128, stride=2), :] = t[:, :LANES]
+            wide[pl.ds(9 + i * 256, 128, stride=2), :] = t[:, LANES:]
             return carry
 
-        lax.fori_loop(0, rows // 128, widen, 0)
-
-    def pick(i, carry):
-        for k in range(unroll):
-            at = i * unroll + k
-            picked[pl.ds(at * 2, 2), :] = wide[pl.ds(ids_ref[step * count + at] * 2, 2), :]
-        return carry
-
-    lax.fori_loop(0, count // unroll, pick, 0)
-
-    def join(i, carry):
-        left = picked[pl.ds(i * 256, 128, stride=2), :]
-        right = picked[pl.ds(i * 256 + 1, 128, stride=2), :]
-        out_ref[pl.ds(pl.multiple_of(i * 128, 128), 128), :] = jnp.concatenate(
-            [left, right], axis=1
-        ).astype(BF)
-        return carry
-
-    lax.fori_loop(0, count // 128, join, 0)
-
-
-def gather_call(ids, table, steps=1, unroll=64):
+        lax.fori_loop(0, given // 128, widen, 0)
+
+    for p in range(parts):
+
+        def pick(owner, carry):
+            for k in range(each):
+                at = owner * each + k
+                picked[pl.ds(at * 2, 2), :] = wide[pl.ds(ids_ref[owner, k] * 2 + 8, 2), :]
+            return carry
+
+        lax.fori_loop(p * taken, (p + 1) * taken, pick, 0)
+
+        def join(i, carry):
+            left = picked[pl.ds(i * 256, 128, stride=2), :]
+            right = picked[pl.ds(i * 256 + 1, 128, stride=2), :]
+            out[here(i, 128), :] = jnp.concatenate([left, right], axis=1).astype(BF)
+            return carry
+
+        lax.fori_loop(p * taken * each // 128, (p + 1) * taken * each // 128, join, 0)
+        outward[p].start()
+    for copy in outward:
+        copy.wait()
+
+
+def gather_call(ids, table, parts=8):
     rows, feat = table.shape
-    count = ids.shape[0]
+    count = ids.size
     return pl.pallas_call(
-        functools.partial(gather_body, unroll),
-        grid=(steps,),
-        in_specs=[whole_smem(), whole_vmem()],
-        out_specs=pl.BlockSpec((count // steps, feat), lambda i: (i, 0)),
+        functools.partial(gather_body, parts),
+        in_specs=[whole_smem(), pl.BlockSpec(memory_space=pl.ANY)],
+        out_specs=pl.BlockSpec(memory_space=pl.ANY),
         out_shape=jax.ShapeDtypeStruct((count, feat), BF),
         scratch_shapes=[
-            pltpu.VMEM((2 * rows, LANES), F32),
-            pltpu.VMEM((2 * count // steps, LANES), F32),
+            pltpu.VMEM((rows, feat), BF),
+            pltpu.VMEM((2 * rows + 8, LANES), F32),
+            pltpu.VMEM((2 * count, LANES), F32),
+            pltpu.VMEM((count, feat), BF),
+            pltpu.SemaphoreType.DMA((2, parts)),
         ],
         compiler_params=params(60),
         name="gather_rows",
@@ -248,24 +271,34 @@
     )(*plan, given)
 
 
-def spread_body(pairs, *refs):
+def spread_body(pairs, firsts, d_inputs_ref, *refs):
+    part_refs = refs[3 * pairs :]
+    feat = part_refs[0].shape[1]
+
+    @pl.when(pl.program_id(0) == 0)
+    def _():
+        for i, first in enumerate(firsts):
+            d_mean = d_inputs_ref[:, first : first + feat]
+            part_refs[i][...] = (d_mean / refs[2 * i + 1][...]).astype(BF)
+
     for i in range(pairs):
-        counts_ref, part_ref, out_ref = refs[2 * i], refs[2 * i + 1], refs[2 * pairs + i]
-        out_ref[...] = left_product(counts_ref[...].astype(BF), part_ref[...]).astype(BF)
-
-
-def spread_call(counts, parts, steps):
-    n, feat = parts[0].shape
-    specs, args = [], []
-    for c, p in zip(counts, parts):
+        counts_ref, out_ref = refs[2 * i], refs[2 * pairs + i]
+        out_ref[...] = left_product(counts_ref[...].astype(BF), part_refs[i][...]).astype(BF)
+
+
+def spread_call(counts, lengths, d_inputs, firsts, feat, steps):
+    n = d_inputs.shape[0]
+    specs, args = [whole_vmem()], [d_inputs]
+    for c, x in zip(counts, lengths):
         specs += [pl.BlockSpec((n, c.shape[1] // steps), lambda i: (0, i)), whole_vmem()]
-        args += [c, p]
+        args += [c, x]
     return pl.pallas_call(
-        functools.partial(spread_body, len(counts)),
+        functools.partial(spread_body, len(counts), firsts),
         grid=(steps,),
         in_specs=specs,
         out_specs=[pl.BlockSpec((c.shape[1] // steps, feat), lambda i: (i, 0)) for c in counts],
         out_shape=[jax.ShapeDtypeStruct((c.shape[1], feat), BF) for c in counts],
+        scratch_shapes=[pltpu.VMEM((n, feat), BF)] * len(counts),
         compiler_params=params(60),
         name="spread",
     )(*args)
@@ -335,10 +368,9 @@
 def softmax_body(
     inv_count,
     chunk,
-    mask_ref,
-    table_ref,
-    table_t_ref,
-    user_ref,
+    mask_hbm,
+    table_hbm,
+    table_t_hbm,
     user_t_ref,
     label_ref,
     d_user_t_ref,
@@ -346,28 +378,49 @@
     loss_ref,
     logits,
     grad_sum,
+    mask_ref,
+    table_ref,
+    table_t_ref,
+    sems,
 ):
     rows, feat = table_ref.shape
-    block = user_ref.shape[0]
+    block = user_t_ref.shape[1]
     chunks = rows // chunk
     step = pl.program_id(0)
+    last = pl.num_programs(0) - 1
+
+    def at(c):
+        return pl.ds(pl.multiple_of(c * chunk, chunk), chunk)
+
+    def fetches(c):
+        return (
+            pltpu.make_async_copy(table_hbm.at[at(c)], table_ref.at[at(c)], sems.at[0, c]),
+            pltpu.make_async_copy(mask_hbm.at[at(c)], mask_ref.at[at(c)], sems.at[1, c]),
+        )
+
+    turned = pltpu.make_async_copy(table_t_hbm, table_t_ref, sems.at[2, 0])
 
     @pl.when(step == 0)
     def _():
-        grad_sum[...] = jnp.zeros(grad_sum.shape, F32)
+        for c in range(chunks):
+            for fetch in fetches(c):
+                fetch.start()
+        turned.start()
 
     label = label_ref[...]
     user_t = user_t_ref[...]
-    user = user_ref[...]
+    user = user_t.astype(F32).T.astype(BF)
     iota = lax.broadcasted_iota(jnp.int32, (chunk, block), 0)
-
-    def at(c):
-        return pl.ds(pl.multiple_of(c * chunk, chunk), chunk)
 
     def fold(v, op):
         return op(v.reshape(chunk // 8, 8, block), axis=0)
 
     def first(c, carry):
+        @pl.when(step == 0)
+        def _():
+            for fetch in fetches(c):
+                fetch.wait()
+
         peak, pos = carry
         s = jnp.dot(table_ref[at(c), :], user_t, preferred_element_type=F32)
         pos = pos + fold(jnp.where(iota == label - c * chunk, s, 0.0), jnp.sum)
@@ -396,45 +449,66 @@
     scale = inv_count / total
     d_pos = (pos_exp / total - 1.0) * inv_count
 
-    def third(c, d_user_t):
-        d = logits[at(c), :] * scale
-        d = jnp.where(iota == label - c * chunk, d + d_pos, d).astype(BF)
-        grad_sum[at(c), :] += jnp.dot(d, user, preferred_element_type=F32)
-        return d_user_t + jnp.dot(table_t_ref[:, at(c)], d, preferred_element_type=F32)
-
-    d_user_t = lax.fori_loop(0, chunks, third, jnp.zeros((feat, block), F32))
-    d_user_t_ref[...] = d_user_t.astype(BF)
-
-    @pl.when(step == pl.num_programs(0) - 1)
+    @pl.when(step == 0)
     def _():
-        grad_ref[...] = grad_sum[...].astype(BF)
+        turned.wait()
+
+    def back(add, store):
+        def third(c, d_user_t):
+            d = logits[at(c), :] * scale
+            d = jnp.where(iota == label - c * chunk, d + d_pos, d).astype(BF)
+            term = jnp.dot(d, user, preferred_element_type=F32)
+            if add:
+                term = grad_sum[at(c), :] + term
+            if store:
+                grad_ref[at(c), :] = term.astype(BF)
+            else:
+                grad_sum[at(c), :] = term
+            return d_user_t + jnp.dot(table_t_ref[:, at(c)], d, preferred_element_type=F32)
+
+        d_user_t = lax.fori_loop(0, chunks, third, jnp.zeros((feat, block), F32))
+        d_user_t_ref[...] = d_user_t.astype(BF)
+
+    @pl.when(step == 0)
+    def _():
+        back(False, False)
+
+    @pl.when((step > 0) & (step < last))
+    def _():
+        back(True, False)
+
+    @pl.when(step == last)
+    def _():
+        back(True, True)
 
 
 def softmax_call(mask, table, table_t, user, labels, block=512, chunk=2048):
     n, feat = user.shape
     rows = table.shape[0]
     across = lambda h: pl.BlockSpec((h, block), lambda i: (0, i))
+    any_place = pl.BlockSpec(memory_space=pl.ANY)
     return pl.pallas_call(
         functools.partial(softmax_body, 1.0 / n, chunk),
         grid=(n // block,),
-        in_specs=[
-            whole_vmem(),
-            whole_vmem(),
-            whole_vmem(),
-            pl.BlockSpec((block, feat), lambda i: (i, 0)),
-            across(feat),
-            across(1),
-        ],
+        in_specs=[any_place] * 3
+        + [across(feat), across(1)],
         out_specs=[across(feat), whole_vmem(), across(1)],
         out_shape=[
             jax.ShapeDtypeStruct((feat, n), BF),
             jax.ShapeDtypeStruct((rows, feat), BF),
             jax.ShapeDtypeStruct((1, n), F32),
         ],
-        scratch_shapes=[pltpu.VMEM((rows, block), F32), pltpu.VMEM((rows, feat), F32)],
-        compiler_params=params(46),
+        scratch_shapes=[
+            pltpu.VMEM((rows, block), F32),
+            pltpu.VMEM((rows, feat), F32),
+            pltpu.VMEM((rows, LANES), F32),
+            pltpu.VMEM((rows, feat), BF),
+            pltpu.VMEM((feat, rows), BF),
+            pltpu.SemaphoreType.DMA((3, rows // chunk)),
+        ],
+        compiler_params=params(58),
         name="sampled_softmax",
-    )(mask, table, table_t, user, user.T, labels.reshape(1, n))
+    )(mask, table, table_t, user.T, labels.reshape(1, n))
 
 
 def sampled_mask(negatives, rows):
@@ -500,8 +574,7 @@
     search_float = search_len[:, None].astype(F32)
 
     asked = lax.all_to_all(requests, "wide", split_axis=0, concat_axis=0, tiled=True)
-    asked = asked.reshape(slots)
-    looked = gather_call(jnp.maximum(asked, 0), tail_table)
+    looked = gather_call(asked, tail_table)
     returned = lax.all_to_all(
         looked.reshape(owners, per_owner, feat), "wide", split_axis=0, concat_axis=0, tiled=True
     ).reshape(slots, feat)
@@ -517,7 +590,7 @@
     out_table_t = out_table.T
     mask = sampled_mask(negatives, out_table.shape[0])
     unroll = 16
-    plan = row_plan(asked, shard_rows, unroll)
+    plan = row_plan(asked.reshape(slots), shard_rows, unroll)
     ids, out_table_t, mask, plan, looked = lax.optimization_barrier(
         (ids, out_table_t, mask, plan, looked)
     )
@@ -541,10 +614,10 @@
     d_pre_second = gelu_back(pre_second, right_product(d_user, w_third)).astype(BF)
     d_pre_first = gelu_back(pre_first, right_product(d_pre_second, w_second)).astype(BF)
     d_inputs = right_product(d_pre_first, w_first[: 2 * feat])
-    hist_part = (d_inputs[:, :feat] / hist_float).astype(BF)
-    word_part = (d_inputs[:, feat:] / search_float).astype(BF)
-
-    hot_grad, word_grad = spread_call((hot_counts, word_counts), (hist_part, word_part), 4)
+
+    hot_grad, word_grad = spread_call(
+        (hot_counts, word_counts), (hist_float, search_float), d_inputs, (0, feat), feat, 4
+    )
     w1_grad = left_product(inputs, d_pre_first).astype(BF)
     w2_grad = left_product(act_first, d_pre_second).astype(BF)
     w3_grad = left_product(act_second, d_user).astype(BF)
@@ -565,10 +638,10 @@
         w2_grad,
         jnp.concatenate([w3_grad, small_rows], axis=0),
     )
-    packed, hist_part = lax.optimization_barrier((packed, hist_part))
+    packed, slot_counts = lax.optimization_barrier((packed, slot_counts))
     summed = lax.psum(packed, ("group", "wide"))
 
-    (slot_grad,) = spread_call((slot_counts,), (hist_part,), 4)
+    (slot_grad,) = spread_call((slot_counts,), (hist_float,), d_inputs, (0,), feat, 4)
     owed = lax.all_to_all(
         slot_grad.reshape(owners, per_owner, feat), "wide", split_axis=0, concat_axis=0, tiled=True
     ).reshape(slots, feat)

time: 409 us -> 411 us (level)
  waiting for transfers between devices: 106 us -> 101 us
    unnamed x68 -> x56, local copies, waits for them, and re-layouts: 10.1 us -> 8.34 us
  transfers between devices with their start and end apart: 6 -> 6, of which waited for: 5 -> 4; matrix products, arithmetic and copies ran while one was open for 4% -> 4% of each run, Pallas kernels for 17% -> 17%
where the time goes in v3:
time: 411 us; the launch traced here: 406 us
  Pallas kernels  135 us (33%)
  waiting for transfers between devices  101 us (25%)
  blocking collectives  88.8 us (22%)
  matrix products  34.6 us (8%)
  between operations  16.8 us (4%)
  local copies, waits for them, and re-layouts  13.8 us (3%)
  starting transfers between devices  11.5 us (3%)
  other arithmetic  5.39 us (1%)
    psum x1, waiting for transfers between devices, local(): summed = lax.psum(packed, ('group', 'wide'))  94.4 us
    all_to_all x1, blocking collectives, local(): lax.all_to_all(slot_grad.reshape(owners, per_owner, feat), 'wide', split_...  68.1 us
    pallas_call x1, Pallas kernels, counts_call(): pl.pallas_call(functools.partial(counts_body, cuts), grid=(n // block,),...  34.5 us
    pallas_call x1, Pallas kernels, softmax_call(): pl.pallas_call(functools.partial(softmax_body, 1.0 / n, chunk), grid=(n /...  29.1 us
    all_to_all x1, blocking collectives, local(): lax.all_to_all(requests, 'wide', split_axis=0, concat_axis=0, tiled=True)  20.7 us
    pallas_call x2, Pallas kernels, spread_call(): pl.pallas_call(functools.partial(spread_body, len(counts), firsts), grid=...  19.5 us
    pallas_call x1, Pallas kernels, add_rows_call(): pl.pallas_call(functools.partial(add_rows_body, unroll), in_specs=[whole_...  18.3 us
    pallas_call x1, Pallas kernels, gather_call(): pl.pallas_call(functools.partial(gather_body, parts), in_specs=[whole_sme...  14.1 us
  transfers between devices with their start and end apart: 6, of which 4 were waited for; matrix products, arithmetic and copies ran while one was open for 4% of the time, Pallas kernels for 17%

profile of v3, /device:TPU:1, one launch (start us, length us, event | category | flops | bytes accessed | tf_op | source)
XLA Modules:
  0.0 406.3 jit_solution(2997316804416500451)
XLA Ops:
  7.2 20.7 %all_to_all.21 = s32[64,1,128]{2,1,0:T(1,128)} all-to-all(s32[64,1,128]{2,1,0:T(1,128)} %bitcast.53), channel_id=1, replica_groups=mesh['group'=2,'wide'=64] {'wide'}, dimensions={0} | all-to-all | bytes 65536 | tf_op jit(solution)/shard_map/all_to_all | solution.py:576
  27.9 14.1 %gather_rows.1 = bf16[8192,256]{1,0:T(8,128)(2,1)} custom-call(s32[64,128]{1,0:T(8,128)} %bitcast.49, bf16[8192,256]{1,0:T(8,128)(2,1)} %table_hbm.2), custom_call_target="tpu_custom_call" | custom-call | tf_op jit(solution)/shard_map/gather_rows/pallas_call | solution.py:157
  42.0 5.8 %all-to-all-start.1 = ((bf16[64,128,256]{2,1,0:T(8,128)(2,1)}), bf16[64,128,256]{2,1,0:T(8,128)(2,1)}, u32[]{:S(2)}, u32[]{:S(2)}) async-start(bf16[64,128,256]{2,1,0:T(8,128)(2,1)} %bitcast.46), calls=%async_computation.1 | async-start | bytes 8388608 | tf_op jit(solution)/shard_map/all_to_all | solution.py:578
  48.6 6.6 %copy.55 = bf16[8192,256]{0,1:T(8,128)(2,1)} copy(bf16[8192,256]{1,0:T(8,128)(2,1)} %table_hbm.3) | data formatting | bytes 8388608 | tf_op args[3]
  60.7 2.6 broadcast_in_dim.18.mask_hbm
  63.3 34.5 %counts.1 = (s8[1024,4096]{1,0:T(32,128)(4,1)}, s8[1024,8192]{1,0:T(32,128)(4,1)}, s8[1024,4096]{1,0:T(32,128)(4,1)}, f32[1024,256]{1,0:T(8,128)}, f32[1024,256]{1,0:T(8,128)}) custom-call(s32[1024,128]{1,0:T(8,128)} %select_add_fusion.ids_ref, bf16[4096,256]{1,0:T(8,128)(2,1)} %hot_ref.1, bf16[4096,256]{1,0:T(8,128)(2,1)} %word_ref.1), custom_call_target="tpu_custom_call" | custom-call | tf_op jit(solution)/shard_map/counts/pallas_call | solution.py:85
  99.3 9.5 %fusion.24 = bf16[1024,256]{1,0:T(8,128)(2,1)S(1)} fusion(f32[1024,256]{1,0:T(8,128)} %get-tuple-element.62, bf16[8192,256]{1,0:T(8,128)(2,1)} %bitcast.6, s8[1024,8192]{1,0:T(32,128)(4,1)} %get-tuple-element.81.refs_0_, f32[1024]{0:T(1024)S(1)} %convert_element_type.77), kind=kOutput, calls=%fused_computation.32 | convolution fusion | flops 4304142336 | bytes 14159872 | tf_op jit(solution)/shard_map/dot_general | solution.py:601
  108.8 4.4 %multiply_convert_fusion = (bf16[1024,1024]{1,0:T(8,128)(2,1)S(1)}, f32[1024,1024]{1,0:T(8,128)}) fusion(f32[1024]{0:T(1024)S(1)} %convert_element_type.79, bf16[600,1024]{1,0:T(8,128)(2,1)S(1)} %copy-done.20, bf16[1024,88]{1,0:T(8,128)(2,1)S(1)} %copy.61, bf16[1024,256]{1,0:T(8,128)(2,1)S(1)} %divide_convert_fusion, bf16[1024,256]{1,0:T(8,128)(2,1)S(1)} %fusion.24), kind=kOutput, calls=%fused_computation.11 | convolution fusion | flops 1272463360 | bytes 8753152 | tf_op jit(solution)/shard_map/dot_general | solution.py:604
  113.2 3.0 multiply_convert_fusion.1
  117.4 29.1 %sampled_softmax.1 = (bf16[256,1024]{1,0:T(8,128)(2,1)}, bf16[8192,256]{1,0:T(8,128)(2,1)}, f32[1,1024]{1,0:T(1,128)}) custom-call(f32[8192,128]{1,0:T(8,128)} %broadcast_in_dim.18.mask_hbm, bf16[8192,256]{1,0:T(8,128)(2,1)} %table_hbm.3, bf16[256,8192]{1,0:T(8,128)(2,1)} %bitcast.45, bf16[256,1024]{1,0:T(8,128)(2,1)} %fusion.28.user_t_ref, s32[1,1024]{1,0:T(1,128)} %bitcast.55), custom_call_target="tpu_custom_call" | custom-call | tf_op jit(solution)/shard_map/sampled_softmax/pallas_call | solution.py:490
  146.5 3.7 fusion.49
  150.3 4.3 %fusion.50 = (bf16[1024]{0:T(1024)(128)(2,1)S(1)}, bf16[1024,1024]{1,0:T(8,128)(2,1)S(1)}) fusion(f32[1024,1024]{1,0:T(8,128)S(1)} %copy-done.25, f32[1024]{0:T(1024)S(1)} %convert_element_type.79, bf16[1024,512]{1,0:T(8,128)(2,1)S(1)} %get-tuple-element.118, bf16[1024,512]{1,0:T(8,128)(2,1)S(1)} %copy-done), kind=kOutput, calls=%fused_computation.81 | convolution fusion | flops 1096809472 | bytes 8394752 | tf_op jit(solution)/shard_map/dot_general | solution.py:530
  154.5 2.6 fusion.32.d_inputs_ref
  157.2 2.5 convolution_convert_fusion
  159.7 2.3 convolution_convert_fusion.1
  163.4 9.8 %spread.2 = (bf16[4096,256]{1,0:T(8,128)(2,1)}, bf16[4096,256]{1,0:T(8,128)(2,1)}) custom-call(f32[1024,512]{1,0:T(8,128)} %fusion.32.d_inputs_ref, s8[1024,4096]{1,0:T(32,128)(4,1)} %get-tuple-element.66.refs_0_, f32[1024,1]{1,0:T(8,128)} %copy.63.refs_1_, s8[1024,4096]{1,0:T(32,128)(4,1)} %get-tuple-element.67.refs_2_, f32[1024,1]{1,0:T(8,128)} %copy.64.refs_3_), custom_call_target="tpu_custom_call" | custom-call | tf_op jit(solution)/shard_map/spread/pallas_call | solution.py:295
  173.3 9.7 %spread.3 = bf16[8192,256]{1,0:T(8,128)(2,1)} custom-call(f32[1024,512]{1,0:T(8,128)} %fusion.32.d_inputs_ref, s8[1024,8192]{1,0:T(32,128)(4,1)} %get-tuple-element.81.refs_0_, f32[1024,1]{1,0:T(8,128)} %copy.63.refs_1_), custom_call_target="tpu_custom_call" | custom-call | tf_op jit(solution)/shard_map/spread/pallas_call | solution.py:295
  182.9 68.1 %all_to_all.22 = bf16[64,128,256]{2,1,0:T(8,128)(2,1)} all-to-all(bf16[64,128,256]{2,1,0:T(8,128)(2,1)} %bitcast.48), channel_id=1, replica_groups=mesh['group'=2,'wide'=64] {'wide'}, dimensions={0} | all-to-all | bytes 8388608 | tf_op jit(solution)/shard_map/all_to_all | solution.py:645
  251.1 18.3 %add_rows.1 = (bf16[2048,256]{1,0:T(8,128)(2,1)S(1)}, bf16[2048,256]{1,0:T(8,128)(2,1)S(1)}, bf16[2048,256]{1,0:T(8,128)(2,1)S(1)}, bf16[2048,256]{1,0:T(8,128)(2,1)S(1)}) custom-call(s32[8192]{0:T(1024)S(1)} %get-tuple-element.78.ids_ref, s32[8192]{0:T(1024)S(1)} %get-tuple-element.79.again_ref, s32[544]{0:T(1024)S(1)} %pad_add_fusion.clash_ref, ...), custom_call_target="tpu_custom_call" | custom-call | tf_op jit(solution)/shard_map/add_rows/pallas_call | solution.py:261
  269.4 5.1 %collective-permute-start = (bf16[2048,256]{1,0:T(8,128)(2,1)S(1)}, bf16[2048,256]{1,0:T(8,128)(2,1)S(1)}, u32[]{:S(2)}, u32[]{:S(2)}) collective-permute-start(bf16[2048,256]{1,0:T(8,128)(2,1)S(1)} %get-tuple-element.82.refs_0_), channel_id=1, source_target_pairs={{0,64},{64,0},{1,65},{65,1},{2,66},{66,2},{3,67},{67,3},{4,68},{68... | collective-permute-start | bytes 3145736 | tf_op jit(solution)/shard_map/ppermute | solution.py:649
  276.7 3.0 collective-permute-done.1.refs_5_
  282.3 7.2 %add_parts.1 = f32[8192,256]{1,0:T(8,128)} custom-call(bf16[2048,256]{1,0:T(8,128)(2,1)} %copy-done.2, bf16[2048,256]{1,0:T(8,128)(2,1)} %copy-done.3, bf16[2048,256]{1,0:T(8,128)(2,1)} %copy-done.4, bf16[2048,256]{1,0:T(8,128)(2,1)} %copy-done.5, bf16[2048,256]{1,0:T(8,128)(2,1)} %copy-done.6, bf16[2048,256]{1,0:T(8,128)(2,1)} %copy-done.7, ...), custom_call_target="tpu_custom_call" | custom-call | tf_op jit(solution)/shard_map/add_parts/pallas_call | solution.py:356
  289.5 94.4 %all-reduce.6.cloned.1.call-done = (bf16[4096,256]{1,0:T(8,128)(2,1)}, bf16[4096,256]{1,0:T(8,128)(2,1)}, bf16[8192,256]{1,0:T(8,128)(2,1)}, bf16[600,1024]{1,0:...) async-done(((bf16[4096,256]{1,0:T(8,128)(2,1)}, bf16[4096,256]{1,0:T(8,128)(2,1)}, bf16[8192,256]{1,0:T(8,128)(2,1)}, bf16[600,1024]{1,0:T(8,128)(2,1)}, ...) | async-done | bytes 10936336 | tf_op jit(solution)/shard_map/psum | solution.py:642
  383.9 12.0 %widen.1 = (f32[4096,256]{1,0:T(8,128)}, f32[4096,256]{1,0:T(8,128)}, f32[8192,256]{1,0:T(8,128)}, f32[1024,512]{1,0:T(8,128)}, f32[600,1024]{1,0:T(8,128)}, /*i...) custom-call(bf16[4096,256]{1,0:T(8,128)(2,1)} %get-tuple-element.86.refs_0_,, ...), custom_call_target="tpu_custom_call" | custom-call | tf_op jit(solution)/shard_map/widen/pallas_call | solution.py:333
  (102 shorter events, 16.3 us)
Async XLA Ops:
  7.2 106.0 %copy-start = (bf16[1024,512]{1,0:T(8,128)(2,1)S(1)}, bf16[1024,512]{1,0:T(8,128)(2,1)}, u32[]{:S(2)}) copy-start(bf16[1024,512]{1,0:T(8,128)(2,1)} %param.24) | copy-start | bytes 3145732
  42.0 5.9 %copy-start.18 = (bf16[1024]{0:T(1024)(128)(2,1)S(1)}, bf16[1024]{0:T(1024)(128)(2,1)}, u32[]{:S(2)}) copy-start(bf16[1024]{0:T(1024)(128)(2,1)} %param.23) | copy-start | bytes 6148
  42.0 5.9 %copy-start.13 = (bf16[1024,88]{0,1:T(8,128)(2,1)S(1)}, bf16[1024,88]{0,1:T(8,128)(2,1)}, u32[]{:S(2)}) copy-start(bf16[1024,88]{0,1:T(8,128)(2,1)} %param.28) | copy-start | bytes 540676
  42.0 6.1 %copy-start.11 = (s32[1024,50]{0,1:T(8,128)S(1)}, s32[1024,50]{0,1:T(8,128)}, u32[]{:S(2)}) copy-start(s32[1024,50]{0,1:T(8,128)} %param.31) | copy-start | bytes 614404
  42.0 6.3 %copy-start.12 = (s32[1024,50]{0,1:T(8,128)S(1)}, s32[1024,50]{0,1:T(8,128)}, u32[]{:S(2)}) copy-start(s32[1024,50]{0,1:T(8,128)} %param.29) | copy-start | bytes 614404
  42.0 57.2 %all-to-all-start.1 = ((bf16[64,128,256]{2,1,0:T(8,128)(2,1)}), bf16[64,128,256]{2,1,0:T(8,128)(2,1)}, u32[]{:S(2)}, u32[]{:S(2)}) async-start(bf16[64,128,256]{2,1,0:T(8,128)(2,1)} %bitcast.46), calls=%async_computation.1 | async-start | bytes 8388608 | tf_op jit(solution)/shard_map/all_to_all | solution.py:578
  47.9 336.0 %all-reduce.6.cloned.1.call-start = ((), (), s32[]{:S(2)}) async-start(), calls=%async_computation.3 | async-start | bytes 21872640 | tf_op jit(solution)/shard_map/psum | solution.py:642
  48.6 6.8 %copy-start.15 = (s32[1024]{0:T(1024)S(1)}, s32[1024]{0:T(1024)}, u32[]{:S(2)}) copy-start(s32[1024]{0:T(1024)} %param.32) | copy-start | bytes 12292
  48.6 6.8 %copy-start.16 = (s32[1024]{0:T(1024)S(1)}, s32[1024]{0:T(1024)}, u32[]{:S(2)}) copy-start(s32[1024]{0:T(1024)} %param.30) | copy-start | bytes 12292
  48.6 6.8 %copy-start.19 = (bf16[512]{0:T(512)(128)(2,1)S(1)}, bf16[512]{0:T(512)(128)(2,1)}, u32[]{:S(2)}) copy-start(bf16[512]{0:T(512)(128)(2,1)} %param.25) | copy-start | bytes 3076
  48.6 6.8 %copy-start.22 = (bf16[256]{0:T(256)(128)(2,1)S(1)}, bf16[256]{0:T(256)(128)(2,1)}, u32[]{:S(2)}) copy-start(bf16[256]{0:T(256)(128)(2,1)} %param.27) | copy-start | bytes 1540
  99.3 9.5 %copy-start.20 = (bf16[600,1024]{1,0:T(8,128)(2,1)S(1)}, bf16[600,1024]{1,0:T(8,128)(2,1)}, u32[]{:S(2)}) copy-start(bf16[600,1024]{1,0:T(8,128)(2,1)} %param.22) | copy-start | bytes 3686404
  113.1 3.0 copy-start.23
  146.5 3.7 copy-start.25
  269.3 11.9 %copy-start.5 = (bf16[2048,256]{1,0:T(8,128)(2,1)}, bf16[2048,256]{1,0:T(8,128)(2,1)S(1)}, u32[]{:S(2)}) copy-start(bf16[2048,256]{1,0:T(8,128)(2,1)S(1)} %get-tuple-element.85.refs_3_) | copy-start | bytes 3145732
  269.3 12.9 %copy-start.2 = (bf16[2048,256]{1,0:T(8,128)(2,1)}, bf16[2048,256]{1,0:T(8,128)(2,1)S(1)}, u32[]{:S(2)}) copy-start(bf16[2048,256]{1,0:T(8,128)(2,1)S(1)} %get-tuple-element.82.refs_0_) | copy-start | bytes 3145732
  269.3 12.9 %copy-start.3 = (bf16[2048,256]{1,0:T(8,128)(2,1)}, bf16[2048,256]{1,0:T(8,128)(2,1)S(1)}, u32[]{:S(2)}) copy-start(bf16[2048,256]{1,0:T(8,128)(2,1)S(1)} %get-tuple-element.83.refs_1_) | copy-start | bytes 3145732
  269.4 12.9 %copy-start.4 = (bf16[2048,256]{1,0:T(8,128)(2,1)}, bf16[2048,256]{1,0:T(8,128)(2,1)S(1)}, u32[]{:S(2)}) copy-start(bf16[2048,256]{1,0:T(8,128)(2,1)S(1)} %get-tuple-element.84.refs_2_) | copy-start | bytes 3145732
  269.4 7.4 %collective-permute-start = (bf16[2048,256]{1,0:T(8,128)(2,1)S(1)}, bf16[2048,256]{1,0:T(8,128)(2,1)S(1)}, u32[]{:S(2)}, u32[]{:S(2)}) collective-permute-start(bf16[2048,256]{1,0:T(8,128)(2,1)S(1)} %get-tuple-element.82.refs_0_), channel_id=1, source_target_pairs={{0,64},{64,0},{1,65},{65,1},{2,66},{66,2},{3,67},{67,3},{4,68},{68... | collective-permute-start | bytes 3145736 | tf_op jit(solution)/shard_map/ppermute | solution.py:649
  274.4 5.3 %collective-permute-start.1 = (bf16[2048,256]{1,0:T(8,128)(2,1)S(1)}, bf16[2048,256]{1,0:T(8,128)(2,1)S(1)}, u32[]{:S(2)}, u32[]{:S(2)}) collective-permute-start(bf16[2048,256]{1,0:T(8,128)(2,1)S(1)} %get-tuple-element.83.refs_1_), channel_id=1, source_target_pairs={{0,64},{64,0},{1,65},{65,1},{2,66},{66,2},{3,67},{67,3},{4,68},{68... | collective-permute-start | bytes 3145736 | tf_op jit(solution)/shard_map/ppermute | solution.py:649
  274.5 6.7 %collective-permute-start.2 = (bf16[2048,256]{1,0:T(8,128)(2,1)S(1)}, bf16[2048,256]{1,0:T(8,128)(2,1)S(1)}, u32[]{:S(2)}, u32[]{:S(2)}) collective-permute-start(bf16[2048,256]{1,0:T(8,128)(2,1)S(1)} %get-tuple-element.84.refs_2_), channel_id=1, source_target_pairs={{0,64},{64,0},{1,65},{65,1},{2,66},{66,2},{3,67},{67,3},{4,68},{68... | collective-permute-start | bytes 3145736 | tf_op jit(solution)/shard_map/ppermute | solution.py:649
  275.0 7.3 %collective-permute-start.3 = (bf16[2048,256]{1,0:T(8,128)(2,1)S(1)}, bf16[2048,256]{1,0:T(8,128)(2,1)}, u32[]{:S(2)}, u32[]{:S(2)}) collective-permute-start(bf16[2048,256]{1,0:T(8,128)(2,1)S(1)} %get-tuple-element.85.refs_3_), channel_id=1, source_target_pairs={{0,64},{64,0},{1,65},{65,1},{2,66},{66,2},{3,67},{67,3},{4,68},{68... | collective-permute-start | bytes 3145736 | tf_op jit(solution)/shard_map/ppermute | solution.py:649
  276.7 4.5 %copy-start.6 = (bf16[2048,256]{1,0:T(8,128)(2,1)}, bf16[2048,256]{1,0:T(8,128)(2,1)S(1)}, u32[]{:S(2)}) copy-start(bf16[2048,256]{1,0:T(8,128)(2,1)S(1)} %collective-permute-done.refs_4_) | copy-start | bytes 3145732
  383.9 14.0 %copy-start.1 = (bf16[1024,512]{1,0:T(8,128)(2,1)S(1)}, bf16[1024,512]{1,0:T(8,128)(2,1)}, u32[]{:S(2)}) copy-start(bf16[1024,512]{1,0:T(8,128)(2,1)} %param.24) | copy-start | bytes 3145732
  (8 other events, 15.7 us)
Sparse Core Ops, SparseCore 0:
  173.4 210.4 all-reduce.5

commit v4 on v3

--- a/solution.py
+++ b/solution.py
@@ -171,9 +171,10 @@
     )(ids, table)
 
 
-def add_rows_body(unroll, ids_ref, again_ref, clash_ref, rows_ref, *refs):
-    out_refs, (total_a, total_b, wide) = refs[:-3], refs[-3:]
-    count = rows_ref.shape[0]
+def add_rows_body(unroll, given_parts, ids_ref, again_ref, clash_ref, *refs):
+    given_refs, out_refs = refs[:given_parts], refs[given_parts:-3]
+    total_a, total_b, wide = refs[-3:]
+    count = sum(ref.shape[0] for ref in given_refs)
     part = out_refs[0].shape[0]
     rows = part * len(out_refs)
 
@@ -184,13 +185,17 @@
 
     lax.fori_loop(0, rows // 128, clear, 0)
 
-    def widen(i, carry):
-        t = rows_ref[pl.ds(pl.multiple_of(i * 128, 128), 128), :].astype(F32)
-        wide[pl.ds(i * 256, 128, stride=2), :] = t[:, :LANES]
-        wide[pl.ds(i * 256 + 1, 128, stride=2), :] = t[:, LANES:]
-        return carry
-
-    lax.fori_loop(0, count // 128, widen, 0)
+    start = 0
+    for ref in given_refs:
+
+        def widen(i, carry, ref=ref, start=start):
+            t = ref[pl.ds(pl.multiple_of(i * 128, 128), 128), :].astype(F32)
+            wide[pl.ds(2 * start + i * 256, 128, stride=2), :] = t[:, :LANES]
+            wide[pl.ds(2 * start + i * 256 + 1, 128, stride=2), :] = t[:, LANES:]
+            return carry
+
+        lax.fori_loop(0, ref.shape[0] // 128, widen, 0)
+        start += ref.shape[0]
 
     def given(at):
         return wide[pl.ds(at * 2, 2), :]
@@ -257,10 +262,10 @@
 
 
 def add_rows_call(plan, given, rows, unroll, parts):
-    count, feat = given.shape
+    count, feat = sum(x.shape[0] for x in given), given[0].shape[1]
     return pl.pallas_call(
-        functools.partial(add_rows_body, unroll),
-        in_specs=[whole_smem()] * 3 + [whole_vmem()],
+        functools.partial(add_rows_body, unroll, len(given)),
+        in_specs=[whole_smem()] * 3 + [whole_vmem()] * len(given),
         out_specs=[whole_vmem()] * parts,
         out_shape=[jax.ShapeDtypeStruct((rows // parts, feat), BF)] * parts,
         scratch_shapes=[pltpu.VMEM((2 * (rows + unroll), LANES), F32)] * 2
@@ -268,7 +273,7 @@
         compiler_params=params(48),
         name="add_rows",
         cost_estimate=pl.CostEstimate(flops=0, bytes_accessed=0, transcendentals=0),
-    )(*plan, given)
+    )(*plan, *given)
 
 
 def spread_body(pairs, firsts, d_inputs_ref, *refs):
@@ -302,6 +307,38 @@
         compiler_params=params(60),
         name="spread",
     )(*args)
+
+
+def slot_spread_body(cuts, counts_ref, length_ref, d_inputs_ref, *refs):
+    out_refs, part_ref = refs[:-1], refs[-1]
+    feat = part_ref.shape[1]
+
+    @pl.when(pl.program_id(0) == 0)
+    def _():
+        part_ref[...] = (d_inputs_ref[:, :feat] / length_ref[...]).astype(BF)
+
+    grad = left_product(counts_ref[...].astype(BF), part_ref[...])
+    grad = grad.reshape(-1, sum(cuts), feat)
+    start = 0
+    for ref, cut in zip(out_refs, cuts):
+        ref[...] = grad[:, start : start + cut, :].astype(BF)
+        start += cut
+
+
+def slot_spread_call(counts, lengths, d_inputs, feat, cuts, steps):
+    n, slots = counts.shape
+    owners = slots // sum(cuts)
+    return pl.pallas_call(
+        functools.partial(slot_spread_body, cuts),
+        grid=(steps,),
+        in_specs=[pl.BlockSpec((n, slots // steps), lambda i: (0, i)), whole_vmem(), whole_vmem()],
+        out_specs=[pl.BlockSpec((owners // steps, cut, feat), lambda i: (i, 0, 0)) for cut in cuts],
+        out_shape=[jax.ShapeDtypeStruct((owners, cut, feat), BF) for cut in cuts],
+        scratch_shapes=[pltpu.VMEM((n, feat), BF)],
+        compiler_params=params(60),
+        cost_estimate=pl.CostEstimate(flops=0, bytes_accessed=0, transcendentals=0),
+        name="slot_spread",
+    )(counts, lengths, d_inputs)
 
 
 def widen_body(blocked, *refs):
@@ -410,7 +447,12 @@
     label = label_ref[...]
     user_t = user_t_ref[...]
     user = user_t.astype(F32).T.astype(BF)
-    iota = lax.broadcasted_iota(jnp.int32, (chunk, block), 0)
+    sublane = lax.broadcasted_iota(jnp.int32, (8, block), 0)
+
+    def hits(c):
+        place = label - c * chunk - sublane
+        return jnp.concatenate([place == 8 * g for g in range(chunk // 8)], axis=0)
+
 
     def fold(v, op):
         return op(v.reshape(chunk // 8, 8, block), axis=0)
@@ -423,7 +465,7 @@
 
         peak, pos = carry
         s = jnp.dot(table_ref[at(c), :], user_t, preferred_element_type=F32)
-        pos = pos + fold(jnp.where(iota == label - c * chunk, s, 0.0), jnp.sum)
+        pos = pos + fold(jnp.where(hits(c), s, 0.0), jnp.sum)
         s = s + jnp.concatenate([mask_ref[at(c), :]] * (block // LANES), axis=1)
         logits[at(c), :] = s
         return jnp.maximum(peak, fold(s, jnp.max)), pos
@@ -456,7 +498,7 @@
     def back(add, store):
         def third(c, d_user_t):
             d = logits[at(c), :] * scale
-            d = jnp.where(iota == label - c * chunk, d + d_pos, d).astype(BF)
+            d = jnp.where(hits(c), d + d_pos, d).astype(BF)
             term = jnp.dot(d, user, preferred_element_type=F32)
             if add:
                 term = grad_sum[at(c), :] + term
@@ -482,7 +524,7 @@
         back(True, True)
 
 
-def softmax_call(mask, table, table_t, user, labels, block=512, chunk=2048):
+def softmax_call(mask, table, table_t, user, labels, block=512, chunk=4096):
     n, feat = user.shape
     rows = table.shape[0]
     across = lambda h: pl.BlockSpec((h, block), lambda i: (0, i))
@@ -590,7 +632,10 @@
     out_table_t = out_table.T
     mask = sampled_mask(negatives, out_table.shape[0])
     unroll = 16
-    plan = row_plan(asked.reshape(slots), shard_rows, unroll)
+    cuts = (16, 16, 16, 32, 16, 16, 16)
+    edges = [sum(cuts[:i]) for i in range(len(cuts) + 1)]
+    asked_parts = [asked[:, i:j].reshape(-1) for i, j in zip(edges, edges[1:])]
+    plan = row_plan(jnp.concatenate(asked_parts), shard_rows, unroll)
     ids, out_table_t, mask, plan, looked = lax.optimization_barrier(
         (ids, out_table_t, mask, plan, looked)
     )
@@ -641,10 +686,13 @@
     packed, slot_counts = lax.optimization_barrier((packed, slot_counts))
     summed = lax.psum(packed, ("group", "wide"))
 
-    (slot_grad,) = spread_call((slot_counts,), (hist_float,), d_inputs, (0,), feat, 4)
-    owed = lax.all_to_all(
-        slot_grad.reshape(owners, per_owner, feat), "wide", split_axis=0, concat_axis=0, tiled=True
-    ).reshape(slots, feat)
+    slot_grads = slot_spread_call(slot_counts, hist_float, d_inputs, feat, cuts, 4)
+    owed = []
+    for part in slot_grads:
+        if owed:
+            part, owed[-1] = lax.optimization_barrier((part, owed[-1]))
+        owed.append(lax.all_to_all(part, "wide", split_axis=0, concat_axis=0, tiled=True))
+    owed = [x.reshape(-1, feat) for x in owed]
     own = add_rows_call(plan, owed, shard_rows, unroll, 4)
     others = [lax.ppermute(x, "group", [(0, 1), (1, 0)]) for x in own]
     tail_grad = add_pair_call(own, others)

time: 411 us -> 386 us (0.939)
  waiting for transfers between devices: 101 us -> 14 us
  blocking collectives: 88.8 us -> 145 us
  starting transfers between devices: 11.5 us -> 16.9 us
    psum x1, waiting for transfers between devices: 94.4 us -> 5.81 us  [local(): summed = lax.psum(packed, ('group', 'wide'))]
    all_to_all x1 -> x7, blocking collectives: 68.1 us -> 124 us  [local(): lax.all_to_all(part, 'wide', split_axis=0, concat_axis=0, tiled=True)]
    pallas_call x1 -> x2, Pallas kernels: 18.3 us -> 28.7 us  [the longest x1 19.1 us: add_rows_call(): pl.pallas_call(functools.partial(add_rows_body, unroll, len(given)), in_s...]
    pallas_call x2 -> x1, Pallas kernels: 19.5 us -> 9.8 us  [spread_call(): pl.pallas_call(functools.partial(spread_body, len(counts), firsts), grid=...]
    ppermute x4, starting transfers between devices: 5.68 us -> 10.9 us  [local(): others = [lax.ppermute(x, 'group', [(0, 1), (1, 0)]) for x in own]]
    unnamed x56 -> x68, local copies, waits for them, and re-layouts: 8.34 us -> 9.12 us
  transfers between devices with their start and end apart: 6 -> 6, of which waited for: 4 -> 3; matrix products, arithmetic and copies ran while one was open for 4% -> 4% of each run, Pallas kernels for 17% -> 18%
where the time goes in v4:
time: 386 us; the launch traced here: 381 us
  blocking collectives  145 us (38%)
  Pallas kernels  133 us (34%)
  matrix products  34.7 us (9%)
  starting transfers between devices  16.9 us (4%)
  between operations  16.6 us (4%)
  local copies, waits for them, and re-layouts  15.3 us (4%)
  waiting for transfers between devices  14 us (4%)
  other arithmetic  5.39 us (1%)
    all_to_all x7, blocking collectives, local(): lax.all_to_all(part, 'wide', split_axis=0, concat_axis=0, tiled=True)  124 us
    pallas_call x1, Pallas kernels, counts_call(): pl.pallas_call(functools.partial(counts_body, cuts), grid=(n // block,),...  34.5 us
    pallas_call x1, Pallas kernels, softmax_call(): pl.pallas_call(functools.partial(softmax_body, 1.0 / n, chunk), grid=(n /...  26.8 us
    all_to_all x1, blocking collectives, local(): lax.all_to_all(requests, 'wide', split_axis=0, concat_axis=0, tiled=True)  20.7 us
    pallas_call x1, Pallas kernels, add_rows_call(): pl.pallas_call(functools.partial(add_rows_body, unroll, len(given)), in_s...  19.1 us
    pallas_call x1, Pallas kernels, gather_call(): pl.pallas_call(functools.partial(gather_body, parts), in_specs=[whole_sme...  14.1 us
    pallas_call x1, Pallas kernels, widen_call(): pl.pallas_call(functools.partial(widen_body, len(arrays)), grid=(steps,),...  12 us
    dot_general x4, matrix products, right_product(): lax.dot_general(first_op, second_op, (((1,), (1,)), ((), ())), preferred_...  11 us
  transfers between devices with their start and end apart: 6, of which 3 were waited for; matrix products, arithmetic and copies ran while one was open for 4% of the time, Pallas kernels for 18%

profile of v4, /device:TPU:1, one launch (start us, length us, event | category | flops | bytes accessed | tf_op | source)
XLA Modules:
  0.0 381.1 jit_solution(17814293180252993407)
XLA Ops:
  7.2 20.7 %all_to_all.51 = s32[64,1,128]{2,1,0:T(1,128)} all-to-all(s32[64,1,128]{2,1,0:T(1,128)} %bitcast.51), channel_id=1, replica_groups=mesh['group'=2,'wide'=64] {'wide'}, dimensions={0} | all-to-all | bytes 65536 | tf_op jit(solution)/shard_map/all_to_all | solution.py:618
  27.9 14.1 %gather_rows.1 = bf16[8192,256]{1,0:T(8,128)(2,1)} custom-call(s32[64,128]{1,0:T(8,128)} %bitcast.47, bf16[8192,256]{1,0:T(8,128)(2,1)} %table_hbm.2), custom_call_target="tpu_custom_call" | custom-call | tf_op jit(solution)/shard_map/gather_rows/pallas_call | solution.py:157
  42.0 5.8 %all-to-all-start.1 = ((bf16[64,128,256]{2,1,0:T(8,128)(2,1)}), bf16[64,128,256]{2,1,0:T(8,128)(2,1)}, u32[]{:S(2)}, u32[]{:S(2)}) async-start(bf16[64,128,256]{2,1,0:T(8,128)(2,1)} %bitcast.45), calls=%async_computation.1 | async-start | bytes 8388608 | tf_op jit(solution)/shard_map/all_to_all | solution.py:620
  48.8 6.4 %copy.55 = bf16[8192,256]{0,1:T(8,128)(2,1)} copy(bf16[8192,256]{1,0:T(8,128)(2,1)} %table_hbm.3) | data formatting | bytes 8388608 | tf_op args[3]
  64.1 34.5 %counts.1 = (s8[1024,4096]{1,0:T(32,128)(4,1)}, s8[1024,8192]{1,0:T(32,128)(4,1)}, s8[1024,4096]{1,0:T(32,128)(4,1)}, f32[1024,256]{1,0:T(8,128)}, f32[1024,256]{1,0:T(8,128)}) custom-call(s32[1024,128]{1,0:T(8,128)} %select_add_fusion.ids_ref, bf16[4096,256]{1,0:T(8,128)(2,1)} %hot_ref.1, bf16[4096,256]{1,0:T(8,128)(2,1)} %word_ref.1), custom_call_target="tpu_custom_call" | custom-call | tf_op jit(solution)/shard_map/counts/pallas_call | solution.py:85
  100.1 9.5 %fusion.24 = bf16[1024,256]{1,0:T(8,128)(2,1)S(1)} fusion(f32[1024,256]{1,0:T(8,128)} %get-tuple-element.81, bf16[8192,256]{1,0:T(8,128)(2,1)} %bitcast.5, s8[1024,8192]{1,0:T(32,128)(4,1)} %get-tuple-element.100.counts_ref, f32[1024]{0:T(1024)S(1)} %convert_element_type.77), kind=kOutput, calls=%fused_computation.32 | convolution fusion | flops 4304142336 | bytes 14159872 | tf_op jit(solution)/shard_map/dot_general | solution.py:646
  109.6 4.6 %multiply_convert_fusion = (bf16[1024,1024]{1,0:T(8,128)(2,1)S(1)}, f32[1024,1024]{1,0:T(8,128)}) fusion(f32[1024]{0:T(1024)S(1)} %convert_element_type.79, bf16[600,1024]{1,0:T(8,128)(2,1)S(1)} %copy-done.23, bf16[1024,88]{1,0:T(8,128)(2,1)S(1)} %copy.61, bf16[1024,256]{1,0:T(8,128)(2,1)S(1)} %divide_convert_fusion, bf16[1024,256]{1,0:T(8,128)(2,1)S(1)} %fusion.24), kind=kOutput, calls=%fused_computation.11 | convolution fusion | flops 1272463360 | bytes 8753152 | tf_op jit(solution)/shard_map/dot_general | solution.py:649
  118.5 26.8 %sampled_softmax.1 = (bf16[256,1024]{1,0:T(8,128)(2,1)}, bf16[8192,256]{1,0:T(8,128)(2,1)}, f32[1,1024]{1,0:T(1,128)}) custom-call(f32[8192,128]{1,0:T(8,128)} %broadcast_in_dim.18.mask_hbm, bf16[8192,256]{1,0:T(8,128)(2,1)} %table_hbm.3, bf16[256,8192]{1,0:T(8,128)(2,1)} %bitcast.44, bf16[256,1024]{1,0:T(8,128)(2,1)} %fusion.28.user_t_ref, s32[1,1024]{1,0:T(1,128)} %bitcast.53), custom_call_target="tpu_custom_call" | custom-call | tf_op jit(solution)/shard_map/sampled_softmax/pallas_call | solution.py:532
  149.0 4.0 %fusion.52 = (bf16[1024]{0:T(1024)(128)(2,1)S(1)}, bf16[1024,1024]{1,0:T(8,128)(2,1)S(1)}) fusion(f32[1024,1024]{1,0:T(8,128)S(1)} %copy-done.28, f32[1024]{0:T(1024)S(1)} %convert_element_type.79, bf16[1024,512]{1,0:T(8,128)(2,1)S(1)} %get-tuple-element.162, bf16[1024,512]{1,0:T(8,128)(2,1)S(1)} %copy-done), kind=kOutput, calls=%fused_computation.89 | convolution fusion | flops 1096809472 | bytes 8394752 | tf_op jit(solution)/shard_map/dot_general | solution.py:572
  162.1 9.8 %spread.1 = (bf16[4096,256]{1,0:T(8,128)(2,1)}, bf16[4096,256]{1,0:T(8,128)(2,1)}) custom-call(f32[1024,512]{1,0:T(8,128)} %fusion.32.d_inputs_ref, s8[1024,4096]{1,0:T(32,128)(4,1)} %get-tuple-element.85.refs_0_, f32[1024,1]{1,0:T(8,128)} %copy.63.refs_1_.length_ref, s8[1024,4096]{1,0:T(32,128)(4,1)} %get-tuple-element.86.refs_2_, f32[1024,1]{1,0:T(8,128)} %copy.64.refs_3_), custom_call_target="tpu_custom_call" | custom-call | tf_op jit(solution)/shard_map/spread/pallas_call | solution.py:300
  171.9 9.5 %slot_spread.1 = (bf16[64,16,256]{2,1,0:T(8,128)(2,1)}, bf16[64,16,256]{2,1,0:T(8,128)(2,1)}, bf16[64,16,256]{2,1,0:T(8,128)(2,1)}, bf16[64,32,256]{2,1,0:T(8,12...) custom-call(s8[1024,8192]{1,0:T(32,128)(4,1)} %get-tuple-element.100.counts_ref, ...), custom_call_target="tpu_custom_call" | custom-call | tf_op jit(solution)/shard_map/slot_spread/pallas_call | solution.py:331
  181.4 24.0 %all_to_all.52 = bf16[64,16,256]{2,1,0:T(8,128)(2,1)S(1)} all-to-all(bf16[64,16,256]{2,1,0:T(8,128)(2,1)} %get-tuple-element.102), channel_id=1, replica_groups=mesh['group'=2,'wide'=64] {'wide'}, dimensions={0} | all-to-all | bytes 1048576 | tf_op jit(solution)/shard_map/all_to_all | solution.py:694
  205.4 18.3 %all_to_all.53 = bf16[64,16,256]{2,1,0:T(8,128)(2,1)S(1)} all-to-all(bf16[64,16,256]{2,1,0:T(8,128)(2,1)} %get-tuple-element.105), channel_id=1, replica_groups=mesh['group'=2,'wide'=64] {'wide'}, dimensions={0} | all-to-all | bytes 1048576 | tf_op jit(solution)/shard_map/all_to_all | solution.py:694
  223.7 16.6 %all_to_all.54 = bf16[64,16,256]{2,1,0:T(8,128)(2,1)S(1)} all-to-all(bf16[64,16,256]{2,1,0:T(8,128)(2,1)S(1)} %copy-done.13), channel_id=1, replica_groups=mesh['group'=2,'wide'=64] {'wide'}, dimensions={0} | all-to-all | bytes 1048576 | tf_op jit(solution)/shard_map/all_to_all | solution.py:694
  240.2 20.1 %all_to_all.55 = bf16[64,32,256]{2,1,0:T(8,128)(2,1)} all-to-all(bf16[64,32,256]{2,1,0:T(8,128)(2,1)S(1)} %copy-done.8), channel_id=1, replica_groups=mesh['group'=2,'wide'=64] {'wide'}, dimensions={0} | all-to-all | bytes 2097152 | tf_op jit(solution)/shard_map/all_to_all | solution.py:694
  260.3 15.0 %all_to_all.56 = bf16[64,16,256]{2,1,0:T(8,128)(2,1)S(1)} all-to-all(bf16[64,16,256]{2,1,0:T(8,128)(2,1)S(1)} %copy-done.12), channel_id=1, replica_groups=mesh['group'=2,'wide'=64] {'wide'}, dimensions={0} | all-to-all | bytes 1048576 | tf_op jit(solution)/shard_map/all_to_all | solution.py:694
  275.3 15.4 %all_to_all.57 = bf16[64,16,256]{2,1,0:T(8,128)(2,1)S(1)} all-to-all(bf16[64,16,256]{2,1,0:T(8,128)(2,1)S(1)} %copy-done.11), channel_id=1, replica_groups=mesh['group'=2,'wide'=64] {'wide'}, dimensions={0} | all-to-all | bytes 1048576 | tf_op jit(solution)/shard_map/all_to_all | solution.py:694
  290.8 15.0 %all_to_all.58 = bf16[64,16,256]{2,1,0:T(8,128)(2,1)S(1)} all-to-all(bf16[64,16,256]{2,1,0:T(8,128)(2,1)S(1)} %copy-done.10), channel_id=1, replica_groups=mesh['group'=2,'wide'=64] {'wide'}, dimensions={0} | all-to-all | bytes 1048576 | tf_op jit(solution)/shard_map/all_to_all | solution.py:694
  305.8 19.1 %add_rows.1 = (bf16[2048,256]{1,0:T(8,128)(2,1)S(1)}, bf16[2048,256]{1,0:T(8,128)(2,1)S(1)}, bf16[2048,256]{1,0:T(8,128)(2,1)}, bf16[2048,256]{1,0:T(8,128)(2,1)}) custom-call(s32[8192]{0:T(1024)S(1)} %get-tuple-element.97.ids_ref, s32[8192]{0:T(1024)S(1)} %get-tuple-element.98.again_ref, s32[544]{0:T(1024)S(1)} %pad_add_fusion.clash_ref, ...), custom_call_target="tpu_custom_call" | custom-call | tf_op jit(solution)/shard_map/add_rows/pallas_call | solution.py:266
  324.9 10.3 %collective-permute-start = (bf16[2048,256]{1,0:T(8,128)(2,1)S(1)}, bf16[2048,256]{1,0:T(8,128)(2,1)S(1)}, u32[]{:S(2)}, u32[]{:S(2)}) collective-permute-start(bf16[2048,256]{1,0:T(8,128)(2,1)S(1)} %get-tuple-element.120.refs_0_), channel_id=1, source_target_pairs={{0,64},{64,0},{1,65},{65,1},{2,66},{66,2},{3,67},{67,3},{4,68},{68... | collective-permute-start | bytes 3145736 | tf_op jit(solution)/shard_map/ppermute | solution.py:697
  339.3 4.7 %collective-permute-done.1.refs_5_ = bf16[2048,256]{1,0:T(8,128)(2,1)S(1)} collective-permute-done((bf16[2048,256]{1,0:T(8,128)(2,1)S(1)}, bf16[2048,256]{1,0:T(8,128)(2,1)S(1)}, u32[]{:S(2)}, u32[]{:S(2)}) %collective-permute-start.1) | collective-permute-done | bytes 1048608 | tf_op jit(solution)/shard_map/ppermute | solution.py:697
  345.9 7.3 %add_parts.1 = f32[8192,256]{1,0:T(8,128)} custom-call(bf16[2048,256]{1,0:T(8,128)(2,1)} %copy-done.2, bf16[2048,256]{1,0:T(8,128)(2,1)} %copy-done.3, bf16[2048,256]{1,0:T(8,128)(2,1)} %get-tuple-element.122.refs_2_, bf16[2048,256]{1,0:T(8,128)(2,1)} %get-tuple-element.123.refs_3_, bf16[2048,256]{1,0:T(8,128)(2,1)} %copy-done.5, ...), custom_call_target="tpu_custom_call" | custom-call | tf_op jit(solution)/shard_map/add_parts/pallas_call | solution.py:393
  353.2 5.8 %all-reduce.6.cloned.1.call-done = (bf16[4096,256]{1,0:T(8,128)(2,1)}, bf16[4096,256]{1,0:T(8,128)(2,1)}, bf16[8192,256]{1,0:T(8,128)(2,1)}, bf16[600,1024]{1,0:...) async-done(((bf16[4096,256]{1,0:T(8,128)(2,1)}, bf16[4096,256]{1,0:T(8,128)(2,1)}, bf16[8192,256]{1,0:T(8,128)(2,1)}, bf16[600,1024]{1,0:T(8,128)(2,1)}, ...) | async-done | bytes 10936336 | tf_op jit(solution)/shard_map/psum | solution.py:687
  359.0 12.0 %widen.1 = (f32[4096,256]{1,0:T(8,128)}, f32[4096,256]{1,0:T(8,128)}, f32[8192,256]{1,0:T(8,128)}, f32[1024,512]{1,0:T(8,128)}, f32[600,1024]{1,0:T(8,128)}, /*i...) custom-call(bf16[4096,256]{1,0:T(8,128)(2,1)} %get-tuple-element.124.refs_0_, ...), custom_call_target="tpu_custom_call" | custom-call | tf_op jit(solution)/shard_map/widen/pallas_call | solution.py:370
  (130 shorter events, 35.3 us)
Async XLA Ops:
  7.2 107.1 %copy-start = (bf16[1024,512]{1,0:T(8,128)(2,1)S(1)}, bf16[1024,512]{1,0:T(8,128)(2,1)}, u32[]{:S(2)}) copy-start(bf16[1024,512]{1,0:T(8,128)(2,1)} %param.24) | copy-start | bytes 3145732
  42.0 6.1 %copy-start.16 = (bf16[1024,88]{0,1:T(8,128)(2,1)S(1)}, bf16[1024,88]{0,1:T(8,128)(2,1)}, u32[]{:S(2)}) copy-start(bf16[1024,88]{0,1:T(8,128)(2,1)} %param.28) | copy-start | bytes 540676
  42.0 6.3 %copy-start.14 = (s32[1024,50]{0,1:T(8,128)S(1)}, s32[1024,50]{0,1:T(8,128)}, u32[]{:S(2)}) copy-start(s32[1024,50]{0,1:T(8,128)} %param.31) | copy-start | bytes 614404
  42.0 6.5 %copy-start.15 = (s32[1024,50]{0,1:T(8,128)S(1)}, s32[1024,50]{0,1:T(8,128)}, u32[]{:S(2)}) copy-start(s32[1024,50]{0,1:T(8,128)} %param.29) | copy-start | bytes 614404
  42.0 58.1 %all-to-all-start.1 = ((bf16[64,128,256]{2,1,0:T(8,128)(2,1)}), bf16[64,128,256]{2,1,0:T(8,128)(2,1)}, u32[]{:S(2)}, u32[]{:S(2)}) async-start(bf16[64,128,256]{2,1,0:T(8,128)(2,1)} %bitcast.45), calls=%async_computation.1 | async-start | bytes 8388608 | tf_op jit(solution)/shard_map/all_to_all | solution.py:620
  47.8 311.1 %all-reduce.6.cloned.1.call-start = ((), (), s32[]{:S(2)}) async-start(), calls=%async_computation.9 | async-start | bytes 21872640 | tf_op jit(solution)/shard_map/psum | solution.py:687
  48.8 6.6 %copy-start.18 = (s32[1024]{0:T(1024)S(1)}, s32[1024]{0:T(1024)}, u32[]{:S(2)}) copy-start(s32[1024]{0:T(1024)} %param.32) | copy-start | bytes 12292
  48.8 6.7 %copy-start.19 = (s32[1024]{0:T(1024)S(1)}, s32[1024]{0:T(1024)}, u32[]{:S(2)}) copy-start(s32[1024]{0:T(1024)} %param.30) | copy-start | bytes 12292
  48.8 6.7 %copy-start.22 = (bf16[512]{0:T(512)(128)(2,1)S(1)}, bf16[512]{0:T(512)(128)(2,1)}, u32[]{:S(2)}) copy-start(bf16[512]{0:T(512)(128)(2,1)} %param.25) | copy-start | bytes 3076
  48.8 6.7 %copy-start.25 = (bf16[256]{0:T(256)(128)(2,1)S(1)}, bf16[256]{0:T(256)(128)(2,1)}, u32[]{:S(2)}) copy-start(bf16[256]{0:T(256)(128)(2,1)} %param.27) | copy-start | bytes 1540
  100.1 9.5 %copy-start.23 = (bf16[600,1024]{1,0:T(8,128)(2,1)S(1)}, bf16[600,1024]{1,0:T(8,128)(2,1)}, u32[]{:S(2)}) copy-start(bf16[600,1024]{1,0:T(8,128)(2,1)} %param.22) | copy-start | bytes 3686404
  181.4 42.3 %copy-start.13 = (bf16[64,16,256]{2,1,0:T(8,128)(2,1)S(1)}, bf16[64,16,256]{2,1,0:T(8,128)(2,1)}, u32[]{:S(2)}) copy-start(bf16[64,16,256]{2,1,0:T(8,128)(2,1)} %get-tuple-element.108) | copy-start | bytes 1572868
  181.4 58.8 %copy-start.8 = (bf16[64,32,256]{2,1,0:T(8,128)(2,1)S(1)}, bf16[64,32,256]{2,1,0:T(8,128)(2,1)}, u32[]{:S(2)}) copy-start(bf16[64,32,256]{2,1,0:T(8,128)(2,1)} %get-tuple-element.111) | copy-start | bytes 3145732
  205.4 54.9 %copy-start.12 = (bf16[64,16,256]{2,1,0:T(8,128)(2,1)S(1)}, bf16[64,16,256]{2,1,0:T(8,128)(2,1)}, u32[]{:S(2)}) copy-start(bf16[64,16,256]{2,1,0:T(8,128)(2,1)} %get-tuple-element.114) | copy-start | bytes 1572868
  223.7 51.7 %copy-start.11 = (bf16[64,16,256]{2,1,0:T(8,128)(2,1)S(1)}, bf16[64,16,256]{2,1,0:T(8,128)(2,1)}, u32[]{:S(2)}) copy-start(bf16[64,16,256]{2,1,0:T(8,128)(2,1)} %get-tuple-element.117) | copy-start | bytes 1572868
  240.2 50.5 %copy-start.10 = (bf16[64,16,256]{2,1,0:T(8,128)(2,1)S(1)}, bf16[64,16,256]{2,1,0:T(8,128)(2,1)}, u32[]{:S(2)}) copy-start(bf16[64,16,256]{2,1,0:T(8,128)(2,1)} %get-tuple-element.119) | copy-start | bytes 1572868
  324.9 21.0 %copy-start.2 = (bf16[2048,256]{1,0:T(8,128)(2,1)}, bf16[2048,256]{1,0:T(8,128)(2,1)S(1)}, u32[]{:S(2)}) copy-start(bf16[2048,256]{1,0:T(8,128)(2,1)S(1)} %get-tuple-element.120.refs_0_) | copy-start | bytes 3145732
  324.9 21.0 %copy-start.3 = (bf16[2048,256]{1,0:T(8,128)(2,1)}, bf16[2048,256]{1,0:T(8,128)(2,1)S(1)}, u32[]{:S(2)}) copy-start(bf16[2048,256]{1,0:T(8,128)(2,1)S(1)} %get-tuple-element.121.refs_1_) | copy-start | bytes 3145732
  324.9 14.4 %collective-permute-start = (bf16[2048,256]{1,0:T(8,128)(2,1)S(1)}, bf16[2048,256]{1,0:T(8,128)(2,1)S(1)}, u32[]{:S(2)}, u32[]{:S(2)}) collective-permute-start(bf16[2048,256]{1,0:T(8,128)(2,1)S(1)} %get-tuple-element.120.refs_0_), channel_id=1, source_target_pairs={{0,64},{64,0},{1,65},{65,1},{2,66},{66,2},{3,67},{67,3},{4,68},{68... | collective-permute-start | bytes 3145736 | tf_op jit(solution)/shard_map/ppermute | solution.py:697
  335.2 8.8 %collective-permute-start.1 = (bf16[2048,256]{1,0:T(8,128)(2,1)S(1)}, bf16[2048,256]{1,0:T(8,128)(2,1)S(1)}, u32[]{:S(2)}, u32[]{:S(2)}) collective-permute-start(bf16[2048,256]{1,0:T(8,128)(2,1)S(1)} %get-tuple-element.121.refs_1_), channel_id=1, source_target_pairs={{0,64},{64,0},{1,65},{65,1},{2,66},{66,2},{3,67},{67,3},{4,68},{68... | collective-permute-start | bytes 3145736 | tf_op jit(solution)/shard_map/ppermute | solution.py:697
  335.3 9.6 %collective-permute-start.2 = (bf16[2048,256]{1,0:T(8,128)(2,1)}, bf16[2048,256]{1,0:T(8,128)(2,1)S(1)}, u32[]{:S(2)}, u32[]{:S(2)}) collective-permute-start(bf16[2048,256]{1,0:T(8,128)(2,1)} %get-tuple-element.122.refs_2_), channel_id=1, source_target_pairs={{0,64},{64,0},{1,65},{65,1},{2,66},{66,2},{3,67},{67,3},{4,68},{68... | collective-permute-start | bytes 3145736 | tf_op jit(solution)/shard_map/ppermute | solution.py:697
  335.7 10.2 %collective-permute-start.3 = (bf16[2048,256]{1,0:T(8,128)(2,1)}, bf16[2048,256]{1,0:T(8,128)(2,1)}, u32[]{:S(2)}, u32[]{:S(2)}) collective-permute-start(bf16[2048,256]{1,0:T(8,128)(2,1)} %get-tuple-element.123.refs_3_), channel_id=1, source_target_pairs={{0,64},{64,0},{1,65},{65,1},{2,66},{66,2},{3,67},{67,3},{4,68},{68... | collective-permute-start | bytes 3145736 | tf_op jit(solution)/shard_map/ppermute | solution.py:697
  339.3 6.6 %copy-start.5 = (bf16[2048,256]{1,0:T(8,128)(2,1)}, bf16[2048,256]{1,0:T(8,128)(2,1)S(1)}, u32[]{:S(2)}) copy-start(bf16[2048,256]{1,0:T(8,128)(2,1)S(1)} %collective-permute-done.refs_4_) | copy-start | bytes 3145732
  359.0 14.0 %copy-start.1 = (bf16[1024,512]{1,0:T(8,128)(2,1)S(1)}, bf16[1024,512]{1,0:T(8,128)(2,1)}, u32[]{:S(2)}) copy-start(bf16[1024,512]{1,0:T(8,128)(2,1)} %param.24) | copy-start | bytes 3145732
  (11 other events, 28.5 us)
Sparse Core Ops, SparseCore 0:
  172.0 186.9 all-reduce.5

commit v5 on v4

--- a/solution.py
+++ b/solution.py
@@ -276,37 +276,106 @@
     )(*plan, *given)
 
 
-def spread_body(pairs, firsts, d_inputs_ref, *refs):
-    part_refs = refs[3 * pairs :]
-    feat = part_refs[0].shape[1]
-
-    @pl.when(pl.program_id(0) == 0)
-    def _():
-        for i, first in enumerate(firsts):
-            d_mean = d_inputs_ref[:, first : first + feat]
-            part_refs[i][...] = (d_mean / refs[2 * i + 1][...]).astype(BF)
-
-    for i in range(pairs):
-        counts_ref, out_ref = refs[2 * i], refs[2 * pairs + i]
-        out_ref[...] = left_product(counts_ref[...].astype(BF), part_refs[i][...]).astype(BF)
-
-
-def spread_call(counts, lengths, d_inputs, firsts, feat, steps):
-    n = d_inputs.shape[0]
-    specs, args = [whole_vmem()], [d_inputs]
-    for c, x in zip(counts, lengths):
-        specs += [pl.BlockSpec((n, c.shape[1] // steps), lambda i: (0, i)), whole_vmem()]
-        args += [c, x]
+def gradients_body(
+    d_inputs_ref,
+    hist_ref,
+    search_ref,
+    mean_ref,
+    word_mean_ref,
+    dense_ref,
+    act1_ref,
+    act2_ref,
+    d_pre1_ref,
+    d_pre2_ref,
+    d_user_ref,
+    loss_ref,
+    b1_ref,
+    b2_ref,
+    hot_counts_ref,
+    word_counts_ref,
+    hot_ref,
+    word_ref,
+    g1_ref,
+    g2_ref,
+    g3_ref,
+    hot_part,
+    word_part,
+):
+    step = pl.program_id(0)
+    feat = hot_part.shape[1]
+
+    @pl.when(step == 0)
+    def _():
+        hot_part[...] = (d_inputs_ref[:, :feat] / hist_ref[...]).astype(BF)
+        word_part[...] = (d_inputs_ref[:, feat:] / search_ref[...]).astype(BF)
+
+    for counts_ref, part, out_ref in (
+        (hot_counts_ref, hot_part, hot_ref),
+        (word_counts_ref, word_part, word_ref),
+    ):
+        out_ref[...] = left_product(counts_ref[...].astype(BF), part[...]).astype(BF)
+
+    half = g1_ref.shape[1] // 2
+    for k in range(2):
+
+        @pl.when(step == k)
+        def _(k=k):
+            columns = slice(k * half, (k + 1) * half)
+            start = 0
+            for given_ref in (mean_ref, word_mean_ref, dense_ref):
+                end = start + given_ref.shape[1]
+                grad = left_product(given_ref[...], d_pre1_ref[:, columns])
+                g1_ref[start:end, columns] = grad.astype(BF)
+                start = end
+
+    @pl.when(step == 2)
+    def _():
+        g2_ref[...] = left_product(act1_ref[...], d_pre2_ref[...]).astype(BF)
+
+    @pl.when(step == 3)
+    def _():
+        d_user = d_user_ref[...]
+        rows = act2_ref.shape[1]
+        g3_ref[:rows, :] = left_product(act2_ref[...], d_user).astype(BF)
+        b3 = jnp.sum(d_user.astype(F32), axis=0, keepdims=True)
+        small = [
+            x[:, i : i + feat]
+            for x in (loss_ref[...], b1_ref[...], b2_ref[...], b3)
+            for i in range(0, x.shape[1], feat)
+        ]
+        spare = g3_ref.shape[0] - rows - len(small)
+        small.append(jnp.zeros((spare, feat), F32))
+        g3_ref[rows:, :] = jnp.concatenate(small, axis=0).astype(BF)
+
+
+def gradients_call(
+    d_inputs, lengths, inputs, act1, act2, d_pre1, d_pre2, d_user, loss, b1, b2, counts
+):
+    hot_counts, word_counts = counts
+    n, feat = d_user.shape
+    steps = 4
+    small = sum(x.shape[1] // feat for x in (loss, b1, b2, d_user))
+    counts_spec = lambda c: pl.BlockSpec((n, c.shape[1] // steps), lambda i: (0, i))
+    rows_spec = lambda c: pl.BlockSpec((c.shape[1] // steps, feat), lambda i: (i, 0))
+    shapes = [
+        (hot_counts.shape[1], feat),
+        (word_counts.shape[1], feat),
+        (sum(x.shape[1] for x in inputs), d_pre1.shape[1]),
+        (act1.shape[1], d_pre2.shape[1]),
+        (act2.shape[1] + small + -small % 16, feat),
+    ]
     return pl.pallas_call(
-        functools.partial(spread_body, len(counts), firsts),
+        gradients_body,
         grid=(steps,),
-        in_specs=specs,
-        out_specs=[pl.BlockSpec((c.shape[1] // steps, feat), lambda i: (i, 0)) for c in counts],
-        out_shape=[jax.ShapeDtypeStruct((c.shape[1], feat), BF) for c in counts],
-        scratch_shapes=[pltpu.VMEM((n, feat), BF)] * len(counts),
-        compiler_params=params(60),
-        name="spread",
-    )(*args)
+        in_specs=[whole_vmem()] * (11 + len(inputs)) + [counts_spec(hot_counts), counts_spec(word_counts)],
+        out_specs=[rows_spec(hot_counts), rows_spec(word_counts)] + [whole_vmem()] * 3,
+        out_shape=[jax.ShapeDtypeStruct(x, BF) for x in shapes],
+        scratch_shapes=[pltpu.VMEM((n, feat), BF)] * 2,
+        compiler_params=params(50),
+        name="gradients",
+    )(
+        d_inputs, *lengths, *inputs, act1, act2, d_pre1, d_pre2, d_user, loss, b1, b2, *counts
+    )
 
 
 def slot_spread_body(cuts, counts_ref, length_ref, d_inputs_ref, *refs):
@@ -341,7 +410,7 @@
     )(counts, lengths, d_inputs)
 
 
-def widen_body(blocked, *refs):
+def widen_body(blocked, losses, examples, *refs):
     given, outs = refs[: blocked + 2], refs[blocked + 2 :]
     for x_ref, out_ref in zip(given[:blocked], outs[:blocked]):
         out_ref[...] = x_ref[...].astype(F32)
@@ -351,24 +420,24 @@
     @pl.when(pl.program_id(0) == 0)
     def _():
         rows, feat = last_out_ref.shape
-        first_out_ref[...] = first_ref[...].astype(F32)
+        first_out_ref[...] = first_ref[...].astype(F32)[: first_out_ref.shape[0], :]
         last_out_ref[...] = last_ref[:rows, :].astype(F32)
         small = last_ref[rows:, :].astype(F32)
-        start = loss_ref.shape[0]
-        loss_ref[...] = small[:start]
+        start = losses
+        loss_ref[...] = jnp.sum(small[:start], keepdims=True) / examples
         for ref in bias_refs:
             for i in range(ref.shape[1] // feat):
                 ref[:, i * feat : (i + 1) * feat] = small[start : start + 1]
                 start += 1
 
 
-def widen_call(arrays, first, last, last_rows, loss_rows, widths, steps):
+def widen_call(arrays, first, last, first_rows, last_rows, loss_rows, widths, examples, steps):
     feat = last.shape[1]
     spec = lambda a: pl.BlockSpec((a.shape[0] // steps, a.shape[1]), lambda i: (i, 0))
-    shapes = [a.shape for a in (*arrays, first)] + [(last_rows, feat), (loss_rows, feat)]
-    shapes += [(1, w) for w in widths]
+    shapes = [a.shape for a in arrays]
+    shapes += [(first_rows, first.shape[1]), (last_rows, feat), (1, 1)] + [(1, w) for w in widths]
     return pl.pallas_call(
-        functools.partial(widen_body, len(arrays)),
+        functools.partial(widen_body, len(arrays), loss_rows, examples),
         grid=(steps,),
         in_specs=[spec(a) for a in arrays] + [whole_vmem()] * 2,
         out_specs=[spec(a) for a in arrays] + [whole_vmem()] * (len(shapes) - len(arrays)),
@@ -410,7 +479,7 @@
     table_t_hbm,
     user_t_ref,
     label_ref,
-    d_user_t_ref,
+    d_user_ref,
     grad_ref,
     loss_ref,
     logits,
@@ -509,7 +578,7 @@
             return d_user_t + jnp.dot(table_t_ref[:, at(c)], d, preferred_element_type=F32)
 
         d_user_t = lax.fori_loop(0, chunks, third, jnp.zeros((feat, block), F32))
-        d_user_t_ref[...] = d_user_t.astype(BF)
+        d_user_ref[...] = d_user_t.T.astype(BF)
 
     @pl.when(step == 0)
     def _():
@@ -534,9 +603,9 @@
         grid=(n // block,),
         in_specs=[any_place] * 3
         + [across(feat), across(1)],
-        out_specs=[across(feat), whole_vmem(), across(1)],
+        out_specs=[pl.BlockSpec((block, feat), lambda i: (i, 0)), whole_vmem(), across(1)],
         out_shape=[
-            jax.ShapeDtypeStruct((feat, n), BF),
+            jax.ShapeDtypeStruct((n, feat), BF),
             jax.ShapeDtypeStruct((rows, feat), BF),
             jax.ShapeDtypeStruct((1, n), F32),
         ],
@@ -548,7 +617,7 @@
             pltpu.VMEM((feat, rows), BF),
             pltpu.SemaphoreType.DMA((3, rows // chunk)),
         ],
-        compiler_params=params(58),
+        compiler_params=params(46),
         name="sampled_softmax",
     )(mask, table, table_t, user.T, labels.reshape(1, n))
 
@@ -645,7 +714,9 @@
 
     hist_mean = (hot_sum + jnp.dot(slot_counts.astype(BF), returned, preferred_element_type=F32)) / hist_float
     search_mean = word_sum / search_float
-    inputs = jnp.concatenate([hist_mean, search_mean, dense_feats.astype(F32)], axis=1).astype(BF)
+    hist_mean, search_mean = hist_mean.astype(BF), search_mean.astype(BF)
+    dense = jnp.pad(dense_feats, ((0, 0), (0, -w_first.shape[0] % LANES)))
+    inputs = jnp.concatenate([hist_mean, search_mean, dense_feats], axis=1)
     pre_first = jnp.dot(inputs, w_first, preferred_element_type=F32) + b_first.astype(F32)
     act_first = jax.nn.gelu(pre_first).astype(BF)
     pre_second = jnp.dot(act_first, w_second, preferred_element_type=F32) + b_second.astype(F32)
@@ -654,35 +725,27 @@
         BF
     )
 
-    d_user_t, out_grad, per_example = softmax_call(mask, out_table, out_table_t, user, labels)
-    d_user = d_user_t.T
+    d_user, out_grad, per_example = softmax_call(mask, out_table, out_table_t, user, labels)
     d_pre_second = gelu_back(pre_second, right_product(d_user, w_third)).astype(BF)
     d_pre_first = gelu_back(pre_first, right_product(d_pre_second, w_second)).astype(BF)
     d_inputs = right_product(d_pre_first, w_first[: 2 * feat])
 
-    hot_grad, word_grad = spread_call(
-        (hot_counts, word_counts), (hist_float, search_float), d_inputs, (0, feat), feat, 4
-    )
-    w1_grad = left_product(inputs, d_pre_first).astype(BF)
-    w2_grad = left_product(act_first, d_pre_second).astype(BF)
-    w3_grad = left_product(act_second, d_user).astype(BF)
-    small = [
+    packed = gradients_call(
+        d_inputs,
+        (hist_float, search_float),
+        (hist_mean, search_mean, dense),
+        act_first,
+        act_second,
+        d_pre_first,
+        d_pre_second,
+        d_user,
         per_example,
-        jnp.sum(d_pre_first.astype(F32), axis=0),
-        jnp.sum(d_pre_second.astype(F32), axis=0),
-        jnp.sum(d_user.astype(F32), axis=0),
-    ]
-    small_rows = jnp.concatenate([x.reshape(-1, feat) for x in small], axis=0).astype(BF)
-    w3_rows = w3_grad.shape[0]
-    small_rows = jnp.pad(small_rows, ((0, -small_rows.shape[0] % 16), (0, 0)))
-    packed = (
-        hot_grad,
-        word_grad,
-        out_grad,
-        w1_grad,
-        w2_grad,
-        jnp.concatenate([w3_grad, small_rows], axis=0),
-    )
+        jnp.sum(d_pre_first.astype(F32), axis=0)[None],
+        jnp.sum(d_pre_second.astype(F32), axis=0)[None],
+        (hot_counts, word_counts),
+    )
+    packed = (*packed, out_grad)
+    w3_rows = w_third.shape[0]
     packed, slot_counts = lax.optimization_barrier((packed, slot_counts))
     summed = lax.psum(packed, ("group", "wide"))
 
@@ -697,18 +760,19 @@
     others = [lax.ppermute(x, "group", [(0, 1), (1, 0)]) for x in own]
     tail_grad = add_pair_call(own, others)
     summed, tail_grad = lax.optimization_barrier((summed, tail_grad))
-    hot_all, word_all, out_all, w2_all, w1_all, w3_all, losses, b1_all, b2_all, b3_all = widen_call(
-        (summed[0], summed[1], summed[2], summed[4]),
-        summed[3],
-        summed[5],
+    hot_all, word_all, out_all, w2_all, w1_all, w3_all, loss_value, b1_all, b2_all, b3_all = widen_call(
+        (summed[0], summed[1], summed[5], summed[3]),
+        summed[2],
+        summed[4],
+        w_first.shape[0],
         w3_rows,
         examples_dev // feat,
         (b_first.shape[0], b_second.shape[0], b_third.shape[0]),
+        examples_all,
         4,
     )
-    loss_value = jnp.sum(losses) / examples_all
     return (
-        loss_value,
+        loss_value[0, 0],
         hot_all,
         tail_grad,
         word_all,

time: 386 us -> 375 us (0.972)
  matrix products: 34.7 us -> 25.4 us
  waiting for transfers between devices: 14 us -> 9.97 us
    pallas_call x2, Pallas kernels: 21.8 us -> 27.5 us  [the longest x1 15.2 us: gradients_call(): pl.pallas_call(gradients_body, grid=(steps,), in_specs=[whole_vmem()] * (...]
    dot_general x3 -> x0, matrix products: 5.34 us -> none  [left_product(): lax.dot_general(first_op, second_op, (((0,), (0,)), ((), ())), preferred_...]
    unnamed x68 -> x76, local copies, waits for them, and re-layouts: 9.12 us -> 12.3 us
  transfers between devices with their start and end apart: 6 -> 6, of which waited for: 3 -> 3; matrix products, arithmetic and copies ran while one was open for 4% -> 5% of each run, Pallas kernels for 18% -> 19%
where the time goes in v5:
time: 375 us; the launch traced here: 370 us
  blocking collectives  147 us (39%)
  Pallas kernels  136 us (36%)
  matrix products  25.4 us (7%)
  local copies, waits for them, and re-layouts  17.9 us (5%)
  starting transfers between devices  15.2 us (4%)
  between operations  14.9 us (4%)
  waiting for transfers between devices  9.97 us (3%)
    all_to_all x7, blocking collectives, local(): lax.all_to_all(part, 'wide', split_axis=0, concat_axis=0, tiled=True)  126 us
    pallas_call x1, Pallas kernels, counts_call(): pl.pallas_call(functools.partial(counts_body, cuts), grid=(n // block,),...  34.5 us
    pallas_call x1, Pallas kernels, softmax_call(): pl.pallas_call(functools.partial(softmax_body, 1.0 / n, chunk), grid=(n /...  23.3 us
    all_to_all x1, blocking collectives, local(): lax.all_to_all(requests, 'wide', split_axis=0, concat_axis=0, tiled=True)  20.6 us
    pallas_call x1, Pallas kernels, add_rows_call(): pl.pallas_call(functools.partial(add_rows_body, unroll, len(given)), in_s...  19.9 us
    pallas_call x1, Pallas kernels, gradients_call(): pl.pallas_call(gradients_body, grid=(steps,), in_specs=[whole_vmem()] * (...  15.2 us
    pallas_call x1, Pallas kernels, gather_call(): pl.pallas_call(functools.partial(gather_body, parts), in_specs=[whole_sme...  14.1 us
    pallas_call x1, Pallas kernels, widen_call(): pl.pallas_call(functools.partial(widen_body, len(arrays), loss_rows, exam...  12.3 us
  transfers between devices with their start and end apart: 6, of which 3 were waited for; matrix products, arithmetic and copies ran while one was open for 5% of the time, Pallas kernels for 19%

profile of v5, /device:TPU:1, one launch (start us, length us, event | category | flops | bytes accessed | tf_op | source)
XLA Modules:
  0.0 369.6 jit_solution(5750611900233292440)
XLA Ops:
  7.2 20.6 %all_to_all.51 = s32[64,1,128]{2,1,0:T(1,128)} all-to-all(s32[64,1,128]{2,1,0:T(1,128)} %bitcast.52), channel_id=1, replica_groups=mesh['group'=2,'wide'=64] {'wide'}, dimensions={0} | all-to-all | bytes 65536 | tf_op jit(solution)/shard_map/all_to_all | solution.py:687
  27.8 14.1 %gather_rows.1 = bf16[8192,256]{1,0:T(8,128)(2,1)} custom-call(s32[64,128]{1,0:T(8,128)} %bitcast.48, bf16[8192,256]{1,0:T(8,128)(2,1)} %table_hbm.2), custom_call_target="tpu_custom_call" | custom-call | tf_op jit(solution)/shard_map/gather_rows/pallas_call | solution.py:157
  41.9 5.8 %all-to-all-start.1 = ((bf16[64,128,256]{2,1,0:T(8,128)(2,1)}), bf16[64,128,256]{2,1,0:T(8,128)(2,1)}, u32[]{:S(2)}, u32[]{:S(2)}) async-start(bf16[64,128,256]{2,1,0:T(8,128)(2,1)} %bitcast.46), calls=%async_computation.1 | async-start | bytes 8388608 | tf_op jit(solution)/shard_map/all_to_all | solution.py:689
  48.6 6.5 %copy.58 = bf16[8192,256]{0,1:T(8,128)(2,1)} copy(bf16[8192,256]{1,0:T(8,128)(2,1)} %table_hbm.3) | data formatting | bytes 8388608 | tf_op args[3]
  64.2 34.5 %counts.1 = (s8[1024,4096]{1,0:T(32,128)(4,1)}, s8[1024,8192]{1,0:T(32,128)(4,1)}, s8[1024,4096]{1,0:T(32,128)(4,1)}, f32[1024,256]{1,0:T(8,128)}, f32[1024,256]{1,0:T(8,128)}) custom-call(s32[1024,128]{1,0:T(8,128)} %select_add_fusion.ids_ref, bf16[4096,256]{1,0:T(8,128)(2,1)} %hot_ref.1, bf16[4096,256]{1,0:T(8,128)(2,1)} %word_ref.1), custom_call_target="tpu_custom_call" | custom-call | tf_op jit(solution)/shard_map/counts/pallas_call | solution.py:85
  100.2 9.5 %fusion.30.mean_ref = bf16[1024,256]{1,0:T(8,128)(2,1)S(1)} fusion(f32[1024,256]{1,0:T(8,128)} %get-tuple-element.84, bf16[8192,256]{1,0:T(8,128)(2,1)} %bitcast.5, s8[1024,8192]{1,0:T(32,128)(4,1)} %get-tuple-element.106.counts_ref, f32[1024]{0:T(1024)S(1)} %convert_element_type.67), kind=kOutput, calls=%fused_computation.37 | convolution fusion | flops 4304142336 | bytes 14159872 | tf_op jit(solution)/shard_map/dot_general | solution.py:715
  109.7 4.6 %multiply_convert_fusion = (bf16[1024,1024]{1,0:T(8,128)(2,1)S(1)}, f32[1024,1024]{1,0:T(8,128)}) fusion(f32[1024]{0:T(1024)S(1)} %convert_element_type.71, bf16[600,1024]{1,0:T(8,128)(2,1)S(1)} %copy-done.29, bf16[1024,88]{1,0:T(8,128)(2,1)S(1)} %copy-done.15, bf16[1024,256]{1,0:T(8,128)(2,1)S(1)} %divide_convert_fusion.word_mean_ref, ...), kind=kOutput, calls=%fused_computation.12 | convolution fusion | flops 1272463360 | bytes 8753152 | tf_op jit(solution)/shard_map/dot_general | solution.py:720
  116.6 23.3 %sampled_softmax.1 = (bf16[1024,256]{1,0:T(8,128)(2,1)S(1)}, bf16[8192,256]{1,0:T(8,128)(2,1)S(1)}, f32[1,1024]{1,0:T(1,128)S(1)}) custom-call(f32[8192,128]{1,0:T(8,128)} %broadcast_in_dim.37.mask_hbm, bf16[8192,256]{1,0:T(8,128)(2,1)} %table_hbm.3, bf16[256,8192]{1,0:T(8,128)(2,1)} %bitcast.45, bf16[256,1024]{1,0:T(8,128)(2,1)S(1)} %fusion.34.user_t_ref, ...), custom_call_target="tpu_custom_call" | custom-call | tf_op jit(solution)/shard_map/sampled_softmax/pallas_call | solution.py:601
  144.0 4.0 %convert_reduce_fusion = (f32[1024]{0:T(1024)S(1)}, bf16[1024,1024]{1,0:T(8,128)(2,1)S(1)}) fusion(f32[1024,1024]{1,0:T(8,128)S(1)} %copy-done.32, f32[1024]{0:T(1024)S(1)} %convert_element_type.71, bf16[1024,512]{1,0:T(8,128)(2,1)S(1)} %get-tuple-element.170.d_pre2_ref, bf16[1024,512]{1,0:T(8,128)(2,1)S(1)} %copy-done), kind=kOutput, calls=%fused_computation.11 | convolution fusion | flops 1097858048 | bytes 8396800 | tf_op jit(solution)/shard_map/dot_general | solution.py:641
  150.7 15.2 %gradients.1 = (bf16[4096,256]{1,0:T(8,128)(2,1)}, bf16[4096,256]{1,0:T(8,128)(2,1)}, bf16[640,1024]{1,0:T(8,128)(2,1)}, bf16[1024,512]{1,0:T(8,128)(2,1)}, bf16[528,256]{1,0:T(8,128)(2,1)}) custom-call(f32[1024,512]{1,0:T(8,128)} %fusion.38.d_inputs_ref, f32[1024,1]{1,0:T(8,128)S(1)} %copy.67.hist_ref.length_ref, f32[1024,1]{1,0:T(8,128)S(1)} %copy.68.search_ref, ...), custom_call_target="tpu_custom_call" | custom-call | tf_op jit(solution)/shard_map/gradients/pallas_call | solution.py:367
  166.0 9.5 %slot_spread.1 = (bf16[64,16,256]{2,1,0:T(8,128)(2,1)}, bf16[64,16,256]{2,1,0:T(8,128)(2,1)}, bf16[64,16,256]{2,1,0:T(8,128)(2,1)}, bf16[64,32,256]{2,1,0:T(8,12...) custom-call(s8[1024,8192]{1,0:T(32,128)(4,1)} %get-tuple-element.106.counts_ref, ...), custom_call_target="tpu_custom_call" | custom-call | tf_op jit(solution)/shard_map/slot_spread/pallas_call | solution.py:400
  175.5 24.1 %all_to_all.52 = bf16[64,16,256]{2,1,0:T(8,128)(2,1)S(1)} all-to-all(bf16[64,16,256]{2,1,0:T(8,128)(2,1)} %get-tuple-element.108), channel_id=1, replica_groups=mesh['group'=2,'wide'=64] {'wide'}, dimensions={0} | all-to-all | bytes 1048576 | tf_op jit(solution)/shard_map/all_to_all | solution.py:757
  199.7 18.6 %all_to_all.53 = bf16[64,16,256]{2,1,0:T(8,128)(2,1)S(1)} all-to-all(bf16[64,16,256]{2,1,0:T(8,128)(2,1)} %get-tuple-element.111), channel_id=1, replica_groups=mesh['group'=2,'wide'=64] {'wide'}, dimensions={0} | all-to-all | bytes 1048576 | tf_op jit(solution)/shard_map/all_to_all | solution.py:757
  218.3 16.7 %all_to_all.54 = bf16[64,16,256]{2,1,0:T(8,128)(2,1)S(1)} all-to-all(bf16[64,16,256]{2,1,0:T(8,128)(2,1)S(1)} %copy-done.20), channel_id=1, replica_groups=mesh['group'=2,'wide'=64] {'wide'}, dimensions={0} | all-to-all | bytes 1048576 | tf_op jit(solution)/shard_map/all_to_all | solution.py:757
  235.0 20.1 %all_to_all.55 = bf16[64,32,256]{2,1,0:T(8,128)(2,1)} all-to-all(bf16[64,32,256]{2,1,0:T(8,128)(2,1)S(1)} %copy-done.16), channel_id=1, replica_groups=mesh['group'=2,'wide'=64] {'wide'}, dimensions={0} | all-to-all | bytes 2097152 | tf_op jit(solution)/shard_map/all_to_all | solution.py:757
  255.1 16.1 %all_to_all.56 = bf16[64,16,256]{2,1,0:T(8,128)(2,1)S(1)} all-to-all(bf16[64,16,256]{2,1,0:T(8,128)(2,1)S(1)} %copy-done.19), channel_id=1, replica_groups=mesh['group'=2,'wide'=64] {'wide'}, dimensions={0} | all-to-all | bytes 1048576 | tf_op jit(solution)/shard_map/all_to_all | solution.py:757
  271.1 15.4 %all_to_all.57 = bf16[64,16,256]{2,1,0:T(8,128)(2,1)S(1)} all-to-all(bf16[64,16,256]{2,1,0:T(8,128)(2,1)S(1)} %copy-done.18), channel_id=1, replica_groups=mesh['group'=2,'wide'=64] {'wide'}, dimensions={0} | all-to-all | bytes 1048576 | tf_op jit(solution)/shard_map/all_to_all | solution.py:757
  286.6 15.0 %all_to_all.58 = bf16[64,16,256]{2,1,0:T(8,128)(2,1)S(1)} all-to-all(bf16[64,16,256]{2,1,0:T(8,128)(2,1)S(1)} %copy-done.17), channel_id=1, replica_groups=mesh['group'=2,'wide'=64] {'wide'}, dimensions={0} | all-to-all | bytes 1048576 | tf_op jit(solution)/shard_map/all_to_all | solution.py:757
  301.5 19.9 %add_rows.1 = (bf16[2048,256]{1,0:T(8,128)(2,1)S(1)}, bf16[2048,256]{1,0:T(8,128)(2,1)S(1)}, bf16[2048,256]{1,0:T(8,128)(2,1)}, bf16[2048,256]{1,0:T(8,128)(2,1)}) custom-call(s32[8192]{0:T(1024)S(1)} %get-tuple-element.103.ids_ref, s32[8192]{0:T(1024)S(1)} %get-tuple-element.104.again_ref, s32[544]{0:T(1024)S(1)} %pad_add_fusion.clash_ref, ...), custom_call_target="tpu_custom_call" | custom-call | tf_op jit(solution)/shard_map/add_rows/pallas_call | solution.py:266
  321.5 8.6 %collective-permute-start = (bf16[2048,256]{1,0:T(8,128)(2,1)S(1)}, bf16[2048,256]{1,0:T(8,128)(2,1)S(1)}, u32[]{:S(2)}, u32[]{:S(2)}) collective-permute-start(bf16[2048,256]{1,0:T(8,128)(2,1)S(1)} %get-tuple-element.126.refs_0_), channel_id=1, source_target_pairs={{0,64},{64,0},{1,65},{65,1},{2,66},{66,2},{3,67},{67,3},{4,68},{68... | collective-permute-start | bytes 3145736 | tf_op jit(solution)/shard_map/ppermute | solution.py:760
  330.7 4.1 %collective-permute-done.refs_4_ = bf16[2048,256]{1,0:T(8,128)(2,1)S(1)} collective-permute-done((bf16[2048,256]{1,0:T(8,128)(2,1)S(1)}, bf16[2048,256]{1,0:T(8,128)(2,1)S(1)}, u32[]{:S(2)}, u32[]{:S(2)}) %collective-permute-start) | collective-permute-done | bytes 1048608 | tf_op jit(solution)/shard_map/ppermute | solution.py:760
  334.8 3.8 %collective-permute-done.1.refs_5_ = bf16[2048,256]{1,0:T(8,128)(2,1)S(1)} collective-permute-done((bf16[2048,256]{1,0:T(8,128)(2,1)S(1)}, bf16[2048,256]{1,0:T(8,128)(2,1)S(1)}, u32[]{:S(2)}, u32[]{:S(2)}) %collective-permute-start.1) | collective-permute-done | bytes 1048608 | tf_op jit(solution)/shard_map/ppermute | solution.py:760
  340.6 7.6 %add_parts.1 = f32[8192,256]{1,0:T(8,128)} custom-call(bf16[2048,256]{1,0:T(8,128)(2,1)} %copy-done.4, bf16[2048,256]{1,0:T(8,128)(2,1)} %copy-done.5, bf16[2048,256]{1,0:T(8,128)(2,1)} %get-tuple-element.128.refs_2_, bf16[2048,256]{1,0:T(8,128)(2,1)} %get-tuple-element.129.refs_3_, bf16[2048,256]{1,0:T(8,128)(2,1)} %copy-done.11, ...), custom_call_target="tpu_custom_call" | custom-call | tf_op jit(solution)/shard_map/add_parts/pallas_call | solution.py:462
  350.2 12.3 %widen.1 = (f32[4096,256]{1,0:T(8,128)}, f32[4096,256]{1,0:T(8,128)}, f32[8192,256]{1,0:T(8,128)}, f32[1024,512]{1,0:T(8,128)}, f32[600,1024]{1,0:T(8,128)}, /*i...) custom-call(bf16[4096,256]{1,0:T(8,128)(2,1)} %get-tuple-element.130.refs_0_, ...), custom_call_target="tpu_custom_call" | custom-call | tf_op jit(solution)/shard_map/widen/pallas_call | solution.py:439
  (127 shorter events, 24.7 us)
Async XLA Ops:
  7.2 107.2 %copy-start = (bf16[1024,512]{1,0:T(8,128)(2,1)S(1)}, bf16[1024,512]{1,0:T(8,128)(2,1)}, u32[]{:S(2)}) copy-start(bf16[1024,512]{1,0:T(8,128)(2,1)} %param.24) | copy-start | bytes 3145732
  41.9 58.3 %all-to-all-start.1 = ((bf16[64,128,256]{2,1,0:T(8,128)(2,1)}), bf16[64,128,256]{2,1,0:T(8,128)(2,1)}, u32[]{:S(2)}, u32[]{:S(2)}) async-start(bf16[64,128,256]{2,1,0:T(8,128)(2,1)} %bitcast.46), calls=%async_computation.1 | async-start | bytes 8388608 | tf_op jit(solution)/shard_map/all_to_all | solution.py:689
  47.7 302.5 %all-reduce.6.cloned.1.call-start = ((), (), s32[]{:S(2)}) async-start(), calls=%async_computation.9 | async-start | bytes 22036480 | tf_op jit(solution)/shard_map/psum | solution.py:750
  48.6 6.6 %copy-start.26 = (s32[1024]{0:T(1024)S(1)}, s32[1024]{0:T(1024)}, u32[]{:S(2)}) copy-start(s32[1024]{0:T(1024)} %param.30) | copy-start | bytes 12292
  48.6 6.6 %copy-start.23 = (bf16[1024,88]{0,1:T(8,128)(2,1)S(1)}, bf16[1024,88]{0,1:T(8,128)(2,1)}, u32[]{:S(2)}) copy-start(bf16[1024,88]{0,1:T(8,128)(2,1)} %param.28) | copy-start | bytes 540676
  48.6 7.4 %copy-start.27 = (bf16[1024]{0:T(1024)(128)(2,1)S(1)}, bf16[1024]{0:T(1024)(128)(2,1)}, u32[]{:S(2)}) copy-start(bf16[1024]{0:T(1024)(128)(2,1)} %param.23) | copy-start | bytes 6148
  48.6 7.4 %copy-start.28 = (bf16[512]{0:T(512)(128)(2,1)S(1)}, bf16[512]{0:T(512)(128)(2,1)}, u32[]{:S(2)}) copy-start(bf16[512]{0:T(512)(128)(2,1)} %param.25) | copy-start | bytes 3076
  48.6 7.4 %copy-start.31 = (bf16[256]{0:T(256)(128)(2,1)S(1)}, bf16[256]{0:T(256)(128)(2,1)}, u32[]{:S(2)}) copy-start(bf16[256]{0:T(256)(128)(2,1)} %param.27) | copy-start | bytes 1540
  56.3 94.4 %copy-start.2 = (f32[1024,1]{1,0:T(8,128)}, f32[1024,1]{1,0:T(8,128)S(1)}, u32[]{:S(2)}) copy-start(f32[1024,1]{1,0:T(8,128)S(1)} %copy.67.hist_ref.length_ref) | copy-start | bytes 12292
  100.2 9.5 %copy-start.15 = (bf16[1024,88]{1,0:T(8,128)(2,1)S(1)}, bf16[1024,88]{1,0:T(8,128)(2,1)}, u32[]{:S(2)}) copy-start(bf16[1024,88]{1,0:T(8,128)(2,1)} %copy.64) | copy-start | bytes 540676
  100.2 9.5 %copy-start.29 = (bf16[600,1024]{1,0:T(8,128)(2,1)S(1)}, bf16[600,1024]{1,0:T(8,128)(2,1)}, u32[]{:S(2)}) copy-start(bf16[600,1024]{1,0:T(8,128)(2,1)} %param.22) | copy-start | bytes 3686404
  116.1 23.8 %copy-start.10 = (bf16[1024,512]{1,0:T(8,128)(2,1)}, bf16[1024,512]{1,0:T(8,128)(2,1)S(1)}, u32[]{:S(2)}) copy-start(bf16[1024,512]{1,0:T(8,128)(2,1)S(1)} %get-tuple-element.165.act2_ref) | copy-start | bytes 3145732
  175.5 42.8 %copy-start.20 = (bf16[64,16,256]{2,1,0:T(8,128)(2,1)S(1)}, bf16[64,16,256]{2,1,0:T(8,128)(2,1)}, u32[]{:S(2)}) copy-start(bf16[64,16,256]{2,1,0:T(8,128)(2,1)} %get-tuple-element.114) | copy-start | bytes 1572868
  175.5 59.5 %copy-start.16 = (bf16[64,32,256]{2,1,0:T(8,128)(2,1)S(1)}, bf16[64,32,256]{2,1,0:T(8,128)(2,1)}, u32[]{:S(2)}) copy-start(bf16[64,32,256]{2,1,0:T(8,128)(2,1)} %get-tuple-element.117) | copy-start | bytes 3145732
  199.7 55.4 %copy-start.19 = (bf16[64,16,256]{2,1,0:T(8,128)(2,1)S(1)}, bf16[64,16,256]{2,1,0:T(8,128)(2,1)}, u32[]{:S(2)}) copy-start(bf16[64,16,256]{2,1,0:T(8,128)(2,1)} %get-tuple-element.120) | copy-start | bytes 1572868
  218.3 52.9 %copy-start.18 = (bf16[64,16,256]{2,1,0:T(8,128)(2,1)S(1)}, bf16[64,16,256]{2,1,0:T(8,128)(2,1)}, u32[]{:S(2)}) copy-start(bf16[64,16,256]{2,1,0:T(8,128)(2,1)} %get-tuple-element.123) | copy-start | bytes 1572868
  235.0 51.6 %copy-start.17 = (bf16[64,16,256]{2,1,0:T(8,128)(2,1)S(1)}, bf16[64,16,256]{2,1,0:T(8,128)(2,1)}, u32[]{:S(2)}) copy-start(bf16[64,16,256]{2,1,0:T(8,128)(2,1)} %get-tuple-element.125) | copy-start | bytes 1572868
  321.5 19.1 %copy-start.4 = (bf16[2048,256]{1,0:T(8,128)(2,1)}, bf16[2048,256]{1,0:T(8,128)(2,1)S(1)}, u32[]{:S(2)}) copy-start(bf16[2048,256]{1,0:T(8,128)(2,1)S(1)} %get-tuple-element.126.refs_0_) | copy-start | bytes 3145732
  321.5 19.1 %copy-start.5 = (bf16[2048,256]{1,0:T(8,128)(2,1)}, bf16[2048,256]{1,0:T(8,128)(2,1)S(1)}, u32[]{:S(2)}) copy-start(bf16[2048,256]{1,0:T(8,128)(2,1)S(1)} %get-tuple-element.127.refs_1_) | copy-start | bytes 3145732
  321.5 13.3 %collective-permute-start = (bf16[2048,256]{1,0:T(8,128)(2,1)S(1)}, bf16[2048,256]{1,0:T(8,128)(2,1)S(1)}, u32[]{:S(2)}, u32[]{:S(2)}) collective-permute-start(bf16[2048,256]{1,0:T(8,128)(2,1)S(1)} %get-tuple-element.126.refs_0_), channel_id=1, source_target_pairs={{0,64},{64,0},{1,65},{65,1},{2,66},{66,2},{3,67},{67,3},{4,68},{68... | collective-permute-start | bytes 3145736 | tf_op jit(solution)/shard_map/ppermute | solution.py:760
  330.1 8.5 %collective-permute-start.1 = (bf16[2048,256]{1,0:T(8,128)(2,1)S(1)}, bf16[2048,256]{1,0:T(8,128)(2,1)S(1)}, u32[]{:S(2)}, u32[]{:S(2)}) collective-permute-start(bf16[2048,256]{1,0:T(8,128)(2,1)S(1)} %get-tuple-element.127.refs_1_), channel_id=1, source_target_pairs={{0,64},{64,0},{1,65},{65,1},{2,66},{66,2},{3,67},{67,3},{4,68},{68... | collective-permute-start | bytes 3145736 | tf_op jit(solution)/shard_map/ppermute | solution.py:760
  330.1 9.5 %collective-permute-start.2 = (bf16[2048,256]{1,0:T(8,128)(2,1)}, bf16[2048,256]{1,0:T(8,128)(2,1)S(1)}, u32[]{:S(2)}, u32[]{:S(2)}) collective-permute-start(bf16[2048,256]{1,0:T(8,128)(2,1)} %get-tuple-element.128.refs_2_), channel_id=1, source_target_pairs={{0,64},{64,0},{1,65},{65,1},{2,66},{66,2},{3,67},{67,3},{4,68},{68... | collective-permute-start | bytes 3145736 | tf_op jit(solution)/shard_map/ppermute | solution.py:760
  330.6 10.0 %collective-permute-start.3 = (bf16[2048,256]{1,0:T(8,128)(2,1)}, bf16[2048,256]{1,0:T(8,128)(2,1)}, u32[]{:S(2)}, u32[]{:S(2)}) collective-permute-start(bf16[2048,256]{1,0:T(8,128)(2,1)} %get-tuple-element.129.refs_3_), channel_id=1, source_target_pairs={{0,64},{64,0},{1,65},{65,1},{2,66},{66,2},{3,67},{67,3},{4,68},{68... | collective-permute-start | bytes 3145736 | tf_op jit(solution)/shard_map/ppermute | solution.py:760
  350.2 12.3 %copy-start.1 = (bf16[1024,512]{1,0:T(8,128)(2,1)S(1)}, bf16[1024,512]{1,0:T(8,128)(2,1)}, u32[]{:S(2)}) copy-start(bf16[1024,512]{1,0:T(8,128)(2,1)} %param.24) | copy-start | bytes 3145732
  (15 other events, 53.0 us)
Sparse Core Ops, SparseCore 0:
  166.1 184.0 all-reduce.5

commit v6 on v5

--- a/solution.py
+++ b/solution.py
@@ -283,10 +283,10 @@
     mean_ref,
     word_mean_ref,
     dense_ref,
-    act1_ref,
-    act2_ref,
-    d_pre1_ref,
-    d_pre2_ref,
+    act1_any,
+    act2_any,
+    d_pre1_any,
+    d_pre2_any,
     d_user_ref,
     loss_ref,
     b1_ref,
@@ -300,12 +300,26 @@
     g3_ref,
     hot_part,
     word_part,
+    act1_ref,
+    act2_ref,
+    d_pre1_ref,
+    d_pre2_ref,
+    sems,
 ):
     step = pl.program_id(0)
     feat = hot_part.shape[1]
+    pairs = (
+        (act1_any, act1_ref),
+        (act2_any, act2_ref),
+        (d_pre2_any, d_pre2_ref),
+        (d_pre1_any, d_pre1_ref),
+    )
+    fetches = [pltpu.make_async_copy(x, y, sems.at[i]) for i, (x, y) in enumerate(pairs)]
 
     @pl.when(step == 0)
     def _():
+        for fetch in fetches:
+            fetch.start()
         hot_part[...] = (d_inputs_ref[:, :feat] / hist_ref[...]).astype(BF)
         word_part[...] = (d_inputs_ref[:, feat:] / search_ref[...]).astype(BF)
 
@@ -315,25 +329,11 @@
     ):
         out_ref[...] = left_product(counts_ref[...].astype(BF), part[...]).astype(BF)
 
-    half = g1_ref.shape[1] // 2
-    for k in range(2):
-
-        @pl.when(step == k)
-        def _(k=k):
-            columns = slice(k * half, (k + 1) * half)
-            start = 0
-            for given_ref in (mean_ref, word_mean_ref, dense_ref):
-                end = start + given_ref.shape[1]
-                grad = left_product(given_ref[...], d_pre1_ref[:, columns])
-                g1_ref[start:end, columns] = grad.astype(BF)
-                start = end
-
-    @pl.when(step == 2)
+    @pl.when(step == 1)
     def _():
+        for fetch in fetches[:3]:
+            fetch.wait()
         g2_ref[...] = left_product(act1_ref[...], d_pre2_ref[...]).astype(BF)
-
-    @pl.when(step == 3)
-    def _():
         d_user = d_user_ref[...]
         rows = act2_ref.shape[1]
         g3_ref[:rows, :] = left_product(act2_ref[...], d_user).astype(BF)
@@ -346,6 +346,21 @@
         spare = g3_ref.shape[0] - rows - len(small)
         small.append(jnp.zeros((spare, feat), F32))
         g3_ref[rows:, :] = jnp.concatenate(small, axis=0).astype(BF)
+
+    half = g1_ref.shape[1] // 2
+    for k in range(2):
+
+        @pl.when(step == 2 + k)
+        def _(k=k):
+            if k == 0:
+                fetches[3].wait()
+            columns = slice(k * half, (k + 1) * half)
+            start = 0
+            for given_ref in (mean_ref, word_mean_ref, dense_ref):
+                end = start + given_ref.shape[1]
+                grad = left_product(given_ref[...], d_pre1_ref[:, columns])
+                g1_ref[start:end, columns] = grad.astype(BF)
+                start = end
 
 
 def gradients_call(
@@ -367,10 +382,15 @@
     return pl.pallas_call(
         gradients_body,
         grid=(steps,),
-        in_specs=[whole_vmem()] * (11 + len(inputs)) + [counts_spec(hot_counts), counts_spec(word_counts)],
+        in_specs=[whole_vmem()] * (3 + len(inputs))
+        + [pl.BlockSpec(memory_space=pl.ANY)] * 4
+        + [whole_vmem()] * 4
+        + [counts_spec(hot_counts), counts_spec(word_counts)],
         out_specs=[rows_spec(hot_counts), rows_spec(word_counts)] + [whole_vmem()] * 3,
         out_shape=[jax.ShapeDtypeStruct(x, BF) for x in shapes],
-        scratch_shapes=[pltpu.VMEM((n, feat), BF)] * 2,
+        scratch_shapes=[pltpu.VMEM((n, feat), BF)] * 2
+        + [pltpu.VMEM(x.shape, BF) for x in (act1, act2, d_pre1, d_pre2)]
+        + [pltpu.SemaphoreType.DMA((4,))],
         compiler_params=params(50),
         name="gradients",
     )(
@@ -535,7 +555,7 @@
         peak, pos = carry
         s = jnp.dot(table_ref[at(c), :], user_t, preferred_element_type=F32)
         pos = pos + fold(jnp.where(hits(c), s, 0.0), jnp.sum)
-        s = s + jnp.concatenate([mask_ref[at(c), :]] * (block // LANES), axis=1)
+        s = s + jnp.concatenate([mask_ref[at(c), :].astype(F32)] * (block // LANES), axis=1)
         logits[at(c), :] = s
         return jnp.maximum(peak, fold(s, jnp.max)), pos
 
@@ -612,7 +632,7 @@
         scratch_shapes=[
             pltpu.VMEM((rows, block), F32),
             pltpu.VMEM((rows, feat), F32),
-            pltpu.VMEM((rows, LANES), F32),
+            pltpu.VMEM((rows, LANES), BF),
             pltpu.VMEM((rows, feat), BF),
             pltpu.VMEM((feat, rows), BF),
             pltpu.SemaphoreType.DMA((3, rows // chunk)),
@@ -628,7 +648,7 @@
     high_hot = (high == negatives[None, :] // LANES).astype(BF)
     low_hot = (low == negatives[None, :] % LANES).astype(BF)
     sampled = right_product(high_hot, low_hot).reshape(rows, 1)
-    return jnp.broadcast_to(jnp.where(sampled > 0.5, F32(0.0), F32(-1e30)), (rows, LANES))
+    return jnp.broadcast_to(jnp.where(sampled > 0.5, 0.0, -1e30).astype(BF), (rows, LANES))
 
 
 def left_product(first_op, second_op):
@@ -769,7 +789,7 @@
         examples_dev // feat,
         (b_first.shape[0], b_second.shape[0], b_third.shape[0]),
         examples_all,
-        4,
+        2,
     )
     return (
         loss_value[0, 0],

time: 375 us -> 376 us (level)
    unnamed x76 -> x82, local copies, waits for them, and re-layouts: 12.3 us -> 11.7 us
where the time goes in v6:
time: 376 us; the launch traced here: 371 us
  blocking collectives  145 us (39%)
  Pallas kernels  133 us (35%)
  matrix products  25.3 us (7%)
  local copies, waits for them, and re-layouts  19.3 us (5%)
  starting transfers between devices  16.8 us (4%)
  between operations  14.9 us (4%)
  waiting for transfers between devices  12 us (3%)
  other arithmetic  3.98 us (1%)
    all_to_all x7, blocking collectives, local(): lax.all_to_all(part, 'wide', split_axis=0, concat_axis=0, tiled=True)  125 us
    pallas_call x1, Pallas kernels, counts_call(): pl.pallas_call(functools.partial(counts_body, cuts), grid=(n // block,),...  34.6 us
    pallas_call x1, Pallas kernels, softmax_call(): pl.pallas_call(functools.partial(softmax_body, 1.0 / n, chunk), grid=(n /...  23 us
    all_to_all x1, blocking collectives, local(): lax.all_to_all(requests, 'wide', split_axis=0, concat_axis=0, tiled=True)  20.6 us
    pallas_call x1, Pallas kernels, add_rows_call(): pl.pallas_call(functools.partial(add_rows_body, unroll, len(given)), in_s...  19.5 us
    pallas_call x1, Pallas kernels, gather_call(): pl.pallas_call(functools.partial(gather_body, parts), in_specs=[whole_sme...  14.1 us
    pallas_call x1, Pallas kernels, gradients_call(): pl.pallas_call(gradients_body, grid=(steps,), in_specs=[whole_vmem()] * (...  13.6 us
    unnamed x82, local copies, waits for them, and re-layouts  11.7 us
  transfers between devices with their start and end apart: 6, of which 3 were waited for; matrix products, arithmetic and copies ran while one was open for 5% of the time, Pallas kernels for 19%

profile of v6, /device:TPU:1, one launch (start us, length us, event | category | flops | bytes accessed | tf_op | source)
XLA Modules:
  0.0 370.8 jit_solution(7100956562630825985)
XLA Ops:
  7.2 20.6 %all_to_all.51 = s32[64,1,128]{2,1,0:T(1,128)} all-to-all(s32[64,1,128]{2,1,0:T(1,128)} %bitcast.52), channel_id=1, replica_groups=mesh['group'=2,'wide'=64] {'wide'}, dimensions={0} | all-to-all | bytes 65536 | tf_op jit(solution)/shard_map/all_to_all | solution.py:707
  27.8 14.1 %gather_rows.1 = bf16[8192,256]{1,0:T(8,128)(2,1)} custom-call(s32[64,128]{1,0:T(8,128)} %bitcast.48, bf16[8192,256]{1,0:T(8,128)(2,1)} %table_hbm.2), custom_call_target="tpu_custom_call" | custom-call | tf_op jit(solution)/shard_map/gather_rows/pallas_call | solution.py:157
  41.9 5.8 %all-to-all-start.1 = ((bf16[64,128,256]{2,1,0:T(8,128)(2,1)}), bf16[64,128,256]{2,1,0:T(8,128)(2,1)}, u32[]{:S(2)}, u32[]{:S(2)}) async-start(bf16[64,128,256]{2,1,0:T(8,128)(2,1)} %bitcast.46), calls=%async_computation.1 | async-start | bytes 8388608 | tf_op jit(solution)/shard_map/all_to_all | solution.py:709
  50.8 6.6 %copy.58 = bf16[8192,256]{0,1:T(8,128)(2,1)} copy(bf16[8192,256]{1,0:T(8,128)(2,1)} %table_hbm.3) | data formatting | bytes 8388608 | tf_op args[3]
  65.4 34.6 %counts.1 = (s8[1024,4096]{1,0:T(32,128)(4,1)}, s8[1024,8192]{1,0:T(32,128)(4,1)}, s8[1024,4096]{1,0:T(32,128)(4,1)}, f32[1024,256]{1,0:T(8,128)}, f32[1024,256]{1,0:T(8,128)}) custom-call(s32[1024,128]{1,0:T(8,128)} %select_add_fusion.ids_ref, bf16[4096,256]{1,0:T(8,128)(2,1)} %hot_ref.1, bf16[4096,256]{1,0:T(8,128)(2,1)} %word_ref.1), custom_call_target="tpu_custom_call" | custom-call | tf_op jit(solution)/shard_map/counts/pallas_call | solution.py:85
  102.2 9.5 %fusion.30.mean_ref = bf16[1024,256]{1,0:T(8,128)(2,1)S(1)} fusion(f32[1024,256]{1,0:T(8,128)} %get-tuple-element.84, bf16[8192,256]{1,0:T(8,128)(2,1)} %bitcast.5, s8[1024,8192]{1,0:T(32,128)(4,1)} %get-tuple-element.106.counts_ref, f32[1024]{0:T(1024)S(1)} %convert_element_type.80), kind=kOutput, calls=%fused_computation.37 | convolution fusion | flops 4304142336 | bytes 14159872 | tf_op jit(solution)/shard_map/dot_general | solution.py:735
  111.8 4.6 %multiply_convert_fusion = (bf16[1024,1024]{1,0:T(8,128)(2,1)S(1)}, f32[1024,1024]{1,0:T(8,128)}) fusion(f32[1024]{0:T(1024)S(1)} %convert_element_type.84, bf16[600,1024]{1,0:T(8,128)(2,1)S(1)} %copy-done.32, bf16[1024,88]{1,0:T(8,128)(2,1)S(1)} %copy-done.18, bf16[1024,256]{1,0:T(8,128)(2,1)S(1)} %copy-done.4, bf16[1024,256]{1,0:T(8,128)(2,1)S(1)} %fusion.30.mean_ref), kind=kOutput, calls=%fused_computation.12 | convolution fusion | flops 1272463360 | bytes 8753152 | tf_op jit(solution)/shard_map/dot_general | solution.py:740
  118.6 23.0 %sampled_softmax.1 = (bf16[1024,256]{1,0:T(8,128)(2,1)S(1)}, bf16[8192,256]{1,0:T(8,128)(2,1)S(1)}, f32[1,1024]{1,0:T(1,128)S(1)}) custom-call(bf16[8192,128]{1,0:T(8,128)(2,1)S(1)} %broadcast_in_dim.37.mask_hbm, bf16[8192,256]{1,0:T(8,128)(2,1)} %table_hbm.3, bf16[256,8192]{1,0:T(8,128)(2,1)} %bitcast.45, bf16[256,1024]{1,0:T(8,128)(2,1)S(1)} %fusion.34.user_t_ref, ...), custom_call_target="tpu_custom_call" | custom-call | tf_op jit(solution)/shard_map/sampled_softmax/pallas_call | solution.py:621
  145.8 4.0 %convert_reduce_fusion = (f32[1024]{0:T(1024)S(1)}, bf16[1024,1024]{1,0:T(8,128)(2,1)S(1)}) fusion(f32[1024,1024]{1,0:T(8,128)S(1)} %copy-done.35, f32[1024]{0:T(1024)S(1)} %convert_element_type.84, bf16[1024,512]{1,0:T(8,128)(2,1)S(1)} %get-tuple-element.170.d_pre2_any, bf16[1024,512]{1,0:T(8,128)(2,1)S(1)} %copy-done), kind=kOutput, calls=%fused_computation.11 | convolution fusion | flops 1097858048 | bytes 8396800 | tf_op jit(solution)/shard_map/dot_general | solution.py:661
  152.4 13.6 %gradients.1 = (bf16[4096,256]{1,0:T(8,128)(2,1)}, bf16[4096,256]{1,0:T(8,128)(2,1)}, bf16[640,1024]{1,0:T(8,128)(2,1)}, bf16[1024,512]{1,0:T(8,128)(2,1)}, bf16[528,256]{1,0:T(8,128)(2,1)}) custom-call(f32[1024,512]{1,0:T(8,128)} %fusion.39.d_inputs_ref, f32[1024,1]{1,0:T(8,128)S(1)} %copy-done.2, f32[1024,1]{1,0:T(8,128)S(1)} %copy-done.5, ...), custom_call_target="tpu_custom_call" | custom-call | tf_op jit(solution)/shard_map/gradients/pallas_call | solution.py:382
  166.0 9.5 %slot_spread.1 = (bf16[64,16,256]{2,1,0:T(8,128)(2,1)}, bf16[64,16,256]{2,1,0:T(8,128)(2,1)}, bf16[64,16,256]{2,1,0:T(8,128)(2,1)}, bf16[64,32,256]{2,1,0:T(8,12...) custom-call(s8[1024,8192]{1,0:T(32,128)(4,1)} %get-tuple-element.106.counts_ref, ...), custom_call_target="tpu_custom_call" | custom-call | tf_op jit(solution)/shard_map/slot_spread/pallas_call | solution.py:420
  175.6 23.9 %all_to_all.52 = bf16[64,16,256]{2,1,0:T(8,128)(2,1)S(1)} all-to-all(bf16[64,16,256]{2,1,0:T(8,128)(2,1)} %get-tuple-element.108), channel_id=1, replica_groups=mesh['group'=2,'wide'=64] {'wide'}, dimensions={0} | all-to-all | bytes 1048576 | tf_op jit(solution)/shard_map/all_to_all | solution.py:777
  199.5 18.8 %all_to_all.53 = bf16[64,16,256]{2,1,0:T(8,128)(2,1)S(1)} all-to-all(bf16[64,16,256]{2,1,0:T(8,128)(2,1)} %get-tuple-element.111), channel_id=1, replica_groups=mesh['group'=2,'wide'=64] {'wide'}, dimensions={0} | all-to-all | bytes 1048576 | tf_op jit(solution)/shard_map/all_to_all | solution.py:777
  218.3 16.7 %all_to_all.54 = bf16[64,16,256]{2,1,0:T(8,128)(2,1)S(1)} all-to-all(bf16[64,16,256]{2,1,0:T(8,128)(2,1)S(1)} %copy-done.23), channel_id=1, replica_groups=mesh['group'=2,'wide'=64] {'wide'}, dimensions={0} | all-to-all | bytes 1048576 | tf_op jit(solution)/shard_map/all_to_all | solution.py:777
  235.0 19.5 %all_to_all.55 = bf16[64,32,256]{2,1,0:T(8,128)(2,1)} all-to-all(bf16[64,32,256]{2,1,0:T(8,128)(2,1)S(1)} %copy-done.19), channel_id=1, replica_groups=mesh['group'=2,'wide'=64] {'wide'}, dimensions={0} | all-to-all | bytes 2097152 | tf_op jit(solution)/shard_map/all_to_all | solution.py:777
  254.5 15.2 %all_to_all.56 = bf16[64,16,256]{2,1,0:T(8,128)(2,1)S(1)} all-to-all(bf16[64,16,256]{2,1,0:T(8,128)(2,1)S(1)} %copy-done.22), channel_id=1, replica_groups=mesh['group'=2,'wide'=64] {'wide'}, dimensions={0} | all-to-all | bytes 1048576 | tf_op jit(solution)/shard_map/all_to_all | solution.py:777
  269.7 15.3 %all_to_all.57 = bf16[64,16,256]{2,1,0:T(8,128)(2,1)S(1)} all-to-all(bf16[64,16,256]{2,1,0:T(8,128)(2,1)S(1)} %copy-done.21), channel_id=1, replica_groups=mesh['group'=2,'wide'=64] {'wide'}, dimensions={0} | all-to-all | bytes 1048576 | tf_op jit(solution)/shard_map/all_to_all | solution.py:777
  284.9 15.2 %all_to_all.58 = bf16[64,16,256]{2,1,0:T(8,128)(2,1)S(1)} all-to-all(bf16[64,16,256]{2,1,0:T(8,128)(2,1)S(1)} %copy-done.20), channel_id=1, replica_groups=mesh['group'=2,'wide'=64] {'wide'}, dimensions={0} | all-to-all | bytes 1048576 | tf_op jit(solution)/shard_map/all_to_all | solution.py:777
  300.1 19.5 %add_rows.1 = (bf16[2048,256]{1,0:T(8,128)(2,1)S(1)}, bf16[2048,256]{1,0:T(8,128)(2,1)S(1)}, bf16[2048,256]{1,0:T(8,128)(2,1)}, bf16[2048,256]{1,0:T(8,128)(2,1)}) custom-call(s32[8192]{0:T(1024)S(1)} %get-tuple-element.103.ids_ref, s32[8192]{0:T(1024)S(1)} %get-tuple-element.104.again_ref, s32[544]{0:T(1024)S(1)} %pad_add_fusion.clash_ref, ...), custom_call_target="tpu_custom_call" | custom-call | tf_op jit(solution)/shard_map/add_rows/pallas_call | solution.py:266
  319.7 10.3 %collective-permute-start = (bf16[2048,256]{1,0:T(8,128)(2,1)S(1)}, bf16[2048,256]{1,0:T(8,128)(2,1)S(1)}, u32[]{:S(2)}, u32[]{:S(2)}) collective-permute-start(bf16[2048,256]{1,0:T(8,128)(2,1)S(1)} %get-tuple-element.126.refs_0_), channel_id=1, source_target_pairs={{0,64},{64,0},{1,65},{65,1},{2,66},{66,2},{3,67},{67,3},{4,68},{68... | collective-permute-start | bytes 3145736 | tf_op jit(solution)/shard_map/ppermute | solution.py:780
  330.6 4.3 %collective-permute-done.refs_4_ = bf16[2048,256]{1,0:T(8,128)(2,1)S(1)} collective-permute-done((bf16[2048,256]{1,0:T(8,128)(2,1)S(1)}, bf16[2048,256]{1,0:T(8,128)(2,1)S(1)}, u32[]{:S(2)}, u32[]{:S(2)}) %collective-permute-start) | collective-permute-done | bytes 1048608 | tf_op jit(solution)/shard_map/ppermute | solution.py:780
  340.3 7.5 %add_parts.1 = f32[8192,256]{1,0:T(8,128)} custom-call(bf16[2048,256]{1,0:T(8,128)(2,1)} %copy-done.6, bf16[2048,256]{1,0:T(8,128)(2,1)} %copy-done.7, bf16[2048,256]{1,0:T(8,128)(2,1)} %get-tuple-element.128.refs_2_, bf16[2048,256]{1,0:T(8,128)(2,1)} %get-tuple-element.129.refs_3_, bf16[2048,256]{1,0:T(8,128)(2,1)} %copy-done.13, ...), custom_call_target="tpu_custom_call" | custom-call | tf_op jit(solution)/shard_map/add_parts/pallas_call | solution.py:482
  347.8 4.3 %all-reduce.6.cloned.1.call-done = (bf16[4096,256]{1,0:T(8,128)(2,1)}, bf16[4096,256]{1,0:T(8,128)(2,1)}, bf16[640,1024]{1,0:T(8,128)(2,1)}, bf16[1024,512]{1,0:...) async-done(((bf16[4096,256]{1,0:T(8,128)(2,1)}, bf16[4096,256]{1,0:T(8,128)(2,1)}, bf16[640,1024]{1,0:T(8,128)(2,1)}, bf16[1024,512]{1,0:T(8,128)(2,1)}, ...) | async-done | bytes 11018256 | tf_op jit(solution)/shard_map/psum | solution.py:770
  352.1 11.5 %widen.1 = (f32[4096,256]{1,0:T(8,128)}, f32[4096,256]{1,0:T(8,128)}, f32[8192,256]{1,0:T(8,128)}, f32[1024,512]{1,0:T(8,128)}, f32[600,1024]{1,0:T(8,128)}, /*i...) custom-call(bf16[4096,256]{1,0:T(8,128)(2,1)} %get-tuple-element.130.refs_0_, ...), custom_call_target="tpu_custom_call" | custom-call | tf_op jit(solution)/shard_map/widen/pallas_call | solution.py:459
  (133 shorter events, 28.1 us)
Async XLA Ops:
  7.2 109.2 %copy-start = (bf16[1024,512]{1,0:T(8,128)(2,1)S(1)}, bf16[1024,512]{1,0:T(8,128)(2,1)}, u32[]{:S(2)}) copy-start(bf16[1024,512]{1,0:T(8,128)(2,1)} %param.24) | copy-start | bytes 3145732
  41.9 6.0 %copy-start.29 = (s32[1024]{0:T(1024)S(1)}, s32[1024]{0:T(1024)}, u32[]{:S(2)}) copy-start(s32[1024]{0:T(1024)} %param.30) | copy-start | bytes 12292
  41.9 6.0 %copy-start.28 = (s32[1024]{0:T(1024)S(1)}, s32[1024]{0:T(1024)}, u32[]{:S(2)}) copy-start(s32[1024]{0:T(1024)} %param.32) | copy-start | bytes 12292
  41.9 6.2 %copy-start.26 = (bf16[1024,88]{0,1:T(8,128)(2,1)S(1)}, bf16[1024,88]{0,1:T(8,128)(2,1)}, u32[]{:S(2)}) copy-start(bf16[1024,88]{0,1:T(8,128)(2,1)} %param.28) | copy-start | bytes 540676
  41.9 60.3 %all-to-all-start.1 = ((bf16[64,128,256]{2,1,0:T(8,128)(2,1)}), bf16[64,128,256]{2,1,0:T(8,128)(2,1)}, u32[]{:S(2)}, u32[]{:S(2)}) async-start(bf16[64,128,256]{2,1,0:T(8,128)(2,1)} %bitcast.46), calls=%async_computation.1 | async-start | bytes 8388608 | tf_op jit(solution)/shard_map/all_to_all | solution.py:709
  47.7 304.4 %all-reduce.6.cloned.1.call-start = ((), (), s32[]{:S(2)}) async-start(), calls=%async_computation.9 | async-start | bytes 22036480 | tf_op jit(solution)/shard_map/psum | solution.py:770
  48.3 9.1 %copy-start.17 = (bf16[1024,88]{1,0:T(8,128)(2,1)}, bf16[1024,88]{1,0:T(8,128)(2,1)S(1)}, u32[]{:S(2)}) copy-start(bf16[1024,88]{1,0:T(8,128)(2,1)S(1)} %copy.64) | copy-start | bytes 540676
  102.2 9.5 %copy-start.4 = (bf16[1024,256]{1,0:T(8,128)(2,1)S(1)}, bf16[1024,256]{1,0:T(8,128)(2,1)}, u32[]{:S(2)}) copy-start(bf16[1024,256]{1,0:T(8,128)(2,1)} %divide_convert_fusion.word_mean_ref) | copy-start | bytes 1572868
  102.2 9.5 %copy-start.18 = (bf16[1024,88]{1,0:T(8,128)(2,1)S(1)}, bf16[1024,88]{1,0:T(8,128)(2,1)}, u32[]{:S(2)}) copy-start(bf16[1024,88]{1,0:T(8,128)(2,1)} %copy-done.17) | copy-start | bytes 540676
  102.2 9.6 %copy-start.32 = (bf16[600,1024]{1,0:T(8,128)(2,1)S(1)}, bf16[600,1024]{1,0:T(8,128)(2,1)}, u32[]{:S(2)}) copy-start(bf16[600,1024]{1,0:T(8,128)(2,1)} %param.22) | copy-start | bytes 3686404
  118.1 23.6 %copy-start.12 = (bf16[1024,512]{1,0:T(8,128)(2,1)}, bf16[1024,512]{1,0:T(8,128)(2,1)S(1)}, u32[]{:S(2)}) copy-start(bf16[1024,512]{1,0:T(8,128)(2,1)S(1)} %get-tuple-element.165.act2_any) | copy-start | bytes 3145732
  143.8 6.0 %copy-start.14 = (bf16[1024,512]{1,0:T(8,128)(2,1)}, bf16[1024,512]{1,0:T(8,128)(2,1)S(1)}, u32[]{:S(2)}) copy-start(bf16[1024,512]{1,0:T(8,128)(2,1)S(1)} %get-tuple-element.170.d_pre2_any) | copy-start | bytes 3145732
  175.6 42.7 %copy-start.23 = (bf16[64,16,256]{2,1,0:T(8,128)(2,1)S(1)}, bf16[64,16,256]{2,1,0:T(8,128)(2,1)}, u32[]{:S(2)}) copy-start(bf16[64,16,256]{2,1,0:T(8,128)(2,1)} %get-tuple-element.114) | copy-start | bytes 1572868
  175.6 59.5 %copy-start.19 = (bf16[64,32,256]{2,1,0:T(8,128)(2,1)S(1)}, bf16[64,32,256]{2,1,0:T(8,128)(2,1)}, u32[]{:S(2)}) copy-start(bf16[64,32,256]{2,1,0:T(8,128)(2,1)} %get-tuple-element.117) | copy-start | bytes 3145732
  199.5 55.0 %copy-start.22 = (bf16[64,16,256]{2,1,0:T(8,128)(2,1)S(1)}, bf16[64,16,256]{2,1,0:T(8,128)(2,1)}, u32[]{:S(2)}) copy-start(bf16[64,16,256]{2,1,0:T(8,128)(2,1)} %get-tuple-element.120) | copy-start | bytes 1572868
  218.3 51.4 %copy-start.21 = (bf16[64,16,256]{2,1,0:T(8,128)(2,1)S(1)}, bf16[64,16,256]{2,1,0:T(8,128)(2,1)}, u32[]{:S(2)}) copy-start(bf16[64,16,256]{2,1,0:T(8,128)(2,1)} %get-tuple-element.123) | copy-start | bytes 1572868
  235.0 49.9 %copy-start.20 = (bf16[64,16,256]{2,1,0:T(8,128)(2,1)S(1)}, bf16[64,16,256]{2,1,0:T(8,128)(2,1)}, u32[]{:S(2)}) copy-start(bf16[64,16,256]{2,1,0:T(8,128)(2,1)} %get-tuple-element.125) | copy-start | bytes 1572868
  319.6 20.7 %copy-start.6 = (bf16[2048,256]{1,0:T(8,128)(2,1)}, bf16[2048,256]{1,0:T(8,128)(2,1)S(1)}, u32[]{:S(2)}) copy-start(bf16[2048,256]{1,0:T(8,128)(2,1)S(1)} %get-tuple-element.126.refs_0_) | copy-start | bytes 3145732
  319.7 20.7 %copy-start.7 = (bf16[2048,256]{1,0:T(8,128)(2,1)}, bf16[2048,256]{1,0:T(8,128)(2,1)S(1)}, u32[]{:S(2)}) copy-start(bf16[2048,256]{1,0:T(8,128)(2,1)S(1)} %get-tuple-element.127.refs_1_) | copy-start | bytes 3145732
  319.7 15.2 %collective-permute-start = (bf16[2048,256]{1,0:T(8,128)(2,1)S(1)}, bf16[2048,256]{1,0:T(8,128)(2,1)S(1)}, u32[]{:S(2)}, u32[]{:S(2)}) collective-permute-start(bf16[2048,256]{1,0:T(8,128)(2,1)S(1)} %get-tuple-element.126.refs_0_), channel_id=1, source_target_pairs={{0,64},{64,0},{1,65},{65,1},{2,66},{66,2},{3,67},{67,3},{4,68},{68... | collective-permute-start | bytes 3145736 | tf_op jit(solution)/shard_map/ppermute | solution.py:780
  330.0 8.3 %collective-permute-start.1 = (bf16[2048,256]{1,0:T(8,128)(2,1)S(1)}, bf16[2048,256]{1,0:T(8,128)(2,1)S(1)}, u32[]{:S(2)}, u32[]{:S(2)}) collective-permute-start(bf16[2048,256]{1,0:T(8,128)(2,1)S(1)} %get-tuple-element.127.refs_1_), channel_id=1, source_target_pairs={{0,64},{64,0},{1,65},{65,1},{2,66},{66,2},{3,67},{67,3},{4,68},{68... | collective-permute-start | bytes 3145736 | tf_op jit(solution)/shard_map/ppermute | solution.py:780
  330.1 9.2 %collective-permute-start.2 = (bf16[2048,256]{1,0:T(8,128)(2,1)}, bf16[2048,256]{1,0:T(8,128)(2,1)S(1)}, u32[]{:S(2)}, u32[]{:S(2)}) collective-permute-start(bf16[2048,256]{1,0:T(8,128)(2,1)} %get-tuple-element.128.refs_2_), channel_id=1, source_target_pairs={{0,64},{64,0},{1,65},{65,1},{2,66},{66,2},{3,67},{67,3},{4,68},{68... | collective-permute-start | bytes 3145736 | tf_op jit(solution)/shard_map/ppermute | solution.py:780
  330.5 9.8 %collective-permute-start.3 = (bf16[2048,256]{1,0:T(8,128)(2,1)}, bf16[2048,256]{1,0:T(8,128)(2,1)}, u32[]{:S(2)}, u32[]{:S(2)}) collective-permute-start(bf16[2048,256]{1,0:T(8,128)(2,1)} %get-tuple-element.129.refs_3_), channel_id=1, source_target_pairs={{0,64},{64,0},{1,65},{65,1},{2,66},{66,2},{3,67},{67,3},{4,68},{68... | collective-permute-start | bytes 3145736 | tf_op jit(solution)/shard_map/ppermute | solution.py:780
  352.1 11.5 %copy-start.1 = (bf16[1024,512]{1,0:T(8,128)(2,1)S(1)}, bf16[1024,512]{1,0:T(8,128)(2,1)}, u32[]{:S(2)}) copy-start(bf16[1024,512]{1,0:T(8,128)(2,1)} %param.24) | copy-start | bytes 3145732
  (18 other events, 55.0 us)
Sparse Core Ops, SparseCore 0:
  166.2 185.9 all-reduce.5
